TPU v7x, 32 devices: a whole 2x2x4 slice. The times are simulated.
32 devices in a mesh: seq: 8 (over z, y), grp: 4 (over x, core).
Axes of the slice: x: 2, y: 2, z: 4, core: 2. Of those that a mesh axis runs over, the one named last changes fastest.
Arguments:
- q_nope: bfloat16 [128, 128, 128], P('seq', 'grp'), may hold values from -6 to 6
- q_rope: bfloat16 [128, 128, 64], P('seq', 'grp'), may hold values from -256 to 256
- cache: bfloat16 [8192, 576], P('seq'), may hold values from -6 to 6
- w_uk: bfloat16 [128, 65536], P('grp', 'seq'), may hold values from -0.5 to 0.5
- w_uv: bfloat16 [128, 65536], P('grp', 'seq'), may hold values from -0.25 to 0.25
- d_out: bfloat16 [128, 128, 128], P('seq', 'grp'), may hold values from -6 to 6
- sel: int32 [128, 32], P('seq'), may hold values from 0 to 63, as said below
- slot_blocks: int32 [8, 64], P('seq'), may hold values from 0 to 15, as said below
Outputs:
- attn_out: bfloat16 [128, 128, 128], P('seq', 'grp')
- d_q_nope: bfloat16 [128, 128, 128], P('seq', 'grp')
- d_q_rope: bfloat16 [128, 128, 64], P('seq', 'grp')
- d_cache: float32 [8192, 576], P('seq')
Inputs may be any that keep to these rules, and one draw needn't show every extreme that they name: `sel`: each row names 32 different places; place s stands for the block that the row's device asks of device s // 8. `slot_blocks`: entry [r, s] is the index among device s // 8's own blocks of the block that device r asks for in place s; the 8 entries of a row toward one device differ.
All inputs are finite; a program needn't handle non-finite values.
Results may differ from a plain program's by a relative error of at most 0.015.
Values may be sent and summed in bfloat16 or wider, within the bound.
No kernel may reach another device: no remote copies, remote signals or barrier semaphores. Data moves between devices by JAX's collectives and lax.ppermute only.
A program may use at most 128 MiB of HBM per device.

v0:
```python
import functools
import math

import jax
import jax.numpy as jnp
from jax import lax
from jax.experimental import pallas as pl
from jax.experimental.pallas import tpu as pltpu
from jax.sharding import PartitionSpec as P

BLOCK_LEN = 64
LANES = 128
HIDDEN = -1e30
VMEM = pl.BlockSpec(memory_space=pltpu.VMEM)
SMEM = pl.BlockSpec(memory_space=pltpu.SMEM)
ANY = pl.BlockSpec(memory_space=pl.ANY)
F32 = jnp.float32
BF16 = jnp.bfloat16


def call(kernel, name, args, specs, outs, scratch=(), mib=32, tied=None):
    out_shape = [jax.ShapeDtypeStruct(s, d) for s, d in outs]
    out_specs = [VMEM] * len(outs)
    aliases = {}
    body = kernel
    if tied is not None:
        args, specs = (tied, *args), [ANY] + specs
        out_shape, out_specs = [jax.ShapeDtypeStruct(tied.shape, tied.dtype)] + out_shape, [ANY] + out_specs
        aliases = {0: 0}
        n_in = len(args)

        def body(*refs):
            kernel(*refs[1:n_in], *refs[n_in + 1 :])

    return pl.pallas_call(
        body,
        out_shape=out_shape,
        in_specs=specs,
        out_specs=out_specs,
        scratch_shapes=list(scratch),
        input_output_aliases=aliases,
        compiler_params=pltpu.CompilerParams(vmem_limit_bytes=mib * 2**20),
        name=name,
    )(*args)


def nt(a, b):
    return lax.dot_general(a, b, (((1,), (1,)), ((), ())), preferred_element_type=F32)


def nn(a, b):
    return lax.dot_general(a, b, (((1,), (0,)), ((), ())), preferred_element_type=F32)


def swap(x, axis, bit):
    n = lax.axis_size(axis)
    return lax.ppermute(x, axis, [(i, i ^ bit) for i in range(n)])


def seq_swap(x):
    return lax.all_to_all(x, "seq", split_axis=0, concat_axis=0, tiled=True)


def tie_kernel(*refs):
    pass


def cut_kernel(ids, cache, out):
    depth = out.shape[0]
    out[...] = cache[pl.ds(pl.multiple_of(ids[1] * depth, 16), depth), :]


def gather_kernel(per_peer, ids, own, other, *refs):
    owners = len(refs) - 2
    caches, outs = refs[:owners], refs[owners:]
    lanes = per_peer * BLOCK_LEN

    def block(row, i, j):
        b = row[0, (ids[0] ^ (2 * i)) * per_peer + j]
        tile = caches[i][:, pl.ds(pl.multiple_of((b >> 1) * LANES, LANES), LANES)]
        return jnp.where((b & 1) == 1, tile[:, BLOCK_LEN:], tile[:, :BLOCK_LEN])

    for row, out in zip((other, own), outs):
        for i in range(owners):
            for j in range(0, per_peer, 2):
                both = jnp.concatenate([block(row, i, j), block(row, i, j + 1)], axis=1)
                at = i * lanes + j * BLOCK_LEN
                out[:, at : at + 2 * BLOCK_LEN] = both


def scatter_kernel(per_peer, pieces, ids, rows, *refs):
    got, out, acc = refs[:-2], refs[-2], refs[-1]
    me = ids[0]
    depth = out.shape[0]
    acc[...] = jnp.zeros_like(acc)
    blank = jnp.zeros((depth, BLOCK_LEN), F32)
    for k, (ref, place) in enumerate(pieces):
        for j in range(per_peer):
            b = rows[k, me * per_peer + j]
            at = pl.ds(pl.multiple_of((b >> 1) * LANES, LANES), LANES)
            start = (place * per_peer + j) * BLOCK_LEN
            g = got[ref][:, start : start + BLOCK_LEN].astype(F32)
            low = jnp.concatenate([g, blank], axis=1)
            high = jnp.concatenate([blank, g], axis=1)
            acc[:, at] = acc[:, at] + jnp.where((b & 1) == 1, high, low)
    out[...] = acc[...].astype(BF16)


def assemble_kernel(ids, *refs):
    parts, out = refs[:-1], refs[-1]
    depth = parts[0].shape[0]
    for k, y in enumerate(parts):
        out[pl.ds(pl.multiple_of((ids[1] ^ k) * depth, 16), depth), :] = y[...].astype(F32)


def weight_k_of(pack, head, uk_rows, tiles):
    rows = uk_rows // tiles
    peers = pack.shape[0]
    cols = []
    for t in range(tiles):
        cols.append(
            jnp.concatenate(
                [pack[r, head, t * rows : (t + 1) * rows, :] for r in range(peers)], axis=0
            )
        )
    return jnp.concatenate(cols, axis=1)


def stacked(pack, head, start, rows):
    peers = pack.shape[0]
    return jnp.concatenate([pack[r, head, start : start + rows, :] for r in range(peers)], axis=0)


def expand_kernel(sizes, pack, away, over_x, out):
    uk_rows, uv_rows, queries, tiles, latent = sizes
    peers, heads = pack.shape[0], pack.shape[1]
    for h in range(heads):
        wk = weight_k_of(pack, h, uk_rows, tiles)
        wv = stacked(pack, h, uk_rows, uv_rows)
        qn = stacked(pack, h, uk_rows + uv_rows, queries)
        do = stacked(pack, h, uk_rows + uv_rows + queries, queries)
        q_lat = nn(qn, wk).astype(BF16)
        d_olat = nt(do, wv).astype(BF16)
        for r in range(peers):
            out[r, h, :, :latent] = q_lat[r * queries : (r + 1) * queries]
            out[r, h, :, latent:] = d_olat[r * queries : (r + 1) * queries]


def reduce_kernel(sizes, pack, lat, out):
    uk_rows, uv_rows, queries, tiles, latent = sizes
    peers, heads = pack.shape[0], pack.shape[1]
    for h in range(heads):
        wk = weight_k_of(pack, h, uk_rows, tiles)
        wv = stacked(pack, h, uk_rows, uv_rows)
        both = jnp.concatenate([lat[r, h] for r in range(peers)], axis=0)
        attn = nn(both[:, :latent], wv).astype(BF16)
        dqn = nt(both[:, latent:], wk).astype(BF16)
        for r in range(peers):
            out[r, h, :, : attn.shape[1]] = attn[r * queries : (r + 1) * queries]
            out[r, h, :, attn.shape[1] :] = dqn[r * queries : (r + 1) * queries]


def tokens_grad(grads, scale, do, cat, delta, kt, p, width):
    keep, send, at, depth = grads
    latent = do.shape[1]
    dp = nn(do[...], kt[:latent])
    ds = (p.astype(F32) * (dp - delta) * scale).astype(BF16)
    part = nt(ds, kt[:width])
    dk = nn(cat[...], jnp.concatenate([ds, p], axis=0)).astype(BF16)
    for k, ref in enumerate((keep, send, keep, send)):
        ref[k // 2, :, at] = dk[k * depth : (k + 1) * depth]
    return part


def attend_kernel(scale, per_peer, ids, sel, rope, qd, *refs):
    keys, refs = (refs[:4], refs[4:8]), refs[8:]
    keeps, sends, lat, d_rope, refs = (refs[0], refs[2]), (refs[1], refs[3]), refs[4], refs[5], refs[6:]
    kt_near, kt_far, pb_near, pb_far, qx, do, sc, flip, cat, o_full, dq = refs
    rows, latent = do.shape
    heads, queries, rope_dim = rope.shape
    width = latent + rope_dim
    slots = qx.shape[1] - width
    depth, half = keys[0][0].shape
    held = 4
    lanes = half // held
    kts, pbs = (kt_near, kt_far), (pb_near, pb_far)

    picks = sel[...] ^ (ids[0] * per_peer)
    slot = lax.broadcasted_iota(jnp.int32, (queries, slots), 1)
    chosen = picks[:, 0:1] == slot
    for j in range(1, picks.shape[1]):
        chosen = chosen | (picks[:, j : j + 1] == slot)
    bias = jnp.where(chosen, 0.0, HIDDEN).astype(BF16)
    bias = jnp.broadcast_to(bias[None], (heads, queries, slots)).reshape(rows, slots)
    qx[:, :latent] = qd[:, :latent]
    qx[:, latent:] = jnp.concatenate([rope[...].reshape(rows, rope_dim), bias], axis=1)
    do[...] = qd[:, latent:]
    for c in range(2):
        for k in range(4):
            at = pl.ds(pl.multiple_of((ids[1] ^ k) * depth, 16), depth)
            for i in range(held):
                peer = c * held + i
                src = keys[peer % 2][k][:, (peer // 2) * lanes : (peer // 2 + 1) * lanes]
                kts[c][at, i * lanes : (i + 1) * lanes] = src
        place = lax.broadcasted_iota(jnp.int32, (slots, half), 0)
        token = lax.broadcasted_iota(jnp.int32, (slots, half), 1) + c * half
        kts[c][width:, :] = jnp.where(token // BLOCK_LEN == place, 1.0, 0.0).astype(BF16)

    scale2 = scale * math.log2(math.e)
    step = 512
    chunks = [(c, i) for c in range(2) for i in range(0, half, step)]
    top = jnp.full((rows, 1), -jnp.inf, F32)
    total = jnp.zeros((rows, 1), F32)
    tops = []
    for n, (c, i) in enumerate(chunks):
        s = nn(qx[...], kts[c][:, i : i + step]) * scale2
        high = jnp.maximum(top, jnp.max(s, axis=1, keepdims=True))
        e = jnp.exp2(s - high)
        sc[:, n * step : (n + 1) * step] = e
        total = total * jnp.exp2(top - high) + jnp.sum(e, axis=1, keepdims=True)
        top = high
        tops.append(high)
    inv = 1.0 / total
    for n, (c, i) in enumerate(chunks):
        pb = (sc[:, n * step : (n + 1) * step] * (jnp.exp2(tops[n] - top) * inv)).astype(BF16)
        pbs[c][:, i : i + step] = pb
        part = nt(pb, kts[c][:latent, i : i + step])
        if n == 0:
            o_full[...] = part
        else:
            o_full[...] += part
    lat[:, :latent] = o_full[...].astype(BF16)
    delta = jnp.sum(o_full[...] * do[...].astype(F32), axis=1, keepdims=True)

    flip[:, :rows] = qx[:, :width].T
    flip[:latent, rows:] = do[...].T
    flip[latent:, rows:] = jnp.zeros((rope_dim, rows), BF16)
    for k in range(4):
        at = pl.ds(pl.multiple_of((ids[1] ^ k) * depth, 16), depth)
        cat[k * depth : (k + 1) * depth] = flip[at, :]
    for n, (c, i) in enumerate([(c, i) for c in (1, 0) for i in range(0, half, step)]):
        at = slice(i, i + step)
        grads = (keeps[c], sends[c], at, depth)
        kt = kts[c].at[:, at]
        part = tokens_grad(grads, scale, do, cat, delta, kt, pbs[c][:, at], width)
        if n == 0:
            dq[...] = part
        else:
            dq[...] += part
    lat[:, latent:] = dq[:, :latent].astype(BF16)
    d_rope[...] = dq[:, latent:].astype(BF16)


def pair_kernel(keep, got, a0, *a2):
    total = keep[...].astype(F32) + got[...].astype(F32)
    a0[...] = total[0].astype(BF16)
    lanes = a2[0].shape[1]
    for i, a in enumerate(a2):
        a[...] = total[1, :, i * lanes : (i + 1) * lanes].astype(BF16)


def owner_kernel(order, a0, got, *outs):
    total = (a0[...].astype(F32) + got[...].astype(F32)).astype(BF16)
    for places, out in zip(order, outs):
        lanes = out.shape[1] // len(places)
        for i, p in enumerate(places):
            out[:, i * lanes : (i + 1) * lanes] = total[:, p * lanes : (p + 1) * lanes]


def local(q_nope, q_rope, cache, w_uk, w_uv, d_out, sel, slot_blocks):
    peers = lax.axis_size("seq")
    groups = lax.axis_size("grp")
    queries, heads, nope = q_nope.shape
    rope = q_rope.shape[2]
    width = cache.shape[1]
    latent = width - rope
    value = d_out.shape[2]
    slots = slot_blocks.shape[1]
    per_peer = slots // peers
    if not (peers == 8 and groups == 4 and heads % peers == 0 and per_peer % 2 == 0):
        return local_general(q_nope, q_rope, cache, w_uk, w_uv, d_out, sel, slot_blocks)
    ids = jnp.stack([lax.axis_index("seq"), lax.axis_index("grp")]).astype(jnp.int32)
    tokens = cache.shape[0]
    depth = width // groups
    lanes = per_peer * BLOCK_LEN
    held = peers // 2
    half = held * lanes
    share = heads // peers
    rows = heads * queries
    scale = 1.0 / math.sqrt(nope + rope)

    row1 = swap(slot_blocks, "seq", 1)
    (c0,) = call(cut_kernel, "cut", (ids, cache.T), [SMEM, VMEM], [((depth, tokens), BF16)])
    c2 = swap(c0, "seq", 4)
    c1 = swap(c0, "seq", 2)
    asked_y = jnp.concatenate([slot_blocks, row1], axis=0)
    asked = jnp.concatenate([asked_y] + [swap(asked_y, "seq", bit) for bit in (2, 4, 6)], axis=0)

    c3 = swap(c2, "seq", 2)
    away, k0 = call(
        functools.partial(gather_kernel, per_peer),
        "gather",
        (ids, slot_blocks, row1, c0, c1, c2, c3),
        [SMEM] * 3 + [VMEM] * 4,
        [((depth, half), BF16)] * 2,
    )
    k_away, k0_x = swap(away, "seq", 1), swap(k0, "grp", 2)

    n_rows = w_uk.shape[1] // latent
    l_rows = w_uv.shape[1] // value
    tiles = latent // LANES
    uk = w_uk.reshape(heads, n_rows, tiles, LANES).transpose(0, 2, 1, 3)
    pack = jnp.concatenate(
        [
            uk.reshape(heads, n_rows * tiles, LANES),
            w_uv.reshape(heads, l_rows, value),
            q_nope.transpose(1, 0, 2),
            d_out.transpose(1, 0, 2),
        ],
        axis=1,
    )
    (pack,) = call(tie_kernel, "after", (c1, c3, asked), [ANY] * 3, [], tied=pack)
    pack = seq_swap(pack).reshape(peers, share, -1, LANES)
    sizes = (n_rows * tiles, l_rows, queries, tiles, latent)
    (lat,) = call(
        functools.partial(expand_kernel, sizes),
        "expand",
        (pack, k_away, k0_x),
        [VMEM, ANY, ANY],
        [((peers, share, queries, 2 * latent), BF16)],
    )
    qd = seq_swap(lat).reshape(rows, 2 * latent)

    keys = []
    for k, k2 in ((k0, k0_x), (k_away, swap(k_away, "grp", 2))):
        keys += [k, swap(k, "grp", 1), k2, swap(k2, "grp", 1)]
    rope_rows = q_rope.transpose(1, 0, 2)
    near_keep, near_send, far_keep, far_send, lat, d_rope = call(
        functools.partial(attend_kernel, scale, per_peer),
        "attend",
        (ids, sel, rope_rows, qd, *keys),
        [SMEM] + [VMEM] * 11,
        [((2, depth, half), BF16)] * 4 + [((rows, 2 * latent), BF16), ((rows, rope), BF16)],
        [pltpu.VMEM((width + slots, half), BF16)] * 2
        + [pltpu.VMEM((rows, half), BF16)] * 2
        + [
            pltpu.VMEM((rows, width + slots), BF16),
            pltpu.VMEM((rows, latent), BF16),
            pltpu.VMEM((rows, 2 * half), F32),
            pltpu.VMEM((width, 2 * rows), BF16),
            pltpu.VMEM((width, 2 * rows), BF16),
            pltpu.VMEM((rows, latent), F32),
            pltpu.VMEM((rows, width), F32),
        ],
        50,
    )

    def pair(keep, send, tied=None):
        outs = [((depth, half), BF16)] * 2
        return call(pair_kernel, "pair", (keep, swap(send, "grp", 1)), [VMEM] * 2, outs, tied=tied)


    def owner(a0, a2, order, tied=None):
        outs = [((depth, lanes * len(places)), BF16) for places in order]
        kernel = functools.partial(owner_kernel, order)
        return call(kernel, "owner", (a0, swap(a2, "grp", 2)), [VMEM] * 2, outs, tied=tied)

    far = pair(far_keep, far_send)
    first, *near = pair(near_keep, near_send, tied=far[0])
    held_a2, *far = owner(first, far[1], [(0,), (1,), (2,), (3,)], tied=near[1])
    lat = seq_swap(lat.reshape(peers, share, queries, 2 * latent))
    (res,) = call(
        functools.partial(reduce_kernel, sizes),
        "reduce",
        (pack, lat),
        [VMEM] * 2,
        [((peers, share, queries, value + nope), BF16)],
    )
    own, over_y, over_z = owner(near[0], held_a2, [(0,), (1, 3), (2,)])
    from_y = swap(over_y, "seq", 1)
    over_z = jnp.concatenate([over_z, from_y[:, lanes:]], axis=1)
    (over_z,) = call(tie_kernel, "after", (res,), [ANY], [], tied=over_z)
    from_z = swap(over_z, "seq", 2)
    got = [own, from_y, from_z] + [swap(p, "seq", 4 + i) for i, p in enumerate(far)]
    res = seq_swap(res).reshape(heads, queries, value + nope)

    (y0,) = call(
        functools.partial(
            scatter_kernel,
            per_peer,
            [(0, 0), (1, 0), (2, 0), (2, 1), (3, 0), (4, 0), (5, 0), (6, 0)],
        ),
        "scatter",
        (ids, asked, *got),
        [SMEM, SMEM] + [VMEM] * len(got),
        [((depth, tokens), BF16)],
        [pltpu.VMEM((depth, tokens), F32)],
    )
    y2 = swap(y0, "grp", 2)
    y1 = swap(y0, "grp", 1)
    y3 = swap(y2, "grp", 1)
    (d_cache,) = call(
        assemble_kernel,
        "assemble",
        (ids, y0, y1, y2, y3),
        [SMEM] + [VMEM] * 4,
        [((width, tokens), F32)],
    )
    return (
        res[:, :, :value].transpose(1, 0, 2),
        res[:, :, value:].transpose(1, 0, 2),
        d_rope.reshape(heads, queries, rope).transpose(1, 0, 2),
        d_cache.T,
    )


def local_general(q_nope, q_rope, cache, w_uk, w_uv, d_out, sel, slot_blocks):
    peers = lax.axis_size("seq")
    queries, heads, nope = q_nope.shape
    rope = q_rope.shape[2]
    width = cache.shape[1]
    latent = width - rope
    value = d_out.shape[2]
    slot_total = slot_blocks.shape[1]
    per_peer = slot_total // peers
    own_blocks = cache.shape[0] // BLOCK_LEN
    scale = 1.0 / math.sqrt(nope + rope)
    gathered_k, gathered_v = (
        lax.all_gather(w_uk, "seq", axis=1, tiled=True),
        lax.all_gather(w_uv, "seq", axis=1, tiled=True),
    )
    weight_k = gathered_k.reshape(heads, nope, latent)
    weight_v = gathered_v.reshape(heads, latent, value)
    wanted = slot_blocks.reshape(peers, per_peer)
    asked = lax.all_to_all(wanted, "seq", split_axis=0, concat_axis=0, tiled=True)
    blocks = cache.reshape(own_blocks, BLOCK_LEN, width)
    arrived = lax.all_to_all(blocks[asked], "seq", split_axis=0, concat_axis=0, tiled=True)
    keys = arrived.reshape(slot_total * BLOCK_LEN, width)
    keys_lat = keys[:, :latent]
    q_lat = jnp.einsum("qhn,hnl->qhl", q_nope, weight_k, preferred_element_type=jnp.float32).astype(
        jnp.bfloat16
    )
    qfull = jnp.concatenate([q_lat, q_rope], axis=-1)
    chosen = jnp.any(
        sel[:, :, None] == jnp.arange(slot_total, dtype=jnp.int32)[None, None, :], axis=1
    )
    live = jnp.repeat(chosen, BLOCK_LEN, axis=1)[:, None, :]
    score = jnp.einsum("qhc,tc->qht", qfull, keys, preferred_element_type=jnp.float32) * scale
    score = jnp.where(live, score, -jnp.inf)
    prob = jax.nn.softmax(score, axis=-1)
    prob_low = prob.astype(jnp.bfloat16)
    olat = jnp.einsum("qht,tl->qhl", prob_low, keys_lat, preferred_element_type=jnp.float32).astype(
        jnp.bfloat16
    )
    attn_out = jnp.einsum(
        "qhl,hlv->qhv", olat, weight_v, preferred_element_type=jnp.float32
    ).astype(jnp.bfloat16)
    d_olat = jnp.einsum("qhv,hlv->qhl", d_out, weight_v, preferred_element_type=jnp.float32).astype(
        jnp.bfloat16
    )
    dprob = jnp.einsum("qhl,tl->qht", d_olat, keys_lat, preferred_element_type=jnp.float32)
    delta = jnp.sum(prob * dprob, axis=-1, keepdims=True)
    dscore = (prob * (dprob - delta) * scale).astype(jnp.bfloat16)
    dquery = jnp.einsum("qht,tc->qhc", dscore, keys, preferred_element_type=jnp.float32)
    d_q_rope = dquery[:, :, latent:].astype(jnp.bfloat16)
    d_qlat = dquery[:, :, :latent].astype(jnp.bfloat16)
    d_q_nope = jnp.einsum(
        "qhl,hnl->qhn", d_qlat, weight_k, preferred_element_type=jnp.float32
    ).astype(jnp.bfloat16)
    value_part = jnp.einsum("qht,qhl->tl", prob_low, d_olat, preferred_element_type=jnp.float32)
    dkeys = jnp.einsum("qht,qhc->tc", dscore, qfull, preferred_element_type=jnp.float32)
    dkeys = dkeys + jnp.pad(value_part, ((0, 0), (0, rope)))
    one_hot = (
        asked.reshape(-1)[:, None] == jnp.arange(own_blocks, dtype=jnp.int32)[None, :]
    ).astype(jnp.float32)
    returned = lax.all_to_all(
        dkeys.reshape(peers, per_peer, BLOCK_LEN * width).astype(jnp.bfloat16),
        "seq",
        split_axis=0,
        concat_axis=0,
        tiled=True,
    ).astype(jnp.float32)
    local_grad = jnp.dot(
        one_hot.T,
        returned.reshape(peers * per_peer, BLOCK_LEN * width),
        precision=lax.Precision.HIGHEST,
    )
    d_cache = (
        lax.psum(local_grad.astype(jnp.bfloat16), "grp")
        .astype(jnp.float32)
        .reshape(own_blocks * BLOCK_LEN, width)
    )
    return (attn_out, d_q_nope, d_q_rope, d_cache)


def solution(mesh):
    return jax.shard_map(
        local,
        mesh=mesh,
        in_specs=(
            P("seq", "grp", None),
            P("seq", "grp", None),
            P("seq", None),
            P("grp", "seq"),
            P("grp", "seq"),
            P("seq", "grp", None),
            P("seq", None),
            P("seq", None),
        ),
        out_specs=(
            P("seq", "grp", None),
            P("seq", "grp", None),
            P("seq", "grp", None),
            P("seq", None),
        ),
        check_vma=False,
    )
```

profile of v0, /device:TPU:0, one launch (start us, length us, event | category | flops | bytes accessed | tf_op | source)
XLA Modules:
  0.0 205.2 jit_solution(208259498661212888)
XLA Ops:
  0.7 1.3 copy-done.1
  2.6 4.1 %collective-permute-start.1 = (bf16[144,1024]{1,0:T(8,128)(2,1)S(1)}, bf16[144,1024]{1,0:T(8,128)(2,1)S(1)}, u32[]{:S(2)}, u32[]{:S(2)}) collective-permute-start(bf16[144,1024]{1,0:T(8,128)(2,1)S(1)} %cut.1.refs_0_), channel_id=1, source_target_pairs={{0,16},{4,20},{8,24},{12,28},{16,0},{20,4},{24,8},{28,12},{1,17},{... | collective-permute-start | bytes 884744 | tf_op jit(solution)/shard_map/ppermute | solution.py:57
  6.7 1.6 collective-permute-start
  8.3 1.5 collective-permute-start.3
  9.8 10.3 %collective-permute-done.1.refs_2_ = bf16[144,1024]{1,0:T(8,128)(2,1)S(1)} collective-permute-done((bf16[144,1024]{1,0:T(8,128)(2,1)S(1)}, bf16[144,1024]{1,0:T(8,128)(2,1)S(1)}, u32[]{:S(2)}, u32[]{:S(2)}) %collective-permute-start.1) | collective-permute-done | bytes 294944 | tf_op jit(solution)/shard_map/ppermute | solution.py:57
  21.5 2.9 %collective-permute-start.6 = (s32[2,64]{1,0:T(2,128)S(1)}, s32[2,64]{1,0:T(2,128)S(1)}, u32[]{:S(2)}, u32[]{:S(2)}) collective-permute-start(s32[2,64]{1,0:T(2,128)S(1)} %pad_add_fusion), channel_id=1, source_target_pairs={{0,24},{4,28},{8,16},{12,20},{16,8},{20,12},{24,0},{28,4},{1,25},{... | collective-permute-start | bytes 1544 | tf_op jit(solution)/shard_map/ppermute | solution.py:57
  25.0 0.9 collective-permute-start.4
  25.9 1.1 pad_maximum_fusion.refs_0_
  27.1 3.7 %collective-permute-done.6 = s32[2,64]{1,0:T(2,128)S(1)} collective-permute-done((s32[2,64]{1,0:T(2,128)S(1)}, s32[2,64]{1,0:T(2,128)S(1)}, u32[]{:S(2)}, u32[]{:S(2)}) %collective-permute-start.6) | collective-permute-done | bytes 544 | tf_op jit(solution)/shard_map/ppermute | solution.py:57
  30.8 4.0 %all-to-all-start = ((bf16[32,160,128]{2,1,0:T(8,128)(2,1)}), bf16[32,160,128]{2,1,0:T(8,128)(2,1)S(1)}, u32[]{:S(2)}, u32[]{:S(2)}) async-start(bf16[32,160,128]{2,1,0:T(8,128)(2,1)} %after.2), calls=%async_computation | async-start | bytes 2621440 | tf_op jit(solution)/shard_map/all_to_all | solution.py:61
  34.9 3.3 %gather.1 = (bf16[144,2048]{1,0:T(8,128)(2,1)S(1)}, bf16[144,2048]{1,0:T(8,128)(2,1)S(1)}) custom-call(s32[2]{0:T(128)S(1)} %pad_add_fusion.1.ids, s32[1,64]{1,0:T(1,128)S(1)} %copy-done.12, s32[1,64]{1,0:T(1,128)S(1)} %collective-permute-done.3.other, bf16[144,1024]{1,0:T(8,128)(2,1)S(1)} %cut.1.refs_0_, ...), custom_call_target="tpu_custom_call" | custom-call | tf_op jit(solution)/shard_map/gather/pallas_call | solution.py:35
  38.2 2.1 %collective-permute-start.7 = (bf16[144,2048]{1,0:T(8,128)(2,1)S(1)}, bf16[144,2048]{1,0:T(8,128)(2,1)S(1)}, u32[]{:S(2)}, u32[]{:S(2)}) collective-permute-start(bf16[144,2048]{1,0:T(8,128)(2,1)S(1)} %get-tuple-element.25), channel_id=1, source_target_pairs={{0,4},{4,0},{8,12},{12,8},{16,20},{20,16},{24,28},{28,24},{1,5},{5... | collective-permute-start | bytes 1769480 | tf_op jit(solution)/shard_map/ppermute | solution.py:57
  40.3 1.5 collective-permute-start.8
  41.8 21.6 %collective-permute-done.7.away.refs_4_ = bf16[144,2048]{1,0:T(8,128)(2,1)S(1)} collective-permute-done((bf16[144,2048]{1,0:T(8,128)(2,1)S(1)}, bf16[144,2048]{1,0:T(8,128)(2,1)S(1)}, u32[]{:S(2)}, u32[]{:S(2)}) %collective-permute-start.7) | collective-permute-done | bytes 589856 | tf_op jit(solution)/shard_map/ppermute | solution.py:57
  63.4 2.4 %all-to-all-done = bf16[32,160,128]{2,1,0:T(8,128)(2,1)S(1)} async-done(((bf16[32,160,128]{2,1,0:T(8,128)(2,1)}), bf16[32,160,128]{2,1,0:T(8,128)(2,1)S(1)}, u32[]{:S(2)}, u32[]{:S(2)}) %all-to-all-start) | async-done | bytes 1310752 | tf_op jit(solution)/shard_map/all_to_all | solution.py:61
  65.7 1.4 expand.1
  67.1 4.6 %all-to-all-start.1 = ((bf16[8,4,16,1024]{3,2,1,0:T(8,128)(2,1)}), bf16[8,4,16,1024]{3,2,1,0:T(8,128)(2,1)}, u32[]{:S(2)}, u32[]{:S(2)}) async-start(bf16[8,4,16,1024]{3,2,1,0:T(8,128)(2,1)} %expand.1), calls=%async_computation.1 | async-start | bytes 2097152 | tf_op jit(solution)/shard_map/all_to_all | solution.py:61
  71.7 1.6 collective-permute-start.12
  73.8 11.9 %collective-permute-done.12.refs_6_ = bf16[144,2048]{1,0:T(8,128)(2,1)S(1)} collective-permute-done((bf16[144,2048]{1,0:T(8,128)(2,1)S(1)}, bf16[144,2048]{1,0:T(8,128)(2,1)S(1)}, u32[]{:S(2)}, u32[]{:S(2)}) %collective-permute-start.12) | collective-permute-done | bytes 589856 | tf_op jit(solution)/shard_map/ppermute | solution.py:57
  85.8 0.9 copy-done.3
  86.7 0.8 copy-done.5
  88.3 8.7 %all-to-all-done.1 = bf16[8,4,16,1024]{3,2,1,0:T(8,128)(2,1)} async-done(((bf16[8,4,16,1024]{3,2,1,0:T(8,128)(2,1)}), bf16[8,4,16,1024]{3,2,1,0:T(8,128)(2,1)}, u32[]{:S(2)}, u32[]{:S(2)}) %all-to-all-start.1) | async-done | bytes 1048608 | tf_op jit(solution)/shard_map/all_to_all | solution.py:61
  97.0 1.1 copy-done.4
  98.1 1.1 copy-done.6
  99.1 1.1 copy-done.8
  100.2 21.1 %attend.1 = (bf16[2,144,2048]{2,1,0:T(8,128)(2,1)}, bf16[2,144,2048]{2,1,0:T(8,128)(2,1)}, bf16[2,144,2048]{2,1,0:T(8,128)(2,1)}, bf16[2,144,2048]{2,1,0:T(8,128...) custom-call(s32[2]{0:T(128)S(1)} %pad_add_fusion.1.ids, s32[16,32]{1,0:T(8,128)S(1)} %copy-done.11, ...), custom_call_target="tpu_custom_call" | custom-call | tf_op jit(solution)/shard_map/attend/pallas_call | solution.py:35
  122.5 3.6 %all-to-all-start.2 = ((bf16[8,4,16,1024]{3,2,1,0:T(8,128)(2,1)}), bf16[8,4,16,1024]{3,2,1,0:T(8,128)(2,1)S(1)}, u32[]{:S(2)}, u32[]{:S(2)}) async-start(bf16[8,4,16,1024]{3,2,1,0:T(8,128)(2,1)} %bitcast.38), calls=%async_computation.2 | async-start | bytes 2097152 | tf_op jit(solution)/shard_map/all_to_all | solution.py:61
  126.1 1.6 pair.2
  127.7 1.6 collective-permute-start.16
  129.3 1.5 pair.3
  130.8 12.2 %collective-permute-done.16.refs_2_ = bf16[144,2048]{1,0:T(8,128)(2,1)S(1)} collective-permute-done((bf16[144,2048]{1,0:T(8,128)(2,1)S(1)}, bf16[144,2048]{1,0:T(8,128)(2,1)S(1)}, u32[]{:S(2)}, u32[]{:S(2)}) %collective-permute-start.16) | collective-permute-done | bytes 589856 | tf_op jit(solution)/shard_map/ppermute | solution.py:57
  143.2 1.6 collective-permute-start.17
  144.7 12.9 %collective-permute-done.17.got = bf16[144,2048]{1,0:T(8,128)(2,1)S(1)} collective-permute-done((bf16[144,2048]{1,0:T(8,128)(2,1)S(1)}, bf16[144,2048]{1,0:T(8,128)(2,1)S(1)}, u32[]{:S(2)}, u32[]{:S(2)}) %collective-permute-start.17) | collective-permute-done | bytes 589856 | tf_op jit(solution)/shard_map/ppermute | solution.py:57
  157.8 1.4 collective-permute-start.18
  159.2 1.1 reduce.1.refs_1_
  160.3 4.7 %collective-permute-done.18.refs_1_ = bf16[144,1024]{1,0:T(8,128)(2,1)S(1)} collective-permute-done((bf16[144,1024]{1,0:T(8,128)(2,1)S(1)}, bf16[144,1024]{1,0:T(8,128)(2,1)S(1)}, u32[]{:S(2)}, u32[]{:S(2)}) %collective-permute-start.18) | collective-permute-done | bytes 294944 | tf_op jit(solution)/shard_map/ppermute | solution.py:57
  165.1 1.1 collective-permute-start.19
  166.1 2.4 %collective-permute-start.20 = (bf16[144,512]{1,0:T(8,128)(2,1)S(1)}, bf16[144,512]{1,0:T(8,128)(2,1)S(1)}, u32[]{:S(2)}, u32[]{:S(2)}) collective-permute-start(bf16[144,512]{1,0:T(8,128)(2,1)S(1)} %copy-done.16), channel_id=1, source_target_pairs={{0,16},{4,20},{8,24},{12,28},{16,0},{20,4},{24,8},{28,12},{1,17},{... | collective-permute-start | bytes 442376 | tf_op jit(solution)/shard_map/ppermute | solution.py:57
  168.5 1.4 collective-permute-start.21
  170.0 2.4 %collective-permute-start.22 = (bf16[144,512]{1,0:T(8,128)(2,1)S(1)}, bf16[144,512]{1,0:T(8,128)(2,1)S(1)}, u32[]{:S(2)}, u32[]{:S(2)}) collective-permute-start(bf16[144,512]{1,0:T(8,128)(2,1)S(1)} %get-tuple-element.44), channel_id=1, source_target_pairs={{0,24},{4,28},{8,16},{12,20},{16,8},{20,12},{24,0},{28,4},{1,25},{... | collective-permute-start | bytes 442376 | tf_op jit(solution)/shard_map/ppermute | solution.py:57
  172.3 1.4 collective-permute-start.23
  173.8 4.6 %all-to-all-start.3 = ((bf16[8,4,16,256]{3,2,1,0:T(8,128)(2,1)}), bf16[8,4,16,256]{3,2,1,0:T(8,128)(2,1)S(1)}, u32[]{:S(2)}, u32[]{:S(2)}) async-start(bf16[8,4,16,256]{3,2,1,0:T(8,128)(2,1)} %reduce.1.refs_1_), calls=%async_computation.3 | async-start | bytes 524288 | tf_op jit(solution)/shard_map/all_to_all | solution.py:61
  178.3 3.2 %collective-permute-done.20.refs_3_ = bf16[144,512]{1,0:T(8,128)(2,1)S(1)} collective-permute-done((bf16[144,512]{1,0:T(8,128)(2,1)S(1)}, bf16[144,512]{1,0:T(8,128)(2,1)S(1)}, u32[]{:S(2)}, u32[]{:S(2)}) %collective-permute-start.20) | collective-permute-done | bytes 147488 | tf_op jit(solution)/shard_map/ppermute | solution.py:57
  181.5 10.7 %collective-permute-done.21.refs_4_ = bf16[144,512]{1,0:T(8,128)(2,1)S(1)} collective-permute-done((bf16[144,512]{1,0:T(8,128)(2,1)S(1)}, bf16[144,512]{1,0:T(8,128)(2,1)S(1)}, u32[]{:S(2)}, u32[]{:S(2)}) %collective-permute-start.21) | collective-permute-done | bytes 147488 | tf_op jit(solution)/shard_map/ppermute | solution.py:57
  192.2 2.0 scatter.1.refs_0_
  194.2 1.6 collective-permute-start.25
  195.7 5.2 %collective-permute-done.25.refs_2_ = bf16[144,1024]{1,0:T(8,128)(2,1)S(1)} collective-permute-done((bf16[144,1024]{1,0:T(8,128)(2,1)S(1)}, bf16[144,1024]{1,0:T(8,128)(2,1)S(1)}, u32[]{:S(2)}, u32[]{:S(2)}) %collective-permute-start.25) | collective-permute-done | bytes 294944 | tf_op jit(solution)/shard_map/ppermute | solution.py:57
  203.1 2.1 %assemble.1 = f32[576,1024]{1,0:T(8,128)} custom-call(s32[2]{0:T(128)S(1)} %pad_add_fusion.1.ids, bf16[144,1024]{1,0:T(8,128)(2,1)S(1)} %scatter.1.refs_0_, bf16[144,1024]{1,0:T(8,128)(2,1)S(1)} %collective-permute-done.24.refs_1_, bf16[144,1024]{1,0:T(8,128)(2,1)S(1)} %collective-permute-done.25.refs_2_, bf16[144,1024]{1,0:T(8,128)(2,1)S(1)} %collective-permute-done.26.refs_3_), custom_call_target="tpu_custom_call" | custom-call | tf_op jit(solution)/shard_map/assemble/pallas_call | solution.py:35
  (88 shorter events, 7.7 us)
Async XLA Ops:
  0.6 7.6 %copy-start.12 = (s32[1,64]{1,0:T(1,128)S(1)}, s32[1,64]{1,0:T(1,128)}, u32[]{:S(2)}) copy-start(s32[1,64]{1,0:T(1,128)} %own.1) | copy-start | bytes 772
  0.7 1.3 copy-start.1
  2.0 18.7 %copy-start.21 = (bf16[16,32,128]{2,1,0:T(8,128)(2,1)S(1)}, bf16[16,32,128]{2,1,0:T(8,128)(2,1)}, u32[]{:S(2)}) copy-start(bf16[16,32,128]{2,1,0:T(8,128)(2,1)} %param.13) | copy-start | bytes 393220
  2.0 18.7 %copy-start.22 = (bf16[16,32,128]{2,1,0:T(8,128)(2,1)S(1)}, bf16[16,32,128]{2,1,0:T(8,128)(2,1)}, u32[]{:S(2)}) copy-start(bf16[16,32,128]{2,1,0:T(8,128)(2,1)} %param.8) | copy-start | bytes 393220
  2.0 18.9 %copy-start.18 = (bf16[32,8192]{1,0:T(8,128)(2,1)S(1)}, bf16[32,8192]{1,0:T(8,128)(2,1)}, u32[]{:S(2)}) copy-start(bf16[32,8192]{1,0:T(8,128)(2,1)} %param.11) | copy-start | bytes 1572868
  2.6 18.8 %copy-start.19 = (bf16[32,8192]{1,0:T(8,128)(2,1)S(1)}, bf16[32,8192]{1,0:T(8,128)(2,1)}, u32[]{:S(2)}) copy-start(bf16[32,8192]{1,0:T(8,128)(2,1)} %param.12) | copy-start | bytes 1572868
  2.6 17.5 %collective-permute-start.1 = (bf16[144,1024]{1,0:T(8,128)(2,1)S(1)}, bf16[144,1024]{1,0:T(8,128)(2,1)S(1)}, u32[]{:S(2)}, u32[]{:S(2)}) collective-permute-start(bf16[144,1024]{1,0:T(8,128)(2,1)S(1)} %cut.1.refs_0_), channel_id=1, source_target_pairs={{0,16},{4,20},{8,24},{12,28},{16,0},{20,4},{24,8},{28,12},{1,17},{... | collective-permute-start | bytes 884744 | tf_op jit(solution)/shard_map/ppermute | solution.py:57
  6.7 24.1 %collective-permute-start = (bf16[144,1024]{1,0:T(8,128)(2,1)S(1)}, bf16[144,1024]{1,0:T(8,128)(2,1)S(1)}, u32[]{:S(2)}, u32[]{:S(2)}) collective-permute-start(bf16[144,1024]{1,0:T(8,128)(2,1)S(1)} %cut.1.refs_0_), channel_id=1, source_target_pairs={{0,8},{4,12},{8,0},{12,4},{16,24},{20,28},{24,16},{28,20},{1,9},{5... | collective-permute-start | bytes 884744 | tf_op jit(solution)/shard_map/ppermute | solution.py:57
  8.3 13.2 %collective-permute-start.3 = (s32[1,64]{1,0:T(1,128)S(1)}, s32[1,64]{1,0:T(1,128)S(1)}, u32[]{:S(2)}, u32[]{:S(2)}) collective-permute-start(s32[1,64]{1,0:T(1,128)S(1)} %copy-done.12), channel_id=1, source_target_pairs={{0,4},{4,0},{8,12},{12,8},{16,20},{20,16},{24,28},{28,24},{1,5},{5... | collective-permute-start | bytes 776 | tf_op jit(solution)/shard_map/ppermute | solution.py:57
  20.1 10.7 %collective-permute-start.2 = (bf16[144,1024]{1,0:T(8,128)(2,1)S(1)}, bf16[144,1024]{1,0:T(8,128)(2,1)S(1)}, u32[]{:S(2)}, u32[]{:S(2)}) collective-permute-start(bf16[144,1024]{1,0:T(8,128)(2,1)S(1)} %collective-permute-done.1.refs_2_), channel_id=1, source_target_pairs={{0,8},{4,12},{8,0},{12,4},{16,24},{20,28},{24,16},{28,20},{1,9},{5... | collective-permute-start | bytes 884744 | tf_op jit(solution)/shard_map/ppermute | solution.py:57
  21.5 9.3 %collective-permute-start.6 = (s32[2,64]{1,0:T(2,128)S(1)}, s32[2,64]{1,0:T(2,128)S(1)}, u32[]{:S(2)}, u32[]{:S(2)}) collective-permute-start(s32[2,64]{1,0:T(2,128)S(1)} %pad_add_fusion), channel_id=1, source_target_pairs={{0,24},{4,28},{8,16},{12,20},{16,8},{20,12},{24,0},{28,4},{1,25},{... | collective-permute-start | bytes 1544 | tf_op jit(solution)/shard_map/ppermute | solution.py:57
  24.4 6.4 %collective-permute-start.5 = (s32[2,64]{1,0:T(2,128)S(1)}, s32[2,64]{1,0:T(2,128)S(1)}, u32[]{:S(2)}, u32[]{:S(2)}) collective-permute-start(s32[2,64]{1,0:T(2,128)S(1)} %pad_add_fusion), channel_id=1, source_target_pairs={{0,16},{4,20},{8,24},{12,28},{16,0},{20,4},{24,8},{28,12},{1,17},{... | collective-permute-start | bytes 1544 | tf_op jit(solution)/shard_map/ppermute | solution.py:57
  25.0 5.8 %collective-permute-start.4 = (s32[2,64]{1,0:T(2,128)S(1)}, s32[2,64]{1,0:T(2,128)S(1)}, u32[]{:S(2)}, u32[]{:S(2)}) collective-permute-start(s32[2,64]{1,0:T(2,128)S(1)} %pad_add_fusion), channel_id=1, source_target_pairs={{0,8},{4,12},{8,0},{12,4},{16,24},{20,28},{24,16},{28,20},{1,9},{5... | collective-permute-start | bytes 1544 | tf_op jit(solution)/shard_map/ppermute | solution.py:57
  30.8 34.9 %all-to-all-start = ((bf16[32,160,128]{2,1,0:T(8,128)(2,1)}), bf16[32,160,128]{2,1,0:T(8,128)(2,1)S(1)}, u32[]{:S(2)}, u32[]{:S(2)}) async-start(bf16[32,160,128]{2,1,0:T(8,128)(2,1)} %after.2), calls=%async_computation | async-start | bytes 2621440 | tf_op jit(solution)/shard_map/all_to_all | solution.py:61
  38.2 25.1 %collective-permute-start.7 = (bf16[144,2048]{1,0:T(8,128)(2,1)S(1)}, bf16[144,2048]{1,0:T(8,128)(2,1)S(1)}, u32[]{:S(2)}, u32[]{:S(2)}) collective-permute-start(bf16[144,2048]{1,0:T(8,128)(2,1)S(1)} %get-tuple-element.25), channel_id=1, source_target_pairs={{0,4},{4,0},{8,12},{12,8},{16,20},{20,16},{24,28},{28,24},{1,5},{5... | collective-permute-start | bytes 1769480 | tf_op jit(solution)/shard_map/ppermute | solution.py:57
  40.3 23.1 %collective-permute-start.8 = (bf16[144,2048]{1,0:T(8,128)(2,1)S(1)}, bf16[144,2048]{1,0:T(8,128)(2,1)S(1)}, u32[]{:S(2)}, u32[]{:S(2)}) collective-permute-start(bf16[144,2048]{1,0:T(8,128)(2,1)S(1)} %get-tuple-element.26.refs_0_), channel_id=1, source_target_pairs={{0,2},{1,3},{2,0},{3,1},{4,6},{5,7},{6,4},{7,5},{8,10},{9,11},{10,... | collective-permute-start | bytes 1769480 | tf_op jit(solution)/shard_map/ppermute | solution.py:57
  67.1 18.6 %copy-start.20 = (bf16[16,32,64]{2,1,0:T(8,128)(2,1)S(1)}, bf16[16,32,64]{2,1,0:T(8,128)(2,1)}, u32[]{:S(2)}) copy-start(bf16[16,32,64]{2,1,0:T(8,128)(2,1)} %param.9) | copy-start | bytes 196612
  67.1 29.9 %copy-start.11 = (s32[16,32]{1,0:T(8,128)S(1)}, s32[16,32]{1,0:T(8,128)}, u32[]{:S(2)}) copy-start(s32[16,32]{1,0:T(8,128)} %sel.1) | copy-start | bytes 6148
  67.1 29.9 %all-to-all-start.1 = ((bf16[8,4,16,1024]{3,2,1,0:T(8,128)(2,1)}), bf16[8,4,16,1024]{3,2,1,0:T(8,128)(2,1)}, u32[]{:S(2)}, u32[]{:S(2)}) async-start(bf16[8,4,16,1024]{3,2,1,0:T(8,128)(2,1)} %expand.1), calls=%async_computation.1 | async-start | bytes 2097152 | tf_op jit(solution)/shard_map/all_to_all | solution.py:61
  71.7 14.0 %collective-permute-start.12 = (bf16[144,2048]{1,0:T(8,128)(2,1)S(1)}, bf16[144,2048]{1,0:T(8,128)(2,1)S(1)}, u32[]{:S(2)}, u32[]{:S(2)}) collective-permute-start(bf16[144,2048]{1,0:T(8,128)(2,1)S(1)} %collective-permute-done.7.away.refs_4_), channel_id=1, source_target_pairs={{0,2},{1,3},{2,0},{3,1},{4,6},{5,7},{6,4},{7,5},{8,10},{9,11},{10,... | collective-permute-start | bytes 1769480 | tf_op jit(solution)/shard_map/ppermute | solution.py:57
  73.3 12.5 %collective-permute-start.9 = (bf16[144,2048]{1,0:T(8,128)(2,1)S(1)}, bf16[144,2048]{1,0:T(8,128)(2,1)S(1)}, u32[]{:S(2)}, u32[]{:S(2)}) collective-permute-start(bf16[144,2048]{1,0:T(8,128)(2,1)S(1)} %get-tuple-element.26.refs_0_), channel_id=1, source_target_pairs={{0,1},{1,0},{2,3},{3,2},{4,5},{5,4},{6,7},{7,6},{8,9},{9,8},{10,11... | collective-permute-start | bytes 1769480 | tf_op jit(solution)/shard_map/ppermute | solution.py:57
  73.3 13.4 %collective-permute-start.11 = (bf16[144,2048]{1,0:T(8,128)(2,1)S(1)}, bf16[144,2048]{1,0:T(8,128)(2,1)S(1)}, u32[]{:S(2)}, u32[]{:S(2)}) collective-permute-start(bf16[144,2048]{1,0:T(8,128)(2,1)S(1)} %collective-permute-done.7.away.refs_4_), channel_id=1, source_target_pairs={{0,1},{1,0},{2,3},{3,2},{4,5},{5,4},{6,7},{7,6},{8,9},{9,8},{10,11... | collective-permute-start | bytes 1769480 | tf_op jit(solution)/shard_map/ppermute | solution.py:57
  73.8 13.7 %collective-permute-start.10 = (bf16[144,2048]{1,0:T(8,128)(2,1)S(1)}, bf16[144,2048]{1,0:T(8,128)(2,1)S(1)}, u32[]{:S(2)}, u32[]{:S(2)}) collective-permute-start(bf16[144,2048]{1,0:T(8,128)(2,1)S(1)} %collective-permute-done.8.over_x.refs_2_), channel_id=1, source_target_pairs={{0,1},{1,0},{2,3},{3,2},{4,5},{5,4},{6,7},{7,6},{8,9},{9,8},{10,11... | collective-permute-start | bytes 1769480 | tf_op jit(solution)/shard_map/ppermute | solution.py:57
  85.7 1.8 copy-start.17
  85.7 2.6 %collective-permute-start.13 = (bf16[144,2048]{1,0:T(8,128)(2,1)S(1)}, bf16[144,2048]{1,0:T(8,128)(2,1)}, u32[]{:S(2)}, u32[]{:S(2)}) collective-permute-start(bf16[144,2048]{1,0:T(8,128)(2,1)S(1)} %collective-permute-done.12.refs_6_), channel_id=1, source_target_pairs={{0,1},{1,0},{2,3},{3,2},{4,5},{5,4},{6,7},{7,6},{8,9},{9,8},{10,11... | collective-permute-start | bytes 1769480 | tf_op jit(solution)/shard_map/ppermute | solution.py:57
  97.0 1.1 copy-start.4
  122.0 4.1 %copy-start = (bf16[2,144,2048]{2,1,0:T(8,128)(2,1)S(1)}, bf16[2,144,2048]{2,1,0:T(8,128)(2,1)}, u32[]{:S(2)}) copy-start(bf16[2,144,2048]{2,1,0:T(8,128)(2,1)} %get-tuple-element.29.keep) | copy-start | bytes 3538948
  122.0 4.1 %collective-permute-start.14 = (bf16[2,144,2048]{2,1,0:T(8,128)(2,1)}, bf16[2,144,2048]{2,1,0:T(8,128)(2,1)}, u32[]{:S(2)}, u32[]{:S(2)}) collective-permute-start(bf16[2,144,2048]{2,1,0:T(8,128)(2,1)} %get-tuple-element.30), channel_id=1, source_target_pairs={{0,1},{1,0},{2,3},{3,2},{4,5},{5,4},{6,7},{7,6},{8,9},{9,8},{10,11... | collective-permute-start | bytes 3538952 | tf_op jit(solution)/shard_map/ppermute | solution.py:57
  122.0 7.3 %collective-permute-start.15 = (bf16[2,144,2048]{2,1,0:T(8,128)(2,1)}, bf16[2,144,2048]{2,1,0:T(8,128)(2,1)}, u32[]{:S(2)}, u32[]{:S(2)}) collective-permute-start(bf16[2,144,2048]{2,1,0:T(8,128)(2,1)} %get-tuple-element.33), channel_id=1, source_target_pairs={{0,1},{1,0},{2,3},{3,2},{4,5},{5,4},{6,7},{7,6},{8,9},{9,8},{10,11... | collective-permute-start | bytes 3538952 | tf_op jit(solution)/shard_map/ppermute | solution.py:57
  122.5 36.7 %all-to-all-start.2 = ((bf16[8,4,16,1024]{3,2,1,0:T(8,128)(2,1)}), bf16[8,4,16,1024]{3,2,1,0:T(8,128)(2,1)S(1)}, u32[]{:S(2)}, u32[]{:S(2)}) async-start(bf16[8,4,16,1024]{3,2,1,0:T(8,128)(2,1)} %bitcast.38), calls=%async_computation.2 | async-start | bytes 2097152 | tf_op jit(solution)/shard_map/all_to_all | solution.py:61
  126.0 3.2 %copy-start.2 = (bf16[2,144,2048]{2,1,0:T(8,128)(2,1)S(1)}, bf16[2,144,2048]{2,1,0:T(8,128)(2,1)}, u32[]{:S(2)}) copy-start(bf16[2,144,2048]{2,1,0:T(8,128)(2,1)} %get-tuple-element.32.refs_1_) | copy-start | bytes 3538948
  127.7 15.3 %collective-permute-start.16 = (bf16[144,2048]{1,0:T(8,128)(2,1)S(1)}, bf16[144,2048]{1,0:T(8,128)(2,1)S(1)}, u32[]{:S(2)}, u32[]{:S(2)}) collective-permute-start(bf16[144,2048]{1,0:T(8,128)(2,1)S(1)} %get-tuple-element.37), channel_id=1, source_target_pairs={{0,2},{1,3},{2,0},{3,1},{4,6},{5,7},{6,4},{7,5},{8,10},{9,11},{10,... | collective-permute-start | bytes 1769480 | tf_op jit(solution)/shard_map/ppermute | solution.py:57
  143.1 14.6 %copy-start.13 = (bf16[144,512]{1,0:T(8,128)(2,1)}, bf16[144,512]{1,0:T(8,128)(2,1)S(1)}, u32[]{:S(2)}) copy-start(bf16[144,512]{1,0:T(8,128)(2,1)S(1)} %get-tuple-element.43) | copy-start | bytes 442372
  143.2 14.6 %copy-start.15 = (bf16[144,512]{1,0:T(8,128)(2,1)}, bf16[144,512]{1,0:T(8,128)(2,1)S(1)}, u32[]{:S(2)}) copy-start(bf16[144,512]{1,0:T(8,128)(2,1)S(1)} %get-tuple-element.42) | copy-start | bytes 442372
  143.2 14.4 %collective-permute-start.17 = (bf16[144,2048]{1,0:T(8,128)(2,1)S(1)}, bf16[144,2048]{1,0:T(8,128)(2,1)S(1)}, u32[]{:S(2)}, u32[]{:S(2)}) collective-permute-start(bf16[144,2048]{1,0:T(8,128)(2,1)S(1)} %get-tuple-element.38), channel_id=1, source_target_pairs={{0,2},{1,3},{2,0},{3,1},{4,6},{5,7},{6,4},{7,5},{8,10},{9,11},{10,... | collective-permute-start | bytes 1769480 | tf_op jit(solution)/shard_map/ppermute | solution.py:57
  157.8 7.2 %collective-permute-start.18 = (bf16[144,1024]{1,0:T(8,128)(2,1)S(1)}, bf16[144,1024]{1,0:T(8,128)(2,1)S(1)}, u32[]{:S(2)}, u32[]{:S(2)}) collective-permute-start(bf16[144,1024]{1,0:T(8,128)(2,1)S(1)} %get-tuple-element.40), channel_id=1, source_target_pairs={{0,4},{4,0},{8,12},{12,8},{16,20},{20,16},{24,28},{28,24},{1,5},{5... | collective-permute-start | bytes 884744 | tf_op jit(solution)/shard_map/ppermute | solution.py:57
  160.3 5.8 %copy-start.16 = (bf16[144,512]{1,0:T(8,128)(2,1)S(1)}, bf16[144,512]{1,0:T(8,128)(2,1)}, u32[]{:S(2)}) copy-start(bf16[144,512]{1,0:T(8,128)(2,1)} %copy-done.15) | copy-start | bytes 442372
  160.3 8.2 %copy-start.14 = (bf16[144,512]{1,0:T(8,128)(2,1)S(1)}, bf16[144,512]{1,0:T(8,128)(2,1)}, u32[]{:S(2)}) copy-start(bf16[144,512]{1,0:T(8,128)(2,1)} %copy-done.13) | copy-start | bytes 442372
  165.0 35.9 %copy-start.10 = (bf16[512,64]{1,0:T(8,128)(2,1)S(1)}, bf16[512,64]{1,0:T(8,128)(2,1)}, u32[]{:S(2)}) copy-start(bf16[512,64]{1,0:T(8,128)(2,1)} %copy-done.9) | copy-start | bytes 196612
  165.1 27.1 %collective-permute-start.19 = (bf16[144,1024]{1,0:T(8,128)(2,1)S(1)}, bf16[144,1024]{1,0:T(8,128)(2,1)S(1)}, u32[]{:S(2)}, u32[]{:S(2)}) collective-permute-start(bf16[144,1024]{1,0:T(8,128)(2,1)S(1)} %after.3), channel_id=1, source_target_pairs={{0,8},{4,12},{8,0},{12,4},{16,24},{20,28},{24,16},{28,20},{1,9},{5... | collective-permute-start | bytes 884744 | tf_op jit(solution)/shard_map/ppermute | solution.py:57
  166.1 15.4 %collective-permute-start.20 = (bf16[144,512]{1,0:T(8,128)(2,1)S(1)}, bf16[144,512]{1,0:T(8,128)(2,1)S(1)}, u32[]{:S(2)}, u32[]{:S(2)}) collective-permute-start(bf16[144,512]{1,0:T(8,128)(2,1)S(1)} %copy-done.16), channel_id=1, source_target_pairs={{0,16},{4,20},{8,24},{12,28},{16,0},{20,4},{24,8},{28,12},{1,17},{... | collective-permute-start | bytes 442376 | tf_op jit(solution)/shard_map/ppermute | solution.py:57
  168.5 23.7 %collective-permute-start.21 = (bf16[144,512]{1,0:T(8,128)(2,1)S(1)}, bf16[144,512]{1,0:T(8,128)(2,1)S(1)}, u32[]{:S(2)}, u32[]{:S(2)}) collective-permute-start(bf16[144,512]{1,0:T(8,128)(2,1)S(1)} %copy-done.14), channel_id=1, source_target_pairs={{0,20},{4,16},{8,28},{12,24},{16,4},{20,0},{24,12},{28,8},{1,21},{... | collective-permute-start | bytes 442376 | tf_op jit(solution)/shard_map/ppermute | solution.py:57
  170.0 22.2 %collective-permute-start.22 = (bf16[144,512]{1,0:T(8,128)(2,1)S(1)}, bf16[144,512]{1,0:T(8,128)(2,1)S(1)}, u32[]{:S(2)}, u32[]{:S(2)}) collective-permute-start(bf16[144,512]{1,0:T(8,128)(2,1)S(1)} %get-tuple-element.44), channel_id=1, source_target_pairs={{0,24},{4,28},{8,16},{12,20},{16,8},{20,12},{24,0},{28,4},{1,25},{... | collective-permute-start | bytes 442376 | tf_op jit(solution)/shard_map/ppermute | solution.py:57
  172.3 19.9 %collective-permute-start.23 = (bf16[144,512]{1,0:T(8,128)(2,1)S(1)}, bf16[144,512]{1,0:T(8,128)(2,1)S(1)}, u32[]{:S(2)}, u32[]{:S(2)}) collective-permute-start(bf16[144,512]{1,0:T(8,128)(2,1)S(1)} %get-tuple-element.45), channel_id=1, source_target_pairs={{0,28},{4,24},{8,20},{12,16},{16,12},{20,8},{24,4},{28,0},{1,29},{... | collective-permute-start | bytes 442376 | tf_op jit(solution)/shard_map/ppermute | solution.py:57
  173.8 27.9 %all-to-all-start.3 = ((bf16[8,4,16,256]{3,2,1,0:T(8,128)(2,1)}), bf16[8,4,16,256]{3,2,1,0:T(8,128)(2,1)S(1)}, u32[]{:S(2)}, u32[]{:S(2)}) async-start(bf16[8,4,16,256]{3,2,1,0:T(8,128)(2,1)} %reduce.1.refs_1_), calls=%async_computation.3 | async-start | bytes 524288 | tf_op jit(solution)/shard_map/all_to_all | solution.py:61
  194.2 6.8 %collective-permute-start.25 = (bf16[144,1024]{1,0:T(8,128)(2,1)S(1)}, bf16[144,1024]{1,0:T(8,128)(2,1)S(1)}, u32[]{:S(2)}, u32[]{:S(2)}) collective-permute-start(bf16[144,1024]{1,0:T(8,128)(2,1)S(1)} %scatter.1.refs_0_), channel_id=1, source_target_pairs={{0,2},{1,3},{2,0},{3,1},{4,6},{5,7},{6,4},{7,5},{8,10},{9,11},{10,... | collective-permute-start | bytes 884744 | tf_op jit(solution)/shard_map/ppermute | solution.py:57
  195.7 7.4 %collective-permute-start.24 = (bf16[144,1024]{1,0:T(8,128)(2,1)S(1)}, bf16[144,1024]{1,0:T(8,128)(2,1)S(1)}, u32[]{:S(2)}, u32[]{:S(2)}) collective-permute-start(bf16[144,1024]{1,0:T(8,128)(2,1)S(1)} %scatter.1.refs_0_), channel_id=1, source_target_pairs={{0,1},{1,0},{2,3},{3,2},{4,5},{5,4},{6,7},{7,6},{8,9},{9,8},{10,11... | collective-permute-start | bytes 884744 | tf_op jit(solution)/shard_map/ppermute | solution.py:57
  201.0 2.1 %collective-permute-start.26 = (bf16[144,1024]{1,0:T(8,128)(2,1)S(1)}, bf16[144,1024]{1,0:T(8,128)(2,1)S(1)}, u32[]{:S(2)}, u32[]{:S(2)}) collective-permute-start(bf16[144,1024]{1,0:T(8,128)(2,1)S(1)} %collective-permute-done.25.refs_2_), channel_id=1, source_target_pairs={{0,1},{1,0},{2,3},{3,2},{4,5},{5,4},{6,7},{7,6},{8,9},{9,8},{10,11... | collective-permute-start | bytes 884744 | tf_op jit(solution)/shard_map/ppermute | solution.py:57
  (6 other events, 5.3 us)
where the time goes:
time: 209 us; the launch traced here: 205 us
  waiting for transfers between devices  107 us (51%)
  starting transfers between devices  49.9 us (24%)
  Pallas kernels  35 us (17%)
  local copies, waits for them, and re-layouts  10.6 us (5%)
    ppermute x27, waiting for transfers between devices, swap(): return lax.ppermute(x, axis, [(i, i ^ bit) for i in range(n)])  96.4 us
    pallas_call x13, Pallas kernels, call(): pl.pallas_call(body, out_shape=out_shape, in_specs=specs, out_specs=out_s...  35 us
    ppermute x27, starting transfers between devices, swap(): return lax.ppermute(x, axis, [(i, i ^ bit) for i in range(n)])  33.2 us
    all_to_all x4, starting transfers between devices, seq_swap(): return lax.all_to_all(x, 'seq', split_axis=0, concat_axis=0, tiled=True)  16.7 us
    all_to_all x4, waiting for transfers between devices, seq_swap(): return lax.all_to_all(x, 'seq', split_axis=0, concat_axis=0, tiled=True)  11.1 us
    unnamed x50, local copies, waits for them, and re-layouts  9.26 us
  transfers between devices with their start and end apart: 31, of which 12 were waited for; matrix products, arithmetic and copies ran while one was open for 2% of the time, Pallas kernels for 5%

commit v1 on v0

--- a/solution.py
+++ b/solution.py
@@ -88,18 +88,17 @@
                 out[:, at : at + 2 * BLOCK_LEN] = both
 
 
-def scatter_kernel(per_peer, pieces, ids, rows, *refs):
+def scatter_kernel(per_peer, ids, rows, *refs):
     got, out, acc = refs[:-2], refs[-2], refs[-1]
     me = ids[0]
     depth = out.shape[0]
     acc[...] = jnp.zeros_like(acc)
     blank = jnp.zeros((depth, BLOCK_LEN), F32)
-    for k, (ref, place) in enumerate(pieces):
+    for k, piece in enumerate(got):
         for j in range(per_peer):
             b = rows[k, me * per_peer + j]
             at = pl.ds(pl.multiple_of((b >> 1) * LANES, LANES), LANES)
-            start = (place * per_peer + j) * BLOCK_LEN
-            g = got[ref][:, start : start + BLOCK_LEN].astype(F32)
+            g = piece[:, j * BLOCK_LEN : (j + 1) * BLOCK_LEN].astype(F32)
             low = jnp.concatenate([g, blank], axis=1)
             high = jnp.concatenate([blank, g], axis=1)
             acc[:, at] = acc[:, at] + jnp.where((b & 1) == 1, high, low)
@@ -181,8 +180,6 @@
     width = latent + rope_dim
     slots = qx.shape[1] - width
     depth, half = keys[0][0].shape
-    held = 4
-    lanes = half // held
     kts, pbs = (kt_near, kt_far), (pb_near, pb_far)
 
     picks = sel[...] ^ (ids[0] * per_peer)
@@ -198,13 +195,11 @@
     for c in range(2):
         for k in range(4):
             at = pl.ds(pl.multiple_of((ids[1] ^ k) * depth, 16), depth)
-            for i in range(held):
-                peer = c * held + i
-                src = keys[peer % 2][k][:, (peer // 2) * lanes : (peer // 2 + 1) * lanes]
-                kts[c][at, i * lanes : (i + 1) * lanes] = src
+            kts[c][at, :] = keys[c][k][...]
         place = lax.broadcasted_iota(jnp.int32, (slots, half), 0)
-        token = lax.broadcasted_iota(jnp.int32, (slots, half), 1) + c * half
-        kts[c][width:, :] = jnp.where(token // BLOCK_LEN == place, 1.0, 0.0).astype(BF16)
+        block = lax.broadcasted_iota(jnp.int32, (slots, half), 1) // BLOCK_LEN
+        block = block + (block // per_peer + c) * per_peer
+        kts[c][width:, :] = jnp.where(block == place, 1.0, 0.0).astype(BF16)
 
     scale2 = scale * math.log2(math.e)
     step = 512
@@ -259,12 +254,11 @@
         a[...] = total[1, :, i * lanes : (i + 1) * lanes].astype(BF16)
 
 
-def owner_kernel(order, a0, got, *outs):
+def owner_kernel(a0, got, *outs):
     total = (a0[...].astype(F32) + got[...].astype(F32)).astype(BF16)
-    for places, out in zip(order, outs):
-        lanes = out.shape[1] // len(places)
-        for i, p in enumerate(places):
-            out[:, i * lanes : (i + 1) * lanes] = total[:, p * lanes : (p + 1) * lanes]
+    lanes = outs[0].shape[1]
+    for i, out in enumerate(outs):
+        out[...] = total[:, i * lanes : (i + 1) * lanes]
 
 
 def local(q_nope, q_rope, cache, w_uk, w_uv, d_out, sel, slot_blocks):
@@ -291,11 +285,12 @@
 
     row1 = swap(slot_blocks, "seq", 1)
     (c0,) = call(cut_kernel, "cut", (ids, cache.T), [SMEM, VMEM], [((depth, tokens), BF16)])
+    asked_y = jnp.concatenate([slot_blocks, row1], axis=0)
+    asked = jnp.concatenate([asked_y] + [swap(asked_y, "seq", bit) for bit in (2, 4, 6)], axis=0)
     c2 = swap(c0, "seq", 4)
     c1 = swap(c0, "seq", 2)
-    asked_y = jnp.concatenate([slot_blocks, row1], axis=0)
-    asked = jnp.concatenate([asked_y] + [swap(asked_y, "seq", bit) for bit in (2, 4, 6)], axis=0)
-
+
+    (c2,) = call(tie_kernel, "after", (asked,), [ANY], [], tied=c2)
     c3 = swap(c2, "seq", 2)
     away, k0 = call(
         functools.partial(gather_kernel, per_peer),
@@ -319,7 +314,7 @@
         ],
         axis=1,
     )
-    (pack,) = call(tie_kernel, "after", (c1, c3, asked), [ANY] * 3, [], tied=pack)
+    (pack,) = call(tie_kernel, "after", (c1, c3), [ANY] * 2, [], tied=pack)
     pack = seq_swap(pack).reshape(peers, share, -1, LANES)
     sizes = (n_rows * tiles, l_rows, queries, tiles, latent)
     (lat,) = call(
@@ -352,7 +347,7 @@
             pltpu.VMEM((rows, latent), F32),
             pltpu.VMEM((rows, width), F32),
         ],
-        50,
+        60,
     )
 
     def pair(keep, send, tied=None):
@@ -360,14 +355,13 @@
         return call(pair_kernel, "pair", (keep, swap(send, "grp", 1)), [VMEM] * 2, outs, tied=tied)
 
 
-    def owner(a0, a2, order, tied=None):
-        outs = [((depth, lanes * len(places)), BF16) for places in order]
-        kernel = functools.partial(owner_kernel, order)
-        return call(kernel, "owner", (a0, swap(a2, "grp", 2)), [VMEM] * 2, outs, tied=tied)
+    def owner(a0, a2):
+        outs = [((depth, lanes), BF16)] * held
+        return call(owner_kernel, "owner", (a0, swap(a2, "grp", 2)), [VMEM] * 2, outs)
 
     far = pair(far_keep, far_send)
     first, *near = pair(near_keep, near_send, tied=far[0])
-    held_a2, *far = owner(first, far[1], [(0,), (1,), (2,), (3,)], tied=near[1])
+    far = owner(first, far[1])
     lat = seq_swap(lat.reshape(peers, share, queries, 2 * latent))
     (res,) = call(
         functools.partial(reduce_kernel, sizes),
@@ -376,20 +370,14 @@
         [VMEM] * 2,
         [((peers, share, queries, value + nope), BF16)],
     )
-    own, over_y, over_z = owner(near[0], held_a2, [(0,), (1, 3), (2,)])
-    from_y = swap(over_y, "seq", 1)
-    over_z = jnp.concatenate([over_z, from_y[:, lanes:]], axis=1)
-    (over_z,) = call(tie_kernel, "after", (res,), [ANY], [], tied=over_z)
-    from_z = swap(over_z, "seq", 2)
-    got = [own, from_y, from_z] + [swap(p, "seq", 4 + i) for i, p in enumerate(far)]
+    near = owner(*near)
+    got = [near[0]]
+    for k in range(1, peers):
+        got.append(swap((far if k % 2 else near)[k // 2], "seq", k))
     res = seq_swap(res).reshape(heads, queries, value + nope)
 
     (y0,) = call(
-        functools.partial(
-            scatter_kernel,
-            per_peer,
-            [(0, 0), (1, 0), (2, 0), (2, 1), (3, 0), (4, 0), (5, 0), (6, 0)],
-        ),
+        functools.partial(scatter_kernel, per_peer),
         "scatter",
         (ids, asked, *got),
         [SMEM, SMEM] + [VMEM] * len(got),

time: 209 us -> 193 us (0.923)
  waiting for transfers between devices: 107 us -> 92.1 us
  local copies, waits for them, and re-layouts: 10.6 us -> 6.82 us
  starting transfers between devices: 49.9 us -> 53.5 us
    ppermute x27 -> x28, waiting for transfers between devices: 96.4 us -> 81.2 us  [swap(): return lax.ppermute(x, axis, [(i, i ^ bit) for i in range(n)])]
    unnamed x50 -> x42, local copies, waits for them, and re-layouts: 9.26 us -> 5.5 us
    all_to_all x4, starting transfers between devices: 16.7 us -> 19.3 us  [seq_swap(): return lax.all_to_all(x, 'seq', split_axis=0, concat_axis=0, tiled=True)]
    ppermute x27 -> x28, starting transfers between devices: 33.2 us -> 34.2 us  [swap(): return lax.ppermute(x, axis, [(i, i ^ bit) for i in range(n)])]
  transfers between devices with their start and end apart: 31 -> 32, of which waited for: 12 -> 12; matrix products, arithmetic and copies ran while one was open for 2% -> 2% of each run, Pallas kernels for 5% -> 5%
where the time goes in v1:
time: 193 us; the launch traced here: 190 us
  waiting for transfers between devices  92.1 us (48%)
  starting transfers between devices  53.5 us (28%)
  Pallas kernels  35.9 us (19%)
  local copies, waits for them, and re-layouts  6.82 us (4%)
    ppermute x28, waiting for transfers between devices, swap(): return lax.ppermute(x, axis, [(i, i ^ bit) for i in range(n)])  81.2 us
    pallas_call x13, Pallas kernels, call(): pl.pallas_call(body, out_shape=out_shape, in_specs=specs, out_specs=out_s...  35.9 us
    ppermute x28, starting transfers between devices, swap(): return lax.ppermute(x, axis, [(i, i ^ bit) for i in range(n)])  34.2 us
    all_to_all x4, starting transfers between devices, seq_swap(): return lax.all_to_all(x, 'seq', split_axis=0, concat_axis=0, tiled=True)  19.3 us
    all_to_all x4, waiting for transfers between devices, seq_swap(): return lax.all_to_all(x, 'seq', split_axis=0, concat_axis=0, tiled=True)  10.9 us
    unnamed x42, local copies, waits for them, and re-layouts  5.5 us
  transfers between devices with their start and end apart: 32, of which 12 were waited for; matrix products, arithmetic and copies ran while one was open for 2% of the time, Pallas kernels for 5%

profile of v1, /device:TPU:0, one launch (start us, length us, event | category | flops | bytes accessed | tf_op | source)
XLA Modules:
  0.0 190.4 jit_solution(7322994929678350046)
XLA Ops:
  0.7 1.3 copy-done.3
  2.6 4.1 %collective-permute-start.1 = (bf16[144,1024]{1,0:T(8,128)(2,1)S(1)}, bf16[144,1024]{1,0:T(8,128)(2,1)S(1)}, u32[]{:S(2)}, u32[]{:S(2)}) collective-permute-start(bf16[144,1024]{1,0:T(8,128)(2,1)S(1)} %cut.1.refs_0_), channel_id=1, source_target_pairs={{0,16},{4,20},{8,24},{12,28},{16,0},{20,4},{24,8},{28,12},{1,17},{... | collective-permute-start | bytes 884744 | tf_op jit(solution)/shard_map/ppermute | solution.py:57
  6.7 1.5 collective-permute-start.2
  8.2 2.0 %collective-permute-done.2.other = s32[1,64]{1,0:T(1,128)S(1)} collective-permute-done((s32[1,64]{1,0:T(1,128)S(1)}, s32[1,64]{1,0:T(1,128)S(1)}, u32[]{:S(2)}, u32[]{:S(2)}) %collective-permute-start.2) | collective-permute-done | bytes 288 | tf_op jit(solution)/shard_map/ppermute | solution.py:57
  10.2 1.4 collective-permute-start.5
  11.6 1.7 collective-permute-start.4
  13.3 1.3 collective-permute-start.3
  16.0 4.2 %collective-permute-done.4 = s32[2,64]{1,0:T(2,128)S(1)} collective-permute-done((s32[2,64]{1,0:T(2,128)S(1)}, s32[2,64]{1,0:T(2,128)S(1)}, u32[]{:S(2)}, u32[]{:S(2)}) %collective-permute-start.4) | collective-permute-done | bytes 544 | tf_op jit(solution)/shard_map/ppermute | solution.py:57
  20.3 0.7 collective-permute-start.6
  21.1 1.1 pad_maximum_fusion.refs_0_
  22.3 4.2 %collective-permute-done.refs_1_ = bf16[144,1024]{1,0:T(8,128)(2,1)S(1)} collective-permute-done((bf16[144,1024]{1,0:T(8,128)(2,1)S(1)}, bf16[144,1024]{1,0:T(8,128)(2,1)S(1)}, u32[]{:S(2)}, u32[]{:S(2)}) %collective-permute-start) | collective-permute-done | bytes 294944 | tf_op jit(solution)/shard_map/ppermute | solution.py:57
  26.5 6.2 %collective-permute-done.6.refs_2_.refs_3_ = bf16[144,1024]{1,0:T(8,128)(2,1)S(1)} collective-permute-done((bf16[144,1024]{1,0:T(8,128)(2,1)S(1)}, bf16[144,1024]{1,0:T(8,128)(2,1)S(1)}, u32[]{:S(2)}, u32[]{:S(2)}) %collective-permute-start.6) | collective-permute-done | bytes 294944 | tf_op jit(solution)/shard_map/ppermute | solution.py:57
  32.7 4.6 %all-to-all-start = ((bf16[32,160,128]{2,1,0:T(8,128)(2,1)}), bf16[32,160,128]{2,1,0:T(8,128)(2,1)S(1)}, u32[]{:S(2)}, u32[]{:S(2)}) async-start(bf16[32,160,128]{2,1,0:T(8,128)(2,1)} %after.3), calls=%async_computation | async-start | bytes 2621440 | tf_op jit(solution)/shard_map/all_to_all | solution.py:61
  37.4 3.3 %gather.1 = (bf16[144,2048]{1,0:T(8,128)(2,1)S(1)}, bf16[144,2048]{1,0:T(8,128)(2,1)S(1)}) custom-call(s32[2]{0:T(128)S(1)} %pad_add_fusion.1.ids, s32[1,64]{1,0:T(1,128)S(1)} %copy-done.8, s32[1,64]{1,0:T(1,128)S(1)} %collective-permute-done.2.other, bf16[144,1024]{1,0:T(8,128)(2,1)S(1)} %cut.1.refs_0_, bf16[144,1024]{1,0:T(8,128)(2,1)S(1)} %collective-permute-done.refs_1_, ...), custom_call_target="tpu_custom_call" | custom-call | tf_op jit(solution)/shard_map/gather/pallas_call | solution.py:35
  40.7 2.1 %collective-permute-start.7 = (bf16[144,2048]{1,0:T(8,128)(2,1)S(1)}, bf16[144,2048]{1,0:T(8,128)(2,1)S(1)}, u32[]{:S(2)}, u32[]{:S(2)}) collective-permute-start(bf16[144,2048]{1,0:T(8,128)(2,1)S(1)} %get-tuple-element.25), channel_id=1, source_target_pairs={{0,4},{4,0},{8,12},{12,8},{16,20},{20,16},{24,28},{28,24},{1,5},{5... | collective-permute-start | bytes 1769480 | tf_op jit(solution)/shard_map/ppermute | solution.py:57
  42.8 1.5 collective-permute-start.8
  44.3 21.6 %collective-permute-done.7.away.refs_4_ = bf16[144,2048]{1,0:T(8,128)(2,1)S(1)} collective-permute-done((bf16[144,2048]{1,0:T(8,128)(2,1)S(1)}, bf16[144,2048]{1,0:T(8,128)(2,1)S(1)}, u32[]{:S(2)}, u32[]{:S(2)}) %collective-permute-start.7) | collective-permute-done | bytes 589856 | tf_op jit(solution)/shard_map/ppermute | solution.py:57
  65.9 2.3 %all-to-all-done = bf16[32,160,128]{2,1,0:T(8,128)(2,1)S(1)} async-done(((bf16[32,160,128]{2,1,0:T(8,128)(2,1)}), bf16[32,160,128]{2,1,0:T(8,128)(2,1)S(1)}, u32[]{:S(2)}, u32[]{:S(2)}) %all-to-all-start) | async-done | bytes 1310752 | tf_op jit(solution)/shard_map/all_to_all | solution.py:61
  68.2 1.4 expand.1
  69.6 4.6 %all-to-all-start.1 = ((bf16[8,4,16,1024]{3,2,1,0:T(8,128)(2,1)}), bf16[8,4,16,1024]{3,2,1,0:T(8,128)(2,1)}, u32[]{:S(2)}, u32[]{:S(2)}) async-start(bf16[8,4,16,1024]{3,2,1,0:T(8,128)(2,1)} %expand.1), calls=%async_computation.1 | async-start | bytes 2097152 | tf_op jit(solution)/shard_map/all_to_all | solution.py:61
  74.2 1.5 collective-permute-start.12
  76.3 11.8 %collective-permute-done.12.refs_6_ = bf16[144,2048]{1,0:T(8,128)(2,1)S(1)} collective-permute-done((bf16[144,2048]{1,0:T(8,128)(2,1)S(1)}, bf16[144,2048]{1,0:T(8,128)(2,1)S(1)}, u32[]{:S(2)}, u32[]{:S(2)}) %collective-permute-start.12) | collective-permute-done | bytes 589856 | tf_op jit(solution)/shard_map/ppermute | solution.py:57
  88.2 0.8 copy.34
  89.0 0.7 copy-done.10
  90.0 0.9 copy-done.12
  90.9 8.6 %all-to-all-done.1 = bf16[8,4,16,1024]{3,2,1,0:T(8,128)(2,1)} async-done(((bf16[8,4,16,1024]{3,2,1,0:T(8,128)(2,1)}), bf16[8,4,16,1024]{3,2,1,0:T(8,128)(2,1)}, u32[]{:S(2)}, u32[]{:S(2)}) %all-to-all-start.1) | async-done | bytes 1048608 | tf_op jit(solution)/shard_map/all_to_all | solution.py:61
  99.5 22.0 %attend.1 = (bf16[2,144,2048]{2,1,0:T(8,128)(2,1)}, bf16[2,144,2048]{2,1,0:T(8,128)(2,1)}, bf16[2,144,2048]{2,1,0:T(8,128)(2,1)}, bf16[2,144,2048]{2,1,0:T(8,128...) custom-call(s32[2]{0:T(128)} %copy-done.6, s32[16,32]{1,0:T(8,128)} %sel.1, bf16[32,16,64]{2,1,0:T(8,128)(2,1)} %bitcast.38, ...), custom_call_target="tpu_custom_call" | custom-call | tf_op jit(solution)/shard_map/attend/pallas_call | solution.py:35
  121.6 3.7 %all-to-all-start.2 = ((bf16[8,4,16,1024]{3,2,1,0:T(8,128)(2,1)}), bf16[8,4,16,1024]{3,2,1,0:T(8,128)(2,1)S(1)}, u32[]{:S(2)}, u32[]{:S(2)}) async-start(bf16[8,4,16,1024]{3,2,1,0:T(8,128)(2,1)} %bitcast.36), calls=%async_computation.2 | async-start | bytes 2097152 | tf_op jit(solution)/shard_map/all_to_all | solution.py:61
  125.7 1.5 pair.2
  127.3 1.5 collective-permute-start.17
  129.1 1.2 collective-permute-start.16
  130.2 13.3 %collective-permute-done.17.got = bf16[144,2048]{1,0:T(8,128)(2,1)S(1)} collective-permute-done((bf16[144,2048]{1,0:T(8,128)(2,1)S(1)}, bf16[144,2048]{1,0:T(8,128)(2,1)S(1)}, u32[]{:S(2)}, u32[]{:S(2)}) %collective-permute-start.17) | collective-permute-done | bytes 589856 | tf_op jit(solution)/shard_map/ppermute | solution.py:57
  143.5 0.8 owner.3
  144.3 1.6 collective-permute-start.18
  145.9 1.5 collective-permute-start.20
  147.4 3.3 %collective-permute-start.22 = (bf16[144,512]{1,0:T(8,128)(2,1)}, bf16[144,512]{1,0:T(8,128)(2,1)S(1)}, u32[]{:S(2)}, u32[]{:S(2)}) collective-permute-start(bf16[144,512]{1,0:T(8,128)(2,1)} %get-tuple-element.43), channel_id=1, source_target_pairs={{0,20},{4,16},{8,28},{12,24},{16,4},{20,0},{24,12},{28,8},{1,21},{... | collective-permute-start | bytes 442376 | tf_op jit(solution)/shard_map/ppermute | solution.py:57
  151.0 4.5 %collective-permute-done.16.got = bf16[144,2048]{1,0:T(8,128)(2,1)S(1)} collective-permute-done((bf16[144,2048]{1,0:T(8,128)(2,1)S(1)}, bf16[144,2048]{1,0:T(8,128)(2,1)S(1)}, u32[]{:S(2)}, u32[]{:S(2)}) %collective-permute-start.16) | collective-permute-done | bytes 589856 | tf_op jit(solution)/shard_map/ppermute | solution.py:57
  155.5 0.8 owner.2
  156.3 1.7 collective-permute-start.19
  158.0 2.4 %collective-permute-start.21 = (bf16[144,512]{1,0:T(8,128)(2,1)}, bf16[144,512]{1,0:T(8,128)(2,1)S(1)}, u32[]{:S(2)}, u32[]{:S(2)}) collective-permute-start(bf16[144,512]{1,0:T(8,128)(2,1)} %get-tuple-element.42), channel_id=1, source_target_pairs={{0,16},{4,20},{8,24},{12,28},{16,0},{20,4},{24,8},{28,12},{1,17},{... | collective-permute-start | bytes 442376 | tf_op jit(solution)/shard_map/ppermute | solution.py:57
  160.4 1.5 collective-permute-start.23
  161.9 1.1 reduce.1
  163.0 6.3 %all-to-all-start.3 = ((bf16[8,4,16,256]{3,2,1,0:T(8,128)(2,1)}), bf16[8,4,16,256]{3,2,1,0:T(8,128)(2,1)S(1)}, u32[]{:S(2)}, u32[]{:S(2)}) async-start(bf16[8,4,16,256]{3,2,1,0:T(8,128)(2,1)} %reduce.1), calls=%async_computation.3 | async-start | bytes 524288 | tf_op jit(solution)/shard_map/all_to_all | solution.py:61
  169.4 8.1 %collective-permute-done.21.refs_4_ = bf16[144,512]{1,0:T(8,128)(2,1)S(1)} collective-permute-done((bf16[144,512]{1,0:T(8,128)(2,1)}, bf16[144,512]{1,0:T(8,128)(2,1)S(1)}, u32[]{:S(2)}, u32[]{:S(2)}) %collective-permute-start.21) | collective-permute-done | bytes 147488 | tf_op jit(solution)/shard_map/ppermute | solution.py:57
  177.5 2.0 %scatter.1.refs_0_ = bf16[144,1024]{1,0:T(8,128)(2,1)S(1)} custom-call(s32[2]{0:T(128)S(1)} %copy-done.7, s32[8,64]{1,0:T(8,128)S(1)} %concatenate.12.refs_1_.rows, bf16[144,512]{1,0:T(8,128)(2,1)S(1)} %get-tuple-element.36.refs_0_, bf16[144,512]{1,0:T(8,128)(2,1)S(1)} %collective-permute-done.18.refs_1_, ...), custom_call_target="tpu_custom_call" | custom-call | tf_op jit(solution)/shard_map/scatter/pallas_call | solution.py:35
  179.4 1.5 collective-permute-start.26
  180.9 5.3 %collective-permute-done.26.refs_2_ = bf16[144,1024]{1,0:T(8,128)(2,1)S(1)} collective-permute-done((bf16[144,1024]{1,0:T(8,128)(2,1)S(1)}, bf16[144,1024]{1,0:T(8,128)(2,1)S(1)}, u32[]{:S(2)}, u32[]{:S(2)}) %collective-permute-start.26) | collective-permute-done | bytes 294944 | tf_op jit(solution)/shard_map/ppermute | solution.py:57
  188.3 2.1 %assemble.1 = f32[576,1024]{1,0:T(8,128)} custom-call(s32[2]{0:T(128)S(1)} %copy-done.7, bf16[144,1024]{1,0:T(8,128)(2,1)S(1)} %scatter.1.refs_0_, bf16[144,1024]{1,0:T(8,128)(2,1)S(1)} %collective-permute-done.25.refs_1_, bf16[144,1024]{1,0:T(8,128)(2,1)S(1)} %collective-permute-done.26.refs_2_, bf16[144,1024]{1,0:T(8,128)(2,1)S(1)} %collective-permute-done.27.refs_3_), custom_call_target="tpu_custom_call" | custom-call | tf_op jit(solution)/shard_map/assemble/pallas_call | solution.py:35
  (80 shorter events, 6.2 us)
Async XLA Ops:
  0.6 6.1 %copy-start.8 = (s32[1,64]{1,0:T(1,128)S(1)}, s32[1,64]{1,0:T(1,128)}, u32[]{:S(2)}) copy-start(s32[1,64]{1,0:T(1,128)} %own.1) | copy-start | bytes 772
  0.7 36.6 %copy-start.6 = (s32[2]{0:T(128)}, s32[2]{0:T(128)S(1)}, u32[]{:S(2)}) copy-start(s32[2]{0:T(128)S(1)} %pad_add_fusion.1.ids) | copy-start | bytes 28
  0.7 1.3 copy-start.3
  2.0 13.4 %copy-start.13 = (bf16[32,8192]{1,0:T(8,128)(2,1)S(1)}, bf16[32,8192]{1,0:T(8,128)(2,1)}, u32[]{:S(2)}) copy-start(bf16[32,8192]{1,0:T(8,128)(2,1)} %param.11) | copy-start | bytes 1572868
  2.6 13.3 %copy-start.14 = (bf16[32,8192]{1,0:T(8,128)(2,1)S(1)}, bf16[32,8192]{1,0:T(8,128)(2,1)}, u32[]{:S(2)}) copy-start(bf16[32,8192]{1,0:T(8,128)(2,1)} %param.12) | copy-start | bytes 1572868
  2.6 17.7 %collective-permute-start.1 = (bf16[144,1024]{1,0:T(8,128)(2,1)S(1)}, bf16[144,1024]{1,0:T(8,128)(2,1)S(1)}, u32[]{:S(2)}, u32[]{:S(2)}) collective-permute-start(bf16[144,1024]{1,0:T(8,128)(2,1)S(1)} %cut.1.refs_0_), channel_id=1, source_target_pairs={{0,16},{4,20},{8,24},{12,28},{16,0},{20,4},{24,8},{28,12},{1,17},{... | collective-permute-start | bytes 884744 | tf_op jit(solution)/shard_map/ppermute | solution.py:57
  6.7 3.5 %collective-permute-start.2 = (s32[1,64]{1,0:T(1,128)S(1)}, s32[1,64]{1,0:T(1,128)S(1)}, u32[]{:S(2)}, u32[]{:S(2)}) collective-permute-start(s32[1,64]{1,0:T(1,128)S(1)} %copy-done.8), channel_id=1, source_target_pairs={{0,4},{4,0},{8,12},{12,8},{16,20},{20,16},{24,28},{28,24},{1,5},{5... | collective-permute-start | bytes 776 | tf_op jit(solution)/shard_map/ppermute | solution.py:57
  10.2 5.8 %collective-permute-start.5 = (s32[2,64]{1,0:T(2,128)S(1)}, s32[2,64]{1,0:T(2,128)S(1)}, u32[]{:S(2)}, u32[]{:S(2)}) collective-permute-start(s32[2,64]{1,0:T(2,128)S(1)} %pad_add_fusion), channel_id=1, source_target_pairs={{0,24},{4,28},{8,16},{12,20},{16,8},{20,12},{24,0},{28,4},{1,25},{... | collective-permute-start | bytes 1544 | tf_op jit(solution)/shard_map/ppermute | solution.py:57
  11.6 8.6 %collective-permute-start.4 = (s32[2,64]{1,0:T(2,128)S(1)}, s32[2,64]{1,0:T(2,128)S(1)}, u32[]{:S(2)}, u32[]{:S(2)}) collective-permute-start(s32[2,64]{1,0:T(2,128)S(1)} %pad_add_fusion), channel_id=1, source_target_pairs={{0,16},{4,20},{8,24},{12,28},{16,0},{20,4},{24,8},{28,12},{1,17},{... | collective-permute-start | bytes 1544 | tf_op jit(solution)/shard_map/ppermute | solution.py:57
  13.3 6.9 %collective-permute-start.3 = (s32[2,64]{1,0:T(2,128)S(1)}, s32[2,64]{1,0:T(2,128)S(1)}, u32[]{:S(2)}, u32[]{:S(2)}) collective-permute-start(s32[2,64]{1,0:T(2,128)S(1)} %pad_add_fusion), channel_id=1, source_target_pairs={{0,8},{4,12},{8,0},{12,4},{16,24},{20,28},{24,16},{28,20},{1,9},{5... | collective-permute-start | bytes 1544 | tf_op jit(solution)/shard_map/ppermute | solution.py:57
  14.7 11.8 %collective-permute-start = (bf16[144,1024]{1,0:T(8,128)(2,1)S(1)}, bf16[144,1024]{1,0:T(8,128)(2,1)S(1)}, u32[]{:S(2)}, u32[]{:S(2)}) collective-permute-start(bf16[144,1024]{1,0:T(8,128)(2,1)S(1)} %cut.1.refs_0_), channel_id=1, source_target_pairs={{0,8},{4,12},{8,0},{12,4},{16,24},{20,28},{24,16},{28,20},{1,9},{5... | collective-permute-start | bytes 884744 | tf_op jit(solution)/shard_map/ppermute | solution.py:57
  15.7 5.3 %copy-start.17 = (bf16[16,32,128]{2,1,0:T(8,128)(2,1)S(1)}, bf16[16,32,128]{2,1,0:T(8,128)(2,1)}, u32[]{:S(2)}) copy-start(bf16[16,32,128]{2,1,0:T(8,128)(2,1)} %param.13) | copy-start | bytes 393220
  15.7 5.3 %copy-start.18 = (bf16[16,32,128]{2,1,0:T(8,128)(2,1)S(1)}, bf16[16,32,128]{2,1,0:T(8,128)(2,1)}, u32[]{:S(2)}) copy-start(bf16[16,32,128]{2,1,0:T(8,128)(2,1)} %param.8) | copy-start | bytes 393220
  20.3 12.5 %collective-permute-start.6 = (bf16[144,1024]{1,0:T(8,128)(2,1)S(1)}, bf16[144,1024]{1,0:T(8,128)(2,1)S(1)}, u32[]{:S(2)}, u32[]{:S(2)}) collective-permute-start(bf16[144,1024]{1,0:T(8,128)(2,1)S(1)} %after.2.refs_2_), channel_id=1, source_target_pairs={{0,8},{4,12},{8,0},{12,4},{16,24},{20,28},{24,16},{28,20},{1,9},{5... | collective-permute-start | bytes 884744 | tf_op jit(solution)/shard_map/ppermute | solution.py:57
  32.7 35.5 %all-to-all-start = ((bf16[32,160,128]{2,1,0:T(8,128)(2,1)}), bf16[32,160,128]{2,1,0:T(8,128)(2,1)S(1)}, u32[]{:S(2)}, u32[]{:S(2)}) async-start(bf16[32,160,128]{2,1,0:T(8,128)(2,1)} %after.3), calls=%async_computation | async-start | bytes 2621440 | tf_op jit(solution)/shard_map/all_to_all | solution.py:61
  40.7 35.0 %copy-start.5 = (bf16[144,2048]{1,0:T(8,128)(2,1)}, bf16[144,2048]{1,0:T(8,128)(2,1)S(1)}, u32[]{:S(2)}) copy-start(bf16[144,2048]{1,0:T(8,128)(2,1)S(1)} %get-tuple-element.26.refs_0_) | copy-start | bytes 1769476
  40.7 25.1 %collective-permute-start.7 = (bf16[144,2048]{1,0:T(8,128)(2,1)S(1)}, bf16[144,2048]{1,0:T(8,128)(2,1)S(1)}, u32[]{:S(2)}, u32[]{:S(2)}) collective-permute-start(bf16[144,2048]{1,0:T(8,128)(2,1)S(1)} %get-tuple-element.25), channel_id=1, source_target_pairs={{0,4},{4,0},{8,12},{12,8},{16,20},{20,16},{24,28},{28,24},{1,5},{5... | collective-permute-start | bytes 1769480 | tf_op jit(solution)/shard_map/ppermute | solution.py:57
  42.8 23.1 %collective-permute-start.8 = (bf16[144,2048]{1,0:T(8,128)(2,1)S(1)}, bf16[144,2048]{1,0:T(8,128)(2,1)S(1)}, u32[]{:S(2)}, u32[]{:S(2)}) collective-permute-start(bf16[144,2048]{1,0:T(8,128)(2,1)S(1)} %get-tuple-element.26.refs_0_), channel_id=1, source_target_pairs={{0,2},{1,3},{2,0},{3,1},{4,6},{5,7},{6,4},{7,5},{8,10},{9,11},{10,... | collective-permute-start | bytes 1769480 | tf_op jit(solution)/shard_map/ppermute | solution.py:57
  65.9 9.9 %copy-start = (bf16[144,2048]{1,0:T(8,128)(2,1)}, bf16[144,2048]{1,0:T(8,128)(2,1)S(1)}, u32[]{:S(2)}) copy-start(bf16[144,2048]{1,0:T(8,128)(2,1)S(1)} %collective-permute-done.7.away.refs_4_) | copy-start | bytes 1769476
  65.9 10.4 %copy-start.1 = (bf16[144,2048]{1,0:T(8,128)(2,1)}, bf16[144,2048]{1,0:T(8,128)(2,1)S(1)}, u32[]{:S(2)}) copy-start(bf16[144,2048]{1,0:T(8,128)(2,1)S(1)} %collective-permute-done.8.over_x.refs_2_) | copy-start | bytes 1769476
  69.6 18.6 %copy-start.15 = (bf16[16,32,64]{2,1,0:T(8,128)(2,1)S(1)}, bf16[16,32,64]{2,1,0:T(8,128)(2,1)}, u32[]{:S(2)}) copy-start(bf16[16,32,64]{2,1,0:T(8,128)(2,1)} %param.9) | copy-start | bytes 196612
  69.6 29.9 %all-to-all-start.1 = ((bf16[8,4,16,1024]{3,2,1,0:T(8,128)(2,1)}), bf16[8,4,16,1024]{3,2,1,0:T(8,128)(2,1)}, u32[]{:S(2)}, u32[]{:S(2)}) async-start(bf16[8,4,16,1024]{3,2,1,0:T(8,128)(2,1)} %expand.1), calls=%async_computation.1 | async-start | bytes 2097152 | tf_op jit(solution)/shard_map/all_to_all | solution.py:61
  74.2 14.0 %collective-permute-start.12 = (bf16[144,2048]{1,0:T(8,128)(2,1)S(1)}, bf16[144,2048]{1,0:T(8,128)(2,1)S(1)}, u32[]{:S(2)}, u32[]{:S(2)}) collective-permute-start(bf16[144,2048]{1,0:T(8,128)(2,1)S(1)} %collective-permute-done.7.away.refs_4_), channel_id=1, source_target_pairs={{0,2},{1,3},{2,0},{3,1},{4,6},{5,7},{6,4},{7,5},{8,10},{9,11},{10,... | collective-permute-start | bytes 1769480 | tf_op jit(solution)/shard_map/ppermute | solution.py:57
  75.7 13.2 %collective-permute-start.9 = (bf16[144,2048]{1,0:T(8,128)(2,1)S(1)}, bf16[144,2048]{1,0:T(8,128)(2,1)S(1)}, u32[]{:S(2)}, u32[]{:S(2)}) collective-permute-start(bf16[144,2048]{1,0:T(8,128)(2,1)S(1)} %get-tuple-element.26.refs_0_), channel_id=1, source_target_pairs={{0,1},{1,0},{2,3},{3,2},{4,5},{5,4},{6,7},{7,6},{8,9},{9,8},{10,11... | collective-permute-start | bytes 1769480 | tf_op jit(solution)/shard_map/ppermute | solution.py:57
  75.7 13.2 %collective-permute-start.11 = (bf16[144,2048]{1,0:T(8,128)(2,1)S(1)}, bf16[144,2048]{1,0:T(8,128)(2,1)S(1)}, u32[]{:S(2)}, u32[]{:S(2)}) collective-permute-start(bf16[144,2048]{1,0:T(8,128)(2,1)S(1)} %collective-permute-done.7.away.refs_4_), channel_id=1, source_target_pairs={{0,1},{1,0},{2,3},{3,2},{4,5},{5,4},{6,7},{7,6},{8,9},{9,8},{10,11... | collective-permute-start | bytes 1769480 | tf_op jit(solution)/shard_map/ppermute | solution.py:57
  76.2 12.7 %collective-permute-start.10 = (bf16[144,2048]{1,0:T(8,128)(2,1)S(1)}, bf16[144,2048]{1,0:T(8,128)(2,1)S(1)}, u32[]{:S(2)}, u32[]{:S(2)}) collective-permute-start(bf16[144,2048]{1,0:T(8,128)(2,1)S(1)} %collective-permute-done.8.over_x.refs_2_), channel_id=1, source_target_pairs={{0,1},{1,0},{2,3},{3,2},{4,5},{5,4},{6,7},{7,6},{8,9},{9,8},{10,11... | collective-permute-start | bytes 1769480 | tf_op jit(solution)/shard_map/ppermute | solution.py:57
  88.2 2.7 %collective-permute-start.13 = (bf16[144,2048]{1,0:T(8,128)(2,1)S(1)}, bf16[144,2048]{1,0:T(8,128)(2,1)}, u32[]{:S(2)}, u32[]{:S(2)}) collective-permute-start(bf16[144,2048]{1,0:T(8,128)(2,1)S(1)} %collective-permute-done.12.refs_6_), channel_id=1, source_target_pairs={{0,1},{1,0},{2,3},{3,2},{4,5},{5,4},{6,7},{7,6},{8,9},{9,8},{10,11... | collective-permute-start | bytes 1769480 | tf_op jit(solution)/shard_map/ppermute | solution.py:57
  89.0 1.0 copy-start.11
  121.5 4.2 %copy-start.2 = (bf16[2,144,2048]{2,1,0:T(8,128)(2,1)S(1)}, bf16[2,144,2048]{2,1,0:T(8,128)(2,1)}, u32[]{:S(2)}) copy-start(bf16[2,144,2048]{2,1,0:T(8,128)(2,1)} %get-tuple-element.29.keep) | copy-start | bytes 3538948
  121.5 4.2 %collective-permute-start.14 = (bf16[2,144,2048]{2,1,0:T(8,128)(2,1)}, bf16[2,144,2048]{2,1,0:T(8,128)(2,1)}, u32[]{:S(2)}, u32[]{:S(2)}) collective-permute-start(bf16[2,144,2048]{2,1,0:T(8,128)(2,1)} %get-tuple-element.30), channel_id=1, source_target_pairs={{0,1},{1,0},{2,3},{3,2},{4,5},{5,4},{6,7},{7,6},{8,9},{9,8},{10,11... | collective-permute-start | bytes 3538952 | tf_op jit(solution)/shard_map/ppermute | solution.py:57
  121.6 40.3 %all-to-all-start.2 = ((bf16[8,4,16,1024]{3,2,1,0:T(8,128)(2,1)}), bf16[8,4,16,1024]{3,2,1,0:T(8,128)(2,1)S(1)}, u32[]{:S(2)}, u32[]{:S(2)}) async-start(bf16[8,4,16,1024]{3,2,1,0:T(8,128)(2,1)} %bitcast.36), calls=%async_computation.2 | async-start | bytes 2097152 | tf_op jit(solution)/shard_map/all_to_all | solution.py:61
  125.3 3.5 %copy-start.4 = (bf16[2,144,2048]{2,1,0:T(8,128)(2,1)S(1)}, bf16[2,144,2048]{2,1,0:T(8,128)(2,1)}, u32[]{:S(2)}) copy-start(bf16[2,144,2048]{2,1,0:T(8,128)(2,1)} %get-tuple-element.32.refs_1_) | copy-start | bytes 3538948
  125.3 3.5 %collective-permute-start.15 = (bf16[2,144,2048]{2,1,0:T(8,128)(2,1)}, bf16[2,144,2048]{2,1,0:T(8,128)(2,1)S(1)}, u32[]{:S(2)}, u32[]{:S(2)}) collective-permute-start(bf16[2,144,2048]{2,1,0:T(8,128)(2,1)} %get-tuple-element.33), channel_id=1, source_target_pairs={{0,1},{1,0},{2,3},{3,2},{4,5},{5,4},{6,7},{7,6},{8,9},{9,8},{10,11... | collective-permute-start | bytes 3538952 | tf_op jit(solution)/shard_map/ppermute | solution.py:57
  127.3 16.2 %collective-permute-start.17 = (bf16[144,2048]{1,0:T(8,128)(2,1)S(1)}, bf16[144,2048]{1,0:T(8,128)(2,1)S(1)}, u32[]{:S(2)}, u32[]{:S(2)}) collective-permute-start(bf16[144,2048]{1,0:T(8,128)(2,1)S(1)} %get-tuple-element.38), channel_id=1, source_target_pairs={{0,2},{1,3},{2,0},{3,1},{4,6},{5,7},{6,4},{7,5},{8,10},{9,11},{10,... | collective-permute-start | bytes 1769480 | tf_op jit(solution)/shard_map/ppermute | solution.py:57
  129.1 26.4 %collective-permute-start.16 = (bf16[144,2048]{1,0:T(8,128)(2,1)S(1)}, bf16[144,2048]{1,0:T(8,128)(2,1)S(1)}, u32[]{:S(2)}, u32[]{:S(2)}) collective-permute-start(bf16[144,2048]{1,0:T(8,128)(2,1)S(1)} %get-tuple-element.35), channel_id=1, source_target_pairs={{0,2},{1,3},{2,0},{3,1},{4,6},{5,7},{6,4},{7,5},{8,10},{9,11},{10,... | collective-permute-start | bytes 1769480 | tf_op jit(solution)/shard_map/ppermute | solution.py:57
  144.3 13.7 %collective-permute-start.18 = (bf16[144,512]{1,0:T(8,128)(2,1)S(1)}, bf16[144,512]{1,0:T(8,128)(2,1)S(1)}, u32[]{:S(2)}, u32[]{:S(2)}) collective-permute-start(bf16[144,512]{1,0:T(8,128)(2,1)S(1)} %get-tuple-element.39), channel_id=1, source_target_pairs={{0,4},{4,0},{8,12},{12,8},{16,20},{20,16},{24,28},{28,24},{1,5},{5... | collective-permute-start | bytes 442376 | tf_op jit(solution)/shard_map/ppermute | solution.py:57
  145.9 14.5 %collective-permute-start.20 = (bf16[144,512]{1,0:T(8,128)(2,1)S(1)}, bf16[144,512]{1,0:T(8,128)(2,1)S(1)}, u32[]{:S(2)}, u32[]{:S(2)}) collective-permute-start(bf16[144,512]{1,0:T(8,128)(2,1)S(1)} %get-tuple-element.41), channel_id=1, source_target_pairs={{0,12},{4,8},{8,4},{12,0},{16,28},{20,24},{24,20},{28,16},{1,13},{... | collective-permute-start | bytes 442376 | tf_op jit(solution)/shard_map/ppermute | solution.py:57
  147.4 22.0 %collective-permute-start.22 = (bf16[144,512]{1,0:T(8,128)(2,1)}, bf16[144,512]{1,0:T(8,128)(2,1)S(1)}, u32[]{:S(2)}, u32[]{:S(2)}) collective-permute-start(bf16[144,512]{1,0:T(8,128)(2,1)} %get-tuple-element.43), channel_id=1, source_target_pairs={{0,20},{4,16},{8,28},{12,24},{16,4},{20,0},{24,12},{28,8},{1,21},{... | collective-permute-start | bytes 442376 | tf_op jit(solution)/shard_map/ppermute | solution.py:57
  150.7 18.7 %collective-permute-start.24 = (bf16[144,512]{1,0:T(8,128)(2,1)}, bf16[144,512]{1,0:T(8,128)(2,1)S(1)}, u32[]{:S(2)}, u32[]{:S(2)}) collective-permute-start(bf16[144,512]{1,0:T(8,128)(2,1)} %get-tuple-element.45), channel_id=1, source_target_pairs={{0,28},{4,24},{8,20},{12,16},{16,12},{20,8},{24,4},{28,0},{1,29},{... | collective-permute-start | bytes 442376 | tf_op jit(solution)/shard_map/ppermute | solution.py:57
  156.3 13.1 %collective-permute-start.19 = (bf16[144,512]{1,0:T(8,128)(2,1)}, bf16[144,512]{1,0:T(8,128)(2,1)S(1)}, u32[]{:S(2)}, u32[]{:S(2)}) collective-permute-start(bf16[144,512]{1,0:T(8,128)(2,1)} %get-tuple-element.40), channel_id=1, source_target_pairs={{0,8},{4,12},{8,0},{12,4},{16,24},{20,28},{24,16},{28,20},{1,9},{5... | collective-permute-start | bytes 442376 | tf_op jit(solution)/shard_map/ppermute | solution.py:57
  158.0 19.4 %collective-permute-start.21 = (bf16[144,512]{1,0:T(8,128)(2,1)}, bf16[144,512]{1,0:T(8,128)(2,1)S(1)}, u32[]{:S(2)}, u32[]{:S(2)}) collective-permute-start(bf16[144,512]{1,0:T(8,128)(2,1)} %get-tuple-element.42), channel_id=1, source_target_pairs={{0,16},{4,20},{8,24},{12,28},{16,0},{20,4},{24,8},{28,12},{1,17},{... | collective-permute-start | bytes 442376 | tf_op jit(solution)/shard_map/ppermute | solution.py:57
  160.4 17.0 %copy-start.7 = (s32[2]{0:T(128)S(1)}, s32[2]{0:T(128)}, u32[]{:S(2)}) copy-start(s32[2]{0:T(128)} %copy-done.6) | copy-start | bytes 28
  160.4 17.0 %collective-permute-start.23 = (bf16[144,512]{1,0:T(8,128)(2,1)}, bf16[144,512]{1,0:T(8,128)(2,1)S(1)}, u32[]{:S(2)}, u32[]{:S(2)}) collective-permute-start(bf16[144,512]{1,0:T(8,128)(2,1)} %get-tuple-element.44), channel_id=1, source_target_pairs={{0,24},{4,28},{8,16},{12,20},{16,8},{20,12},{24,0},{28,4},{1,25},{... | collective-permute-start | bytes 442376 | tf_op jit(solution)/shard_map/ppermute | solution.py:57
  163.0 23.2 %copy-start.16 = (bf16[512,64]{1,0:T(8,128)(2,1)S(1)}, bf16[512,64]{1,0:T(8,128)(2,1)}, u32[]{:S(2)}) copy-start(bf16[512,64]{1,0:T(8,128)(2,1)} %get-tuple-element.28) | copy-start | bytes 196612
  163.0 23.9 %all-to-all-start.3 = ((bf16[8,4,16,256]{3,2,1,0:T(8,128)(2,1)}), bf16[8,4,16,256]{3,2,1,0:T(8,128)(2,1)S(1)}, u32[]{:S(2)}, u32[]{:S(2)}) async-start(bf16[8,4,16,256]{3,2,1,0:T(8,128)(2,1)} %reduce.1), calls=%async_computation.3 | async-start | bytes 524288 | tf_op jit(solution)/shard_map/all_to_all | solution.py:61
  179.4 6.8 %collective-permute-start.26 = (bf16[144,1024]{1,0:T(8,128)(2,1)S(1)}, bf16[144,1024]{1,0:T(8,128)(2,1)S(1)}, u32[]{:S(2)}, u32[]{:S(2)}) collective-permute-start(bf16[144,1024]{1,0:T(8,128)(2,1)S(1)} %scatter.1.refs_0_), channel_id=1, source_target_pairs={{0,2},{1,3},{2,0},{3,1},{4,6},{5,7},{6,4},{7,5},{8,10},{9,11},{10,... | collective-permute-start | bytes 884744 | tf_op jit(solution)/shard_map/ppermute | solution.py:57
  180.9 7.4 %collective-permute-start.25 = (bf16[144,1024]{1,0:T(8,128)(2,1)S(1)}, bf16[144,1024]{1,0:T(8,128)(2,1)S(1)}, u32[]{:S(2)}, u32[]{:S(2)}) collective-permute-start(bf16[144,1024]{1,0:T(8,128)(2,1)S(1)} %scatter.1.refs_0_), channel_id=1, source_target_pairs={{0,1},{1,0},{2,3},{3,2},{4,5},{5,4},{6,7},{7,6},{8,9},{9,8},{10,11... | collective-permute-start | bytes 884744 | tf_op jit(solution)/shard_map/ppermute | solution.py:57
  186.2 2.1 %collective-permute-start.27 = (bf16[144,1024]{1,0:T(8,128)(2,1)S(1)}, bf16[144,1024]{1,0:T(8,128)(2,1)S(1)}, u32[]{:S(2)}, u32[]{:S(2)}) collective-permute-start(bf16[144,1024]{1,0:T(8,128)(2,1)S(1)} %collective-permute-done.26.refs_2_), channel_id=1, source_target_pairs={{0,1},{1,0},{2,3},{3,2},{4,5},{5,4},{6,7},{7,6},{8,9},{9,8},{10,11... | collective-permute-start | bytes 884744 | tf_op jit(solution)/shard_map/ppermute | solution.py:57
  (3 other events, 2.5 us)

commit v2 on v1

--- a/solution.py
+++ b/solution.py
@@ -202,7 +202,7 @@
         kts[c][width:, :] = jnp.where(block == place, 1.0, 0.0).astype(BF16)
 
     scale2 = scale * math.log2(math.e)
-    step = 512
+    step = 1024
     chunks = [(c, i) for c in range(2) for i in range(0, half, step)]
     top = jnp.full((rows, 1), -jnp.inf, F32)
     total = jnp.zeros((rows, 1), F32)
@@ -290,7 +290,7 @@
     c2 = swap(c0, "seq", 4)
     c1 = swap(c0, "seq", 2)
 
-    (c2,) = call(tie_kernel, "after", (asked,), [ANY], [], tied=c2)
+    (c2,) = call(tie_kernel, "after", (asked, c1), [ANY] * 2, [], tied=c2)
     c3 = swap(c2, "seq", 2)
     away, k0 = call(
         functools.partial(gather_kernel, per_peer),
@@ -371,9 +371,9 @@
         [((peers, share, queries, value + nope), BF16)],
     )
     near = owner(*near)
-    got = [near[0]]
-    for k in range(1, peers):
-        got.append(swap((far if k % 2 else near)[k // 2], "seq", k))
+    got = [near[0]] + [None] * (peers - 1)
+    for k in (7, 5, 3, 1, 6, 4, 2):
+        got[k] = swap((far if k % 2 else near)[k // 2], "seq", k)
     res = seq_swap(res).reshape(heads, queries, value + nope)
 
     (y0,) = call(

time: 193 us -> 191 us (0.990)
  waiting for transfers between devices: 92.1 us -> 87.3 us
  starting transfers between devices: 53.5 us -> 55.8 us
    ppermute x28, waiting for transfers between devices: 81.2 us -> 76.3 us  [swap(): return lax.ppermute(x, axis, [(i, i ^ bit) for i in range(n)])]
  transfers between devices with their start and end apart: 32 -> 32, of which waited for: 12 -> 11; matrix products, arithmetic and copies ran while one was open for 2% -> 3% of each run, Pallas kernels for 5% -> 5%
where the time goes in v2:
time: 191 us; the launch traced here: 188 us
  waiting for transfers between devices  87.3 us (46%)
  starting transfers between devices  55.8 us (29%)
  Pallas kernels  36.2 us (19%)
  local copies, waits for them, and re-layouts  6.82 us (4%)
    ppermute x28, waiting for transfers between devices, swap(): return lax.ppermute(x, axis, [(i, i ^ bit) for i in range(n)])  76.3 us
    pallas_call x13, Pallas kernels, call(): pl.pallas_call(body, out_shape=out_shape, in_specs=specs, out_specs=out_s...  36.2 us
    ppermute x28, starting transfers between devices, swap(): return lax.ppermute(x, axis, [(i, i ^ bit) for i in range(n)])  35.2 us
    all_to_all x4, starting transfers between devices, seq_swap(): return lax.all_to_all(x, 'seq', split_axis=0, concat_axis=0, tiled=True)  20.6 us
    all_to_all x4, waiting for transfers between devices, seq_swap(): return lax.all_to_all(x, 'seq', split_axis=0, concat_axis=0, tiled=True)  11 us
    unnamed x42, local copies, waits for them, and re-layouts  5.5 us
  transfers between devices with their start and end apart: 32, of which 11 were waited for; matrix products, arithmetic and copies ran while one was open for 3% of the time, Pallas kernels for 5%

profile of v2, /device:TPU:0, one launch (start us, length us, event | category | flops | bytes accessed | tf_op | source)
XLA Modules:
  0.0 188.3 jit_solution(187931758597593497)
XLA Ops:
  0.7 1.3 copy-done.3
  2.6 4.1 %collective-permute-start.1 = (bf16[144,1024]{1,0:T(8,128)(2,1)S(1)}, bf16[144,1024]{1,0:T(8,128)(2,1)S(1)}, u32[]{:S(2)}, u32[]{:S(2)}) collective-permute-start(bf16[144,1024]{1,0:T(8,128)(2,1)S(1)} %cut.1.refs_0_), channel_id=1, source_target_pairs={{0,16},{4,20},{8,24},{12,28},{16,0},{20,4},{24,8},{28,12},{1,17},{... | collective-permute-start | bytes 884744 | tf_op jit(solution)/shard_map/ppermute | solution.py:57
  6.7 1.6 collective-permute-start
  8.3 1.5 collective-permute-start.2
  9.8 2.0 %collective-permute-done.2.other = s32[1,64]{1,0:T(1,128)S(1)} collective-permute-done((s32[1,64]{1,0:T(1,128)S(1)}, s32[1,64]{1,0:T(1,128)S(1)}, u32[]{:S(2)}, u32[]{:S(2)}) %collective-permute-start.2) | collective-permute-done | bytes 288 | tf_op jit(solution)/shard_map/ppermute | solution.py:57
  11.9 1.9 %collective-permute-start.4 = (s32[2,64]{1,0:T(2,128)S(1)}, s32[2,64]{1,0:T(2,128)S(1)}, u32[]{:S(2)}, u32[]{:S(2)}) collective-permute-start(s32[2,64]{1,0:T(2,128)S(1)} %pad_add_fusion), channel_id=1, source_target_pairs={{0,16},{4,20},{8,24},{12,28},{16,0},{20,4},{24,8},{28,12},{1,17},{... | collective-permute-start | bytes 1544 | tf_op jit(solution)/shard_map/ppermute | solution.py:57
  13.8 2.5 %collective-permute-start.3 = (s32[2,64]{1,0:T(2,128)S(1)}, s32[2,64]{1,0:T(2,128)S(1)}, u32[]{:S(2)}, u32[]{:S(2)}) collective-permute-start(s32[2,64]{1,0:T(2,128)S(1)} %pad_add_fusion), channel_id=1, source_target_pairs={{0,8},{4,12},{8,0},{12,4},{16,24},{20,28},{24,16},{28,20},{1,9},{5... | collective-permute-start | bytes 1544 | tf_op jit(solution)/shard_map/ppermute | solution.py:57
  16.9 4.3 %collective-permute-done.5 = s32[2,64]{1,0:T(2,128)S(1)} collective-permute-done((s32[2,64]{1,0:T(2,128)S(1)}, s32[2,64]{1,0:T(2,128)S(1)}, u32[]{:S(2)}, u32[]{:S(2)}) %collective-permute-start.5) | collective-permute-done | bytes 544 | tf_op jit(solution)/shard_map/ppermute | solution.py:57
  21.2 0.8 collective-permute-start.6
  22.1 1.1 pad_maximum_fusion.refs_0_
  23.3 5.7 %collective-permute-done.6.refs_2_.refs_3_ = bf16[144,1024]{1,0:T(8,128)(2,1)S(1)} collective-permute-done((bf16[144,1024]{1,0:T(8,128)(2,1)S(1)}, bf16[144,1024]{1,0:T(8,128)(2,1)S(1)}, u32[]{:S(2)}, u32[]{:S(2)}) %collective-permute-start.6) | collective-permute-done | bytes 294944 | tf_op jit(solution)/shard_map/ppermute | solution.py:57
  28.9 6.0 %all-to-all-start = ((bf16[32,160,128]{2,1,0:T(8,128)(2,1)}), bf16[32,160,128]{2,1,0:T(8,128)(2,1)S(1)}, u32[]{:S(2)}, u32[]{:S(2)}) async-start(bf16[32,160,128]{2,1,0:T(8,128)(2,1)} %after.3), calls=%async_computation | async-start | bytes 2621440 | tf_op jit(solution)/shard_map/all_to_all | solution.py:61
  34.9 3.3 %gather.1 = (bf16[144,2048]{1,0:T(8,128)(2,1)S(1)}, bf16[144,2048]{1,0:T(8,128)(2,1)S(1)}) custom-call(s32[2]{0:T(128)S(1)} %pad_add_fusion.1.ids, s32[1,64]{1,0:T(1,128)S(1)} %copy-done.8, s32[1,64]{1,0:T(1,128)S(1)} %collective-permute-done.2.other, bf16[144,1024]{1,0:T(8,128)(2,1)S(1)} %cut.1.refs_0_, ...), custom_call_target="tpu_custom_call" | custom-call | tf_op jit(solution)/shard_map/gather/pallas_call | solution.py:35
  38.2 2.1 %collective-permute-start.7 = (bf16[144,2048]{1,0:T(8,128)(2,1)S(1)}, bf16[144,2048]{1,0:T(8,128)(2,1)S(1)}, u32[]{:S(2)}, u32[]{:S(2)}) collective-permute-start(bf16[144,2048]{1,0:T(8,128)(2,1)S(1)} %get-tuple-element.25), channel_id=1, source_target_pairs={{0,4},{4,0},{8,12},{12,8},{16,20},{20,16},{24,28},{28,24},{1,5},{5... | collective-permute-start | bytes 1769480 | tf_op jit(solution)/shard_map/ppermute | solution.py:57
  40.3 1.5 collective-permute-start.8
  41.8 21.5 %collective-permute-done.7.away.refs_4_ = bf16[144,2048]{1,0:T(8,128)(2,1)S(1)} collective-permute-done((bf16[144,2048]{1,0:T(8,128)(2,1)S(1)}, bf16[144,2048]{1,0:T(8,128)(2,1)S(1)}, u32[]{:S(2)}, u32[]{:S(2)}) %collective-permute-start.7) | collective-permute-done | bytes 589856 | tf_op jit(solution)/shard_map/ppermute | solution.py:57
  63.4 2.4 %all-to-all-done = bf16[32,160,128]{2,1,0:T(8,128)(2,1)S(1)} async-done(((bf16[32,160,128]{2,1,0:T(8,128)(2,1)}), bf16[32,160,128]{2,1,0:T(8,128)(2,1)S(1)}, u32[]{:S(2)}, u32[]{:S(2)}) %all-to-all-start) | async-done | bytes 1310752 | tf_op jit(solution)/shard_map/all_to_all | solution.py:61
  65.8 1.4 expand.1
  67.1 4.6 %all-to-all-start.1 = ((bf16[8,4,16,1024]{3,2,1,0:T(8,128)(2,1)}), bf16[8,4,16,1024]{3,2,1,0:T(8,128)(2,1)}, u32[]{:S(2)}, u32[]{:S(2)}) async-start(bf16[8,4,16,1024]{3,2,1,0:T(8,128)(2,1)} %expand.1), calls=%async_computation.1 | async-start | bytes 2097152 | tf_op jit(solution)/shard_map/all_to_all | solution.py:61
  71.7 1.6 collective-permute-start.12
  73.9 11.8 %collective-permute-done.12.refs_6_ = bf16[144,2048]{1,0:T(8,128)(2,1)S(1)} collective-permute-done((bf16[144,2048]{1,0:T(8,128)(2,1)S(1)}, bf16[144,2048]{1,0:T(8,128)(2,1)S(1)}, u32[]{:S(2)}, u32[]{:S(2)}) %collective-permute-start.12) | collective-permute-done | bytes 589856 | tf_op jit(solution)/shard_map/ppermute | solution.py:57
  85.7 0.8 copy.34
  86.6 0.7 copy-done.10
  87.5 0.9 copy-done.12
  88.4 8.6 %all-to-all-done.1 = bf16[8,4,16,1024]{3,2,1,0:T(8,128)(2,1)} async-done(((bf16[8,4,16,1024]{3,2,1,0:T(8,128)(2,1)}), bf16[8,4,16,1024]{3,2,1,0:T(8,128)(2,1)}, u32[]{:S(2)}, u32[]{:S(2)}) %all-to-all-start.1) | async-done | bytes 1048608 | tf_op jit(solution)/shard_map/all_to_all | solution.py:61
  97.0 22.3 %attend.1 = (bf16[2,144,2048]{2,1,0:T(8,128)(2,1)}, bf16[2,144,2048]{2,1,0:T(8,128)(2,1)}, bf16[2,144,2048]{2,1,0:T(8,128)(2,1)}, bf16[2,144,2048]{2,1,0:T(8,128...) custom-call(s32[2]{0:T(128)} %copy-done.6, s32[16,32]{1,0:T(8,128)} %sel.1, bf16[32,16,64]{2,1,0:T(8,128)(2,1)} %bitcast.38, ...), custom_call_target="tpu_custom_call" | custom-call | tf_op jit(solution)/shard_map/attend/pallas_call | solution.py:35
  119.4 3.7 %all-to-all-start.2 = ((bf16[8,4,16,1024]{3,2,1,0:T(8,128)(2,1)}), bf16[8,4,16,1024]{3,2,1,0:T(8,128)(2,1)S(1)}, u32[]{:S(2)}, u32[]{:S(2)}) async-start(bf16[8,4,16,1024]{3,2,1,0:T(8,128)(2,1)} %bitcast.36), calls=%async_computation.2 | async-start | bytes 2097152 | tf_op jit(solution)/shard_map/all_to_all | solution.py:61
  123.5 1.5 pair.2
  125.1 1.6 collective-permute-start.17
  126.9 1.2 collective-permute-start.16
  128.1 13.2 %collective-permute-done.17.got = bf16[144,2048]{1,0:T(8,128)(2,1)S(1)} collective-permute-done((bf16[144,2048]{1,0:T(8,128)(2,1)S(1)}, bf16[144,2048]{1,0:T(8,128)(2,1)S(1)}, u32[]{:S(2)}, u32[]{:S(2)}) %collective-permute-start.17) | collective-permute-done | bytes 589856 | tf_op jit(solution)/shard_map/ppermute | solution.py:57
  141.3 0.8 owner.3
  142.1 1.6 collective-permute-start.18
  143.7 1.5 collective-permute-start.20
  145.2 3.3 %collective-permute-start.22 = (bf16[144,512]{1,0:T(8,128)(2,1)}, bf16[144,512]{1,0:T(8,128)(2,1)S(1)}, u32[]{:S(2)}, u32[]{:S(2)}) collective-permute-start(bf16[144,512]{1,0:T(8,128)(2,1)} %get-tuple-element.43), channel_id=1, source_target_pairs={{0,20},{4,16},{8,28},{12,24},{16,4},{20,0},{24,12},{28,8},{1,21},{... | collective-permute-start | bytes 442376 | tf_op jit(solution)/shard_map/ppermute | solution.py:57
  148.8 4.5 %collective-permute-done.16.got = bf16[144,2048]{1,0:T(8,128)(2,1)S(1)} collective-permute-done((bf16[144,2048]{1,0:T(8,128)(2,1)S(1)}, bf16[144,2048]{1,0:T(8,128)(2,1)S(1)}, u32[]{:S(2)}, u32[]{:S(2)}) %collective-permute-start.16) | collective-permute-done | bytes 589856 | tf_op jit(solution)/shard_map/ppermute | solution.py:57
  153.3 0.8 owner.2
  154.1 1.7 collective-permute-start.19
  155.8 2.4 %collective-permute-start.21 = (bf16[144,512]{1,0:T(8,128)(2,1)}, bf16[144,512]{1,0:T(8,128)(2,1)S(1)}, u32[]{:S(2)}, u32[]{:S(2)}) collective-permute-start(bf16[144,512]{1,0:T(8,128)(2,1)} %get-tuple-element.42), channel_id=1, source_target_pairs={{0,16},{4,20},{8,24},{12,28},{16,0},{20,4},{24,8},{28,12},{1,17},{... | collective-permute-start | bytes 442376 | tf_op jit(solution)/shard_map/ppermute | solution.py:57
  158.2 1.5 collective-permute-start.23
  159.7 1.1 reduce.1
  160.8 6.4 %all-to-all-start.3 = ((bf16[8,4,16,256]{3,2,1,0:T(8,128)(2,1)}), bf16[8,4,16,256]{3,2,1,0:T(8,128)(2,1)S(1)}, u32[]{:S(2)}, u32[]{:S(2)}) async-start(bf16[8,4,16,256]{3,2,1,0:T(8,128)(2,1)} %reduce.1), calls=%async_computation.3 | async-start | bytes 524288 | tf_op jit(solution)/shard_map/all_to_all | solution.py:61
  167.2 8.0 %collective-permute-done.21.refs_4_ = bf16[144,512]{1,0:T(8,128)(2,1)S(1)} collective-permute-done((bf16[144,512]{1,0:T(8,128)(2,1)}, bf16[144,512]{1,0:T(8,128)(2,1)S(1)}, u32[]{:S(2)}, u32[]{:S(2)}) %collective-permute-start.21) | collective-permute-done | bytes 147488 | tf_op jit(solution)/shard_map/ppermute | solution.py:57
  175.3 2.0 %scatter.1.refs_0_ = bf16[144,1024]{1,0:T(8,128)(2,1)S(1)} custom-call(s32[2]{0:T(128)S(1)} %copy-done.7, s32[8,64]{1,0:T(8,128)S(1)} %concatenate.12.refs_1_.rows, bf16[144,512]{1,0:T(8,128)(2,1)S(1)} %get-tuple-element.36.refs_0_, bf16[144,512]{1,0:T(8,128)(2,1)S(1)} %collective-permute-done.18.refs_1_, ...), custom_call_target="tpu_custom_call" | custom-call | tf_op jit(solution)/shard_map/scatter/pallas_call | solution.py:35
  177.2 1.6 collective-permute-start.26
  178.8 5.2 %collective-permute-done.26.refs_2_ = bf16[144,1024]{1,0:T(8,128)(2,1)S(1)} collective-permute-done((bf16[144,1024]{1,0:T(8,128)(2,1)S(1)}, bf16[144,1024]{1,0:T(8,128)(2,1)S(1)}, u32[]{:S(2)}, u32[]{:S(2)}) %collective-permute-start.26) | collective-permute-done | bytes 294944 | tf_op jit(solution)/shard_map/ppermute | solution.py:57
  184.0 0.7 copy.33
  186.2 2.1 %assemble.1 = f32[576,1024]{1,0:T(8,128)} custom-call(s32[2]{0:T(128)S(1)} %copy-done.7, bf16[144,1024]{1,0:T(8,128)(2,1)S(1)} %scatter.1.refs_0_, bf16[144,1024]{1,0:T(8,128)(2,1)S(1)} %collective-permute-done.25.refs_1_, bf16[144,1024]{1,0:T(8,128)(2,1)S(1)} %collective-permute-done.26.refs_2_, bf16[144,1024]{1,0:T(8,128)(2,1)S(1)} %collective-permute-done.27.refs_3_), custom_call_target="tpu_custom_call" | custom-call | tf_op jit(solution)/shard_map/assemble/pallas_call | solution.py:35
  (80 shorter events, 4.9 us)
Async XLA Ops:
  0.6 7.6 %copy-start.8 = (s32[1,64]{1,0:T(1,128)S(1)}, s32[1,64]{1,0:T(1,128)}, u32[]{:S(2)}) copy-start(s32[1,64]{1,0:T(1,128)} %own.1) | copy-start | bytes 772
  0.7 34.2 %copy-start.6 = (s32[2]{0:T(128)}, s32[2]{0:T(128)S(1)}, u32[]{:S(2)}) copy-start(s32[2]{0:T(128)S(1)} %pad_add_fusion.1.ids) | copy-start | bytes 28
  0.7 1.3 copy-start.3
  2.0 14.3 %copy-start.13 = (bf16[32,8192]{1,0:T(8,128)(2,1)S(1)}, bf16[32,8192]{1,0:T(8,128)(2,1)}, u32[]{:S(2)}) copy-start(bf16[32,8192]{1,0:T(8,128)(2,1)} %param.11) | copy-start | bytes 1572868
  2.6 14.2 %copy-start.14 = (bf16[32,8192]{1,0:T(8,128)(2,1)S(1)}, bf16[32,8192]{1,0:T(8,128)(2,1)}, u32[]{:S(2)}) copy-start(bf16[32,8192]{1,0:T(8,128)(2,1)} %param.12) | copy-start | bytes 1572868
  2.6 18.6 %collective-permute-start.1 = (bf16[144,1024]{1,0:T(8,128)(2,1)S(1)}, bf16[144,1024]{1,0:T(8,128)(2,1)S(1)}, u32[]{:S(2)}, u32[]{:S(2)}) collective-permute-start(bf16[144,1024]{1,0:T(8,128)(2,1)S(1)} %cut.1.refs_0_), channel_id=1, source_target_pairs={{0,16},{4,20},{8,24},{12,28},{16,0},{20,4},{24,8},{28,12},{1,17},{... | collective-permute-start | bytes 884744 | tf_op jit(solution)/shard_map/ppermute | solution.py:57
  6.7 14.5 %collective-permute-start = (bf16[144,1024]{1,0:T(8,128)(2,1)S(1)}, bf16[144,1024]{1,0:T(8,128)(2,1)S(1)}, u32[]{:S(2)}, u32[]{:S(2)}) collective-permute-start(bf16[144,1024]{1,0:T(8,128)(2,1)S(1)} %cut.1.refs_0_), channel_id=1, source_target_pairs={{0,8},{4,12},{8,0},{12,4},{16,24},{20,28},{24,16},{28,20},{1,9},{5... | collective-permute-start | bytes 884744 | tf_op jit(solution)/shard_map/ppermute | solution.py:57
  8.3 3.5 %collective-permute-start.2 = (s32[1,64]{1,0:T(1,128)S(1)}, s32[1,64]{1,0:T(1,128)S(1)}, u32[]{:S(2)}, u32[]{:S(2)}) collective-permute-start(s32[1,64]{1,0:T(1,128)S(1)} %copy-done.8), channel_id=1, source_target_pairs={{0,4},{4,0},{8,12},{12,8},{16,20},{20,16},{24,28},{28,24},{1,5},{5... | collective-permute-start | bytes 776 | tf_op jit(solution)/shard_map/ppermute | solution.py:57
  11.8 9.3 %collective-permute-start.5 = (s32[2,64]{1,0:T(2,128)S(1)}, s32[2,64]{1,0:T(2,128)S(1)}, u32[]{:S(2)}, u32[]{:S(2)}) collective-permute-start(s32[2,64]{1,0:T(2,128)S(1)} %pad_add_fusion), channel_id=1, source_target_pairs={{0,24},{4,28},{8,16},{12,20},{16,8},{20,12},{24,0},{28,4},{1,25},{... | collective-permute-start | bytes 1544 | tf_op jit(solution)/shard_map/ppermute | solution.py:57
  11.9 9.3 %collective-permute-start.4 = (s32[2,64]{1,0:T(2,128)S(1)}, s32[2,64]{1,0:T(2,128)S(1)}, u32[]{:S(2)}, u32[]{:S(2)}) collective-permute-start(s32[2,64]{1,0:T(2,128)S(1)} %pad_add_fusion), channel_id=1, source_target_pairs={{0,16},{4,20},{8,24},{12,28},{16,0},{20,4},{24,8},{28,12},{1,17},{... | collective-permute-start | bytes 1544 | tf_op jit(solution)/shard_map/ppermute | solution.py:57
  13.8 7.4 %collective-permute-start.3 = (s32[2,64]{1,0:T(2,128)S(1)}, s32[2,64]{1,0:T(2,128)S(1)}, u32[]{:S(2)}, u32[]{:S(2)}) collective-permute-start(s32[2,64]{1,0:T(2,128)S(1)} %pad_add_fusion), channel_id=1, source_target_pairs={{0,8},{4,12},{8,0},{12,4},{16,24},{20,28},{24,16},{28,20},{1,9},{5... | collective-permute-start | bytes 1544 | tf_op jit(solution)/shard_map/ppermute | solution.py:57
  16.6 5.4 %copy-start.17 = (bf16[16,32,128]{2,1,0:T(8,128)(2,1)S(1)}, bf16[16,32,128]{2,1,0:T(8,128)(2,1)}, u32[]{:S(2)}) copy-start(bf16[16,32,128]{2,1,0:T(8,128)(2,1)} %param.13) | copy-start | bytes 393220
  16.6 5.4 %copy-start.18 = (bf16[16,32,128]{2,1,0:T(8,128)(2,1)S(1)}, bf16[16,32,128]{2,1,0:T(8,128)(2,1)}, u32[]{:S(2)}) copy-start(bf16[16,32,128]{2,1,0:T(8,128)(2,1)} %param.8) | copy-start | bytes 393220
  21.2 7.7 %collective-permute-start.6 = (bf16[144,1024]{1,0:T(8,128)(2,1)S(1)}, bf16[144,1024]{1,0:T(8,128)(2,1)S(1)}, u32[]{:S(2)}, u32[]{:S(2)}) collective-permute-start(bf16[144,1024]{1,0:T(8,128)(2,1)S(1)} %after.2.refs_2_), channel_id=1, source_target_pairs={{0,8},{4,12},{8,0},{12,4},{16,24},{20,28},{24,16},{28,20},{1,9},{5... | collective-permute-start | bytes 884744 | tf_op jit(solution)/shard_map/ppermute | solution.py:57
  28.9 36.8 %all-to-all-start = ((bf16[32,160,128]{2,1,0:T(8,128)(2,1)}), bf16[32,160,128]{2,1,0:T(8,128)(2,1)S(1)}, u32[]{:S(2)}, u32[]{:S(2)}) async-start(bf16[32,160,128]{2,1,0:T(8,128)(2,1)} %after.3), calls=%async_computation | async-start | bytes 2621440 | tf_op jit(solution)/shard_map/all_to_all | solution.py:61
  38.2 35.1 %copy-start.5 = (bf16[144,2048]{1,0:T(8,128)(2,1)}, bf16[144,2048]{1,0:T(8,128)(2,1)S(1)}, u32[]{:S(2)}) copy-start(bf16[144,2048]{1,0:T(8,128)(2,1)S(1)} %get-tuple-element.26.refs_0_) | copy-start | bytes 1769476
  38.2 25.1 %collective-permute-start.7 = (bf16[144,2048]{1,0:T(8,128)(2,1)S(1)}, bf16[144,2048]{1,0:T(8,128)(2,1)S(1)}, u32[]{:S(2)}, u32[]{:S(2)}) collective-permute-start(bf16[144,2048]{1,0:T(8,128)(2,1)S(1)} %get-tuple-element.25), channel_id=1, source_target_pairs={{0,4},{4,0},{8,12},{12,8},{16,20},{20,16},{24,28},{28,24},{1,5},{5... | collective-permute-start | bytes 1769480 | tf_op jit(solution)/shard_map/ppermute | solution.py:57
  40.3 23.0 %collective-permute-start.8 = (bf16[144,2048]{1,0:T(8,128)(2,1)S(1)}, bf16[144,2048]{1,0:T(8,128)(2,1)S(1)}, u32[]{:S(2)}, u32[]{:S(2)}) collective-permute-start(bf16[144,2048]{1,0:T(8,128)(2,1)S(1)} %get-tuple-element.26.refs_0_), channel_id=1, source_target_pairs={{0,2},{1,3},{2,0},{3,1},{4,6},{5,7},{6,4},{7,5},{8,10},{9,11},{10,... | collective-permute-start | bytes 1769480 | tf_op jit(solution)/shard_map/ppermute | solution.py:57
  63.4 9.9 %copy-start = (bf16[144,2048]{1,0:T(8,128)(2,1)}, bf16[144,2048]{1,0:T(8,128)(2,1)S(1)}, u32[]{:S(2)}) copy-start(bf16[144,2048]{1,0:T(8,128)(2,1)S(1)} %collective-permute-done.7.away.refs_4_) | copy-start | bytes 1769476
  63.4 10.5 %copy-start.1 = (bf16[144,2048]{1,0:T(8,128)(2,1)}, bf16[144,2048]{1,0:T(8,128)(2,1)S(1)}, u32[]{:S(2)}) copy-start(bf16[144,2048]{1,0:T(8,128)(2,1)S(1)} %collective-permute-done.8.over_x.refs_2_) | copy-start | bytes 1769476
  67.1 18.6 %copy-start.15 = (bf16[16,32,64]{2,1,0:T(8,128)(2,1)S(1)}, bf16[16,32,64]{2,1,0:T(8,128)(2,1)}, u32[]{:S(2)}) copy-start(bf16[16,32,64]{2,1,0:T(8,128)(2,1)} %param.9) | copy-start | bytes 196612
  67.1 29.9 %all-to-all-start.1 = ((bf16[8,4,16,1024]{3,2,1,0:T(8,128)(2,1)}), bf16[8,4,16,1024]{3,2,1,0:T(8,128)(2,1)}, u32[]{:S(2)}, u32[]{:S(2)}) async-start(bf16[8,4,16,1024]{3,2,1,0:T(8,128)(2,1)} %expand.1), calls=%async_computation.1 | async-start | bytes 2097152 | tf_op jit(solution)/shard_map/all_to_all | solution.py:61
  71.7 14.0 %collective-permute-start.12 = (bf16[144,2048]{1,0:T(8,128)(2,1)S(1)}, bf16[144,2048]{1,0:T(8,128)(2,1)S(1)}, u32[]{:S(2)}, u32[]{:S(2)}) collective-permute-start(bf16[144,2048]{1,0:T(8,128)(2,1)S(1)} %collective-permute-done.7.away.refs_4_), channel_id=1, source_target_pairs={{0,2},{1,3},{2,0},{3,1},{4,6},{5,7},{6,4},{7,5},{8,10},{9,11},{10,... | collective-permute-start | bytes 1769480 | tf_op jit(solution)/shard_map/ppermute | solution.py:57
  73.3 13.2 %collective-permute-start.9 = (bf16[144,2048]{1,0:T(8,128)(2,1)S(1)}, bf16[144,2048]{1,0:T(8,128)(2,1)S(1)}, u32[]{:S(2)}, u32[]{:S(2)}) collective-permute-start(bf16[144,2048]{1,0:T(8,128)(2,1)S(1)} %get-tuple-element.26.refs_0_), channel_id=1, source_target_pairs={{0,1},{1,0},{2,3},{3,2},{4,5},{5,4},{6,7},{7,6},{8,9},{9,8},{10,11... | collective-permute-start | bytes 1769480 | tf_op jit(solution)/shard_map/ppermute | solution.py:57
  73.3 13.2 %collective-permute-start.11 = (bf16[144,2048]{1,0:T(8,128)(2,1)S(1)}, bf16[144,2048]{1,0:T(8,128)(2,1)S(1)}, u32[]{:S(2)}, u32[]{:S(2)}) collective-permute-start(bf16[144,2048]{1,0:T(8,128)(2,1)S(1)} %collective-permute-done.7.away.refs_4_), channel_id=1, source_target_pairs={{0,1},{1,0},{2,3},{3,2},{4,5},{5,4},{6,7},{7,6},{8,9},{9,8},{10,11... | collective-permute-start | bytes 1769480 | tf_op jit(solution)/shard_map/ppermute | solution.py:57
  73.8 12.7 %collective-permute-start.10 = (bf16[144,2048]{1,0:T(8,128)(2,1)S(1)}, bf16[144,2048]{1,0:T(8,128)(2,1)S(1)}, u32[]{:S(2)}, u32[]{:S(2)}) collective-permute-start(bf16[144,2048]{1,0:T(8,128)(2,1)S(1)} %collective-permute-done.8.over_x.refs_2_), channel_id=1, source_target_pairs={{0,1},{1,0},{2,3},{3,2},{4,5},{5,4},{6,7},{7,6},{8,9},{9,8},{10,11... | collective-permute-start | bytes 1769480 | tf_op jit(solution)/shard_map/ppermute | solution.py:57
  85.7 2.7 %collective-permute-start.13 = (bf16[144,2048]{1,0:T(8,128)(2,1)S(1)}, bf16[144,2048]{1,0:T(8,128)(2,1)}, u32[]{:S(2)}, u32[]{:S(2)}) collective-permute-start(bf16[144,2048]{1,0:T(8,128)(2,1)S(1)} %collective-permute-done.12.refs_6_), channel_id=1, source_target_pairs={{0,1},{1,0},{2,3},{3,2},{4,5},{5,4},{6,7},{7,6},{8,9},{9,8},{10,11... | collective-permute-start | bytes 1769480 | tf_op jit(solution)/shard_map/ppermute | solution.py:57
  86.5 1.0 copy-start.11
  119.3 4.2 %copy-start.2 = (bf16[2,144,2048]{2,1,0:T(8,128)(2,1)S(1)}, bf16[2,144,2048]{2,1,0:T(8,128)(2,1)}, u32[]{:S(2)}) copy-start(bf16[2,144,2048]{2,1,0:T(8,128)(2,1)} %get-tuple-element.29.keep) | copy-start | bytes 3538948
  119.3 4.2 %collective-permute-start.14 = (bf16[2,144,2048]{2,1,0:T(8,128)(2,1)}, bf16[2,144,2048]{2,1,0:T(8,128)(2,1)}, u32[]{:S(2)}, u32[]{:S(2)}) collective-permute-start(bf16[2,144,2048]{2,1,0:T(8,128)(2,1)} %get-tuple-element.30), channel_id=1, source_target_pairs={{0,1},{1,0},{2,3},{3,2},{4,5},{5,4},{6,7},{7,6},{8,9},{9,8},{10,11... | collective-permute-start | bytes 3538952 | tf_op jit(solution)/shard_map/ppermute | solution.py:57
  119.4 40.3 %all-to-all-start.2 = ((bf16[8,4,16,1024]{3,2,1,0:T(8,128)(2,1)}), bf16[8,4,16,1024]{3,2,1,0:T(8,128)(2,1)S(1)}, u32[]{:S(2)}, u32[]{:S(2)}) async-start(bf16[8,4,16,1024]{3,2,1,0:T(8,128)(2,1)} %bitcast.36), calls=%async_computation.2 | async-start | bytes 2097152 | tf_op jit(solution)/shard_map/all_to_all | solution.py:61
  123.1 3.5 %copy-start.4 = (bf16[2,144,2048]{2,1,0:T(8,128)(2,1)S(1)}, bf16[2,144,2048]{2,1,0:T(8,128)(2,1)}, u32[]{:S(2)}) copy-start(bf16[2,144,2048]{2,1,0:T(8,128)(2,1)} %get-tuple-element.32.refs_1_) | copy-start | bytes 3538948
  123.1 3.5 %collective-permute-start.15 = (bf16[2,144,2048]{2,1,0:T(8,128)(2,1)}, bf16[2,144,2048]{2,1,0:T(8,128)(2,1)S(1)}, u32[]{:S(2)}, u32[]{:S(2)}) collective-permute-start(bf16[2,144,2048]{2,1,0:T(8,128)(2,1)} %get-tuple-element.33), channel_id=1, source_target_pairs={{0,1},{1,0},{2,3},{3,2},{4,5},{5,4},{6,7},{7,6},{8,9},{9,8},{10,11... | collective-permute-start | bytes 3538952 | tf_op jit(solution)/shard_map/ppermute | solution.py:57
  125.1 16.2 %collective-permute-start.17 = (bf16[144,2048]{1,0:T(8,128)(2,1)S(1)}, bf16[144,2048]{1,0:T(8,128)(2,1)S(1)}, u32[]{:S(2)}, u32[]{:S(2)}) collective-permute-start(bf16[144,2048]{1,0:T(8,128)(2,1)S(1)} %get-tuple-element.38), channel_id=1, source_target_pairs={{0,2},{1,3},{2,0},{3,1},{4,6},{5,7},{6,4},{7,5},{8,10},{9,11},{10,... | collective-permute-start | bytes 1769480 | tf_op jit(solution)/shard_map/ppermute | solution.py:57
  126.9 26.4 %collective-permute-start.16 = (bf16[144,2048]{1,0:T(8,128)(2,1)S(1)}, bf16[144,2048]{1,0:T(8,128)(2,1)S(1)}, u32[]{:S(2)}, u32[]{:S(2)}) collective-permute-start(bf16[144,2048]{1,0:T(8,128)(2,1)S(1)} %get-tuple-element.35), channel_id=1, source_target_pairs={{0,2},{1,3},{2,0},{3,1},{4,6},{5,7},{6,4},{7,5},{8,10},{9,11},{10,... | collective-permute-start | bytes 1769480 | tf_op jit(solution)/shard_map/ppermute | solution.py:57
  142.1 13.7 %collective-permute-start.18 = (bf16[144,512]{1,0:T(8,128)(2,1)S(1)}, bf16[144,512]{1,0:T(8,128)(2,1)S(1)}, u32[]{:S(2)}, u32[]{:S(2)}) collective-permute-start(bf16[144,512]{1,0:T(8,128)(2,1)S(1)} %get-tuple-element.39), channel_id=1, source_target_pairs={{0,4},{4,0},{8,12},{12,8},{16,20},{20,16},{24,28},{28,24},{1,5},{5... | collective-permute-start | bytes 442376 | tf_op jit(solution)/shard_map/ppermute | solution.py:57
  143.7 14.5 %collective-permute-start.20 = (bf16[144,512]{1,0:T(8,128)(2,1)S(1)}, bf16[144,512]{1,0:T(8,128)(2,1)S(1)}, u32[]{:S(2)}, u32[]{:S(2)}) collective-permute-start(bf16[144,512]{1,0:T(8,128)(2,1)S(1)} %get-tuple-element.41), channel_id=1, source_target_pairs={{0,12},{4,8},{8,4},{12,0},{16,28},{20,24},{24,20},{28,16},{1,13},{... | collective-permute-start | bytes 442376 | tf_op jit(solution)/shard_map/ppermute | solution.py:57
  145.2 22.0 %collective-permute-start.22 = (bf16[144,512]{1,0:T(8,128)(2,1)}, bf16[144,512]{1,0:T(8,128)(2,1)S(1)}, u32[]{:S(2)}, u32[]{:S(2)}) collective-permute-start(bf16[144,512]{1,0:T(8,128)(2,1)} %get-tuple-element.43), channel_id=1, source_target_pairs={{0,20},{4,16},{8,28},{12,24},{16,4},{20,0},{24,12},{28,8},{1,21},{... | collective-permute-start | bytes 442376 | tf_op jit(solution)/shard_map/ppermute | solution.py:57
  148.5 18.7 %collective-permute-start.24 = (bf16[144,512]{1,0:T(8,128)(2,1)}, bf16[144,512]{1,0:T(8,128)(2,1)S(1)}, u32[]{:S(2)}, u32[]{:S(2)}) collective-permute-start(bf16[144,512]{1,0:T(8,128)(2,1)} %get-tuple-element.45), channel_id=1, source_target_pairs={{0,28},{4,24},{8,20},{12,16},{16,12},{20,8},{24,4},{28,0},{1,29},{... | collective-permute-start | bytes 442376 | tf_op jit(solution)/shard_map/ppermute | solution.py:57
  154.1 13.1 %collective-permute-start.19 = (bf16[144,512]{1,0:T(8,128)(2,1)}, bf16[144,512]{1,0:T(8,128)(2,1)S(1)}, u32[]{:S(2)}, u32[]{:S(2)}) collective-permute-start(bf16[144,512]{1,0:T(8,128)(2,1)} %get-tuple-element.40), channel_id=1, source_target_pairs={{0,8},{4,12},{8,0},{12,4},{16,24},{20,28},{24,16},{28,20},{1,9},{5... | collective-permute-start | bytes 442376 | tf_op jit(solution)/shard_map/ppermute | solution.py:57
  155.8 19.4 %collective-permute-start.21 = (bf16[144,512]{1,0:T(8,128)(2,1)}, bf16[144,512]{1,0:T(8,128)(2,1)S(1)}, u32[]{:S(2)}, u32[]{:S(2)}) collective-permute-start(bf16[144,512]{1,0:T(8,128)(2,1)} %get-tuple-element.42), channel_id=1, source_target_pairs={{0,16},{4,20},{8,24},{12,28},{16,0},{20,4},{24,8},{28,12},{1,17},{... | collective-permute-start | bytes 442376 | tf_op jit(solution)/shard_map/ppermute | solution.py:57
  158.2 17.0 %copy-start.7 = (s32[2]{0:T(128)S(1)}, s32[2]{0:T(128)}, u32[]{:S(2)}) copy-start(s32[2]{0:T(128)} %copy-done.6) | copy-start | bytes 28
  158.2 17.0 %collective-permute-start.23 = (bf16[144,512]{1,0:T(8,128)(2,1)}, bf16[144,512]{1,0:T(8,128)(2,1)S(1)}, u32[]{:S(2)}, u32[]{:S(2)}) collective-permute-start(bf16[144,512]{1,0:T(8,128)(2,1)} %get-tuple-element.44), channel_id=1, source_target_pairs={{0,24},{4,28},{8,16},{12,20},{16,8},{20,12},{24,0},{28,4},{1,25},{... | collective-permute-start | bytes 442376 | tf_op jit(solution)/shard_map/ppermute | solution.py:57
  160.8 23.2 %copy-start.16 = (bf16[512,64]{1,0:T(8,128)(2,1)S(1)}, bf16[512,64]{1,0:T(8,128)(2,1)}, u32[]{:S(2)}) copy-start(bf16[512,64]{1,0:T(8,128)(2,1)} %get-tuple-element.28) | copy-start | bytes 196612
  160.8 23.9 %all-to-all-start.3 = ((bf16[8,4,16,256]{3,2,1,0:T(8,128)(2,1)}), bf16[8,4,16,256]{3,2,1,0:T(8,128)(2,1)S(1)}, u32[]{:S(2)}, u32[]{:S(2)}) async-start(bf16[8,4,16,256]{3,2,1,0:T(8,128)(2,1)} %reduce.1), calls=%async_computation.3 | async-start | bytes 524288 | tf_op jit(solution)/shard_map/all_to_all | solution.py:61
  177.2 6.8 %collective-permute-start.26 = (bf16[144,1024]{1,0:T(8,128)(2,1)S(1)}, bf16[144,1024]{1,0:T(8,128)(2,1)S(1)}, u32[]{:S(2)}, u32[]{:S(2)}) collective-permute-start(bf16[144,1024]{1,0:T(8,128)(2,1)S(1)} %scatter.1.refs_0_), channel_id=1, source_target_pairs={{0,2},{1,3},{2,0},{3,1},{4,6},{5,7},{6,4},{7,5},{8,10},{9,11},{10,... | collective-permute-start | bytes 884744 | tf_op jit(solution)/shard_map/ppermute | solution.py:57
  178.8 7.4 %collective-permute-start.25 = (bf16[144,1024]{1,0:T(8,128)(2,1)S(1)}, bf16[144,1024]{1,0:T(8,128)(2,1)S(1)}, u32[]{:S(2)}, u32[]{:S(2)}) collective-permute-start(bf16[144,1024]{1,0:T(8,128)(2,1)S(1)} %scatter.1.refs_0_), channel_id=1, source_target_pairs={{0,1},{1,0},{2,3},{3,2},{4,5},{5,4},{6,7},{7,6},{8,9},{9,8},{10,11... | collective-permute-start | bytes 884744 | tf_op jit(solution)/shard_map/ppermute | solution.py:57
  184.0 2.1 %collective-permute-start.27 = (bf16[144,1024]{1,0:T(8,128)(2,1)S(1)}, bf16[144,1024]{1,0:T(8,128)(2,1)S(1)}, u32[]{:S(2)}, u32[]{:S(2)}) collective-permute-start(bf16[144,1024]{1,0:T(8,128)(2,1)S(1)} %collective-permute-done.26.refs_2_), channel_id=1, source_target_pairs={{0,1},{1,0},{2,3},{3,2},{4,5},{5,4},{6,7},{7,6},{8,9},{9,8},{10,11... | collective-permute-start | bytes 884744 | tf_op jit(solution)/shard_map/ppermute | solution.py:57
  (3 other events, 2.5 us)

commit v3 on v2

--- a/solution.py
+++ b/solution.py
@@ -18,9 +18,9 @@
 BF16 = jnp.bfloat16
 
 
-def call(kernel, name, args, specs, outs, scratch=(), mib=32, tied=None):
+def call(kernel, name, args, specs, outs, scratch=(), mib=32, tied=None, out_specs=None):
     out_shape = [jax.ShapeDtypeStruct(s, d) for s, d in outs]
-    out_specs = [VMEM] * len(outs)
+    out_specs = out_specs or [VMEM] * len(outs)
     aliases = {}
     body = kernel
     if tied is not None:
@@ -65,9 +65,12 @@
     pass
 
 
-def cut_kernel(ids, cache, out):
+def cut_kernel(ids, cache, out, sem):
     depth = out.shape[0]
-    out[...] = cache[pl.ds(pl.multiple_of(ids[1] * depth, 16), depth), :]
+    part = cache.at[pl.ds(pl.multiple_of(ids[1] * depth, 16), depth), :]
+    copy = pltpu.make_async_copy(part, out, sem)
+    copy.start()
+    copy.wait()
 
 
 def gather_kernel(per_peer, ids, own, other, *refs):
@@ -174,13 +177,31 @@
 def attend_kernel(scale, per_peer, ids, sel, rope, qd, *refs):
     keys, refs = (refs[:4], refs[4:8]), refs[8:]
     keeps, sends, lat, d_rope, refs = (refs[0], refs[2]), (refs[1], refs[3]), refs[4], refs[5], refs[6:]
-    kt_near, kt_far, pb_near, pb_far, qx, do, sc, flip, cat, o_full, dq = refs
+    kt_near, kt_far, pb_near, pb_far, qx, do, sc, flip, cat, o_full, dq = refs[:11]
+    keep_far, send_far, key_sems, out_sems = refs[11:]
+    leaving = [
+        pltpu.make_async_copy(src, dst, out_sems.at[n])
+        for n, (src, dst) in enumerate(((keep_far, keeps[1]), (send_far, sends[1])))
+    ]
+    keeps, sends = (keeps[0], keep_far), (sends[0], send_far)
     rows, latent = do.shape
     heads, queries, rope_dim = rope.shape
     width = latent + rope_dim
     slots = qx.shape[1] - width
     depth, half = keys[0][0].shape
     kts, pbs = (kt_near, kt_far), (pb_near, pb_far)
+
+    arriving = []
+    for c in range(2):
+        place = lax.broadcasted_iota(jnp.int32, (slots, half), 0)
+        block = lax.broadcasted_iota(jnp.int32, (slots, half), 1) // BLOCK_LEN
+        block = block + (block // per_peer + c) * per_peer
+        kts[c][width:, :] = jnp.where(block == place, 1.0, 0.0).astype(BF16)
+        for k in range(4):
+            at = pl.ds(pl.multiple_of((ids[1] ^ k) * depth, 16), depth)
+            copy = pltpu.make_async_copy(keys[c][k], kts[c].at[at, :], key_sems.at[4 * c + k])
+            copy.start()
+            arriving.append(copy)
 
     picks = sel[...] ^ (ids[0] * per_peer)
     slot = lax.broadcasted_iota(jnp.int32, (queries, slots), 1)
@@ -192,15 +213,6 @@
     qx[:, :latent] = qd[:, :latent]
     qx[:, latent:] = jnp.concatenate([rope[...].reshape(rows, rope_dim), bias], axis=1)
     do[...] = qd[:, latent:]
-    for c in range(2):
-        for k in range(4):
-            at = pl.ds(pl.multiple_of((ids[1] ^ k) * depth, 16), depth)
-            kts[c][at, :] = keys[c][k][...]
-        place = lax.broadcasted_iota(jnp.int32, (slots, half), 0)
-        block = lax.broadcasted_iota(jnp.int32, (slots, half), 1) // BLOCK_LEN
-        block = block + (block // per_peer + c) * per_peer
-        kts[c][width:, :] = jnp.where(block == place, 1.0, 0.0).astype(BF16)
-
     scale2 = scale * math.log2(math.e)
     step = 1024
     chunks = [(c, i) for c in range(2) for i in range(0, half, step)]
@@ -208,6 +220,9 @@
     total = jnp.zeros((rows, 1), F32)
     tops = []
     for n, (c, i) in enumerate(chunks):
+        if i == 0:
+            for copy in arriving[4 * c : 4 * c + 4]:
+                copy.wait()
         s = nn(qx[...], kts[c][:, i : i + step]) * scale2
         high = jnp.maximum(top, jnp.max(s, axis=1, keepdims=True))
         e = jnp.exp2(s - high)
@@ -234,6 +249,9 @@
         at = pl.ds(pl.multiple_of((ids[1] ^ k) * depth, 16), depth)
         cat[k * depth : (k + 1) * depth] = flip[at, :]
     for n, (c, i) in enumerate([(c, i) for c in (1, 0) for i in range(0, half, step)]):
+        if c == 0 and i == 0:
+            for copy in leaving:
+                copy.start()
         at = slice(i, i + step)
         grads = (keeps[c], sends[c], at, depth)
         kt = kts[c].at[:, at]
@@ -244,6 +262,8 @@
             dq[...] += part
     lat[:, latent:] = dq[:, :latent].astype(BF16)
     d_rope[...] = dq[:, latent:].astype(BF16)
+    for copy in leaving:
+        copy.wait()
 
 
 def pair_kernel(keep, got, a0, *a2):
@@ -284,7 +304,14 @@
     scale = 1.0 / math.sqrt(nope + rope)
 
     row1 = swap(slot_blocks, "seq", 1)
-    (c0,) = call(cut_kernel, "cut", (ids, cache.T), [SMEM, VMEM], [((depth, tokens), BF16)])
+    (c0,) = call(
+        cut_kernel,
+        "cut",
+        (ids, cache.T),
+        [SMEM, ANY],
+        [((depth, tokens), BF16)],
+        [pltpu.SemaphoreType.DMA],
+    )
     asked_y = jnp.concatenate([slot_blocks, row1], axis=0)
     asked = jnp.concatenate([asked_y] + [swap(asked_y, "seq", bit) for bit in (2, 4, 6)], axis=0)
     c2 = swap(c0, "seq", 4)
@@ -334,7 +361,7 @@
         functools.partial(attend_kernel, scale, per_peer),
         "attend",
         (ids, sel, rope_rows, qd, *keys),
-        [SMEM] + [VMEM] * 11,
+        [SMEM] + [VMEM] * 3 + [ANY] * 8,
         [((2, depth, half), BF16)] * 4 + [((rows, 2 * latent), BF16), ((rows, rope), BF16)],
         [pltpu.VMEM((width + slots, half), BF16)] * 2
         + [pltpu.VMEM((rows, half), BF16)] * 2
@@ -346,8 +373,13 @@
             pltpu.VMEM((width, 2 * rows), BF16),
             pltpu.VMEM((rows, latent), F32),
             pltpu.VMEM((rows, width), F32),
+            pltpu.VMEM((2, depth, half), BF16),
+            pltpu.VMEM((2, depth, half), BF16),
+            pltpu.SemaphoreType.DMA((8,)),
+            pltpu.SemaphoreType.DMA((2,)),
         ],
         60,
+        out_specs=[VMEM, VMEM, ANY, ANY, VMEM, VMEM],
     )
 
     def pair(keep, send, tied=None):

time: 191 us -> 192 us (level)
  no operation moved by 1% of the time
where the time goes in v3:
time: 192 us; the launch traced here: 189 us
  waiting for transfers between devices  87.3 us (45%)
  starting transfers between devices  55.8 us (29%)
  Pallas kernels  37.1 us (19%)
  local copies, waits for them, and re-layouts  6.82 us (4%)
    ppermute x28, waiting for transfers between devices, swap(): return lax.ppermute(x, axis, [(i, i ^ bit) for i in range(n)])  76.3 us
    pallas_call x13, Pallas kernels, call(): pl.pallas_call(body, out_shape=out_shape, in_specs=specs, out_specs=out_s...  37.1 us
    ppermute x28, starting transfers between devices, swap(): return lax.ppermute(x, axis, [(i, i ^ bit) for i in range(n)])  35.2 us
    all_to_all x4, starting transfers between devices, seq_swap(): return lax.all_to_all(x, 'seq', split_axis=0, concat_axis=0, tiled=True)  20.6 us
    all_to_all x4, waiting for transfers between devices, seq_swap(): return lax.all_to_all(x, 'seq', split_axis=0, concat_axis=0, tiled=True)  11 us
    unnamed x42, local copies, waits for them, and re-layouts  5.5 us
  transfers between devices with their start and end apart: 32, of which 11 were waited for; matrix products, arithmetic and copies ran while one was open for 3% of the time, Pallas kernels for 5%

profile of v3, /device:TPU:0, one launch (start us, length us, event | category | flops | bytes accessed | tf_op | source)
XLA Modules:
  0.0 189.2 jit_solution(15264379038484936477)
XLA Ops:
  0.7 1.3 copy-done.3
  2.6 4.1 %collective-permute-start.1 = (bf16[144,1024]{1,0:T(8,128)(2,1)S(1)}, bf16[144,1024]{1,0:T(8,128)(2,1)S(1)}, u32[]{:S(2)}, u32[]{:S(2)}) collective-permute-start(bf16[144,1024]{1,0:T(8,128)(2,1)S(1)} %cut.1.refs_0_), channel_id=1, source_target_pairs={{0,16},{4,20},{8,24},{12,28},{16,0},{20,4},{24,8},{28,12},{1,17},{... | collective-permute-start | bytes 884744 | tf_op jit(solution)/shard_map/ppermute | solution.py:57
  6.7 1.6 collective-permute-start
  8.3 1.5 collective-permute-start.2
  9.8 2.0 %collective-permute-done.2.other = s32[1,64]{1,0:T(1,128)S(1)} collective-permute-done((s32[1,64]{1,0:T(1,128)S(1)}, s32[1,64]{1,0:T(1,128)S(1)}, u32[]{:S(2)}, u32[]{:S(2)}) %collective-permute-start.2) | collective-permute-done | bytes 288 | tf_op jit(solution)/shard_map/ppermute | solution.py:57
  11.9 1.9 %collective-permute-start.4 = (s32[2,64]{1,0:T(2,128)S(1)}, s32[2,64]{1,0:T(2,128)S(1)}, u32[]{:S(2)}, u32[]{:S(2)}) collective-permute-start(s32[2,64]{1,0:T(2,128)S(1)} %pad_add_fusion), channel_id=1, source_target_pairs={{0,16},{4,20},{8,24},{12,28},{16,0},{20,4},{24,8},{28,12},{1,17},{... | collective-permute-start | bytes 1544 | tf_op jit(solution)/shard_map/ppermute | solution.py:57
  13.8 2.5 %collective-permute-start.3 = (s32[2,64]{1,0:T(2,128)S(1)}, s32[2,64]{1,0:T(2,128)S(1)}, u32[]{:S(2)}, u32[]{:S(2)}) collective-permute-start(s32[2,64]{1,0:T(2,128)S(1)} %pad_add_fusion), channel_id=1, source_target_pairs={{0,8},{4,12},{8,0},{12,4},{16,24},{20,28},{24,16},{28,20},{1,9},{5... | collective-permute-start | bytes 1544 | tf_op jit(solution)/shard_map/ppermute | solution.py:57
  16.9 4.3 %collective-permute-done.5 = s32[2,64]{1,0:T(2,128)S(1)} collective-permute-done((s32[2,64]{1,0:T(2,128)S(1)}, s32[2,64]{1,0:T(2,128)S(1)}, u32[]{:S(2)}, u32[]{:S(2)}) %collective-permute-start.5) | collective-permute-done | bytes 544 | tf_op jit(solution)/shard_map/ppermute | solution.py:57
  21.3 0.8 collective-permute-start.6
  22.2 1.1 pad_maximum_fusion.refs_0_
  23.3 5.7 %collective-permute-done.6.refs_2_.refs_3_ = bf16[144,1024]{1,0:T(8,128)(2,1)S(1)} collective-permute-done((bf16[144,1024]{1,0:T(8,128)(2,1)S(1)}, bf16[144,1024]{1,0:T(8,128)(2,1)S(1)}, u32[]{:S(2)}, u32[]{:S(2)}) %collective-permute-start.6) | collective-permute-done | bytes 294944 | tf_op jit(solution)/shard_map/ppermute | solution.py:57
  29.0 6.0 %all-to-all-start = ((bf16[32,160,128]{2,1,0:T(8,128)(2,1)}), bf16[32,160,128]{2,1,0:T(8,128)(2,1)S(1)}, u32[]{:S(2)}, u32[]{:S(2)}) async-start(bf16[32,160,128]{2,1,0:T(8,128)(2,1)} %after.3), calls=%async_computation | async-start | bytes 2621440 | tf_op jit(solution)/shard_map/all_to_all | solution.py:61
  34.9 3.3 %gather.1 = (bf16[144,2048]{1,0:T(8,128)(2,1)S(1)}, bf16[144,2048]{1,0:T(8,128)(2,1)S(1)}) custom-call(s32[2]{0:T(128)S(1)} %pad_add_fusion.1.ids, s32[1,64]{1,0:T(1,128)S(1)} %copy-done.8, s32[1,64]{1,0:T(1,128)S(1)} %collective-permute-done.2.other, bf16[144,1024]{1,0:T(8,128)(2,1)S(1)} %cut.1.refs_0_, ...), custom_call_target="tpu_custom_call" | custom-call | tf_op jit(solution)/shard_map/gather/pallas_call | solution.py:35
  38.3 2.1 %collective-permute-start.7 = (bf16[144,2048]{1,0:T(8,128)(2,1)S(1)}, bf16[144,2048]{1,0:T(8,128)(2,1)S(1)}, u32[]{:S(2)}, u32[]{:S(2)}) collective-permute-start(bf16[144,2048]{1,0:T(8,128)(2,1)S(1)} %get-tuple-element.25), channel_id=1, source_target_pairs={{0,4},{4,0},{8,12},{12,8},{16,20},{20,16},{24,28},{28,24},{1,5},{5... | collective-permute-start | bytes 1769480 | tf_op jit(solution)/shard_map/ppermute | solution.py:57
  40.4 1.5 collective-permute-start.8
  41.9 21.5 %collective-permute-done.7.away.refs_4_ = bf16[144,2048]{1,0:T(8,128)(2,1)S(1)} collective-permute-done((bf16[144,2048]{1,0:T(8,128)(2,1)S(1)}, bf16[144,2048]{1,0:T(8,128)(2,1)S(1)}, u32[]{:S(2)}, u32[]{:S(2)}) %collective-permute-start.7) | collective-permute-done | bytes 589856 | tf_op jit(solution)/shard_map/ppermute | solution.py:57
  63.4 2.4 %all-to-all-done = bf16[32,160,128]{2,1,0:T(8,128)(2,1)S(1)} async-done(((bf16[32,160,128]{2,1,0:T(8,128)(2,1)}), bf16[32,160,128]{2,1,0:T(8,128)(2,1)S(1)}, u32[]{:S(2)}, u32[]{:S(2)}) %all-to-all-start) | async-done | bytes 1310752 | tf_op jit(solution)/shard_map/all_to_all | solution.py:61
  65.8 1.4 expand.1
  67.2 4.6 %all-to-all-start.1 = ((bf16[8,4,16,1024]{3,2,1,0:T(8,128)(2,1)}), bf16[8,4,16,1024]{3,2,1,0:T(8,128)(2,1)}, u32[]{:S(2)}, u32[]{:S(2)}) async-start(bf16[8,4,16,1024]{3,2,1,0:T(8,128)(2,1)} %expand.1), calls=%async_computation.1 | async-start | bytes 2097152 | tf_op jit(solution)/shard_map/all_to_all | solution.py:61
  71.8 1.6 collective-permute-start.12
  73.9 11.8 %collective-permute-done.12.refs_6_ = bf16[144,2048]{1,0:T(8,128)(2,1)S(1)} collective-permute-done((bf16[144,2048]{1,0:T(8,128)(2,1)S(1)}, bf16[144,2048]{1,0:T(8,128)(2,1)S(1)}, u32[]{:S(2)}, u32[]{:S(2)}) %collective-permute-start.12) | collective-permute-done | bytes 589856 | tf_op jit(solution)/shard_map/ppermute | solution.py:57
  85.8 0.8 copy.34
  86.6 0.7 copy-done.10
  87.6 0.9 copy-done.12
  88.5 8.6 %all-to-all-done.1 = bf16[8,4,16,1024]{3,2,1,0:T(8,128)(2,1)} async-done(((bf16[8,4,16,1024]{3,2,1,0:T(8,128)(2,1)}), bf16[8,4,16,1024]{3,2,1,0:T(8,128)(2,1)}, u32[]{:S(2)}, u32[]{:S(2)}) %all-to-all-start.1) | async-done | bytes 1048608 | tf_op jit(solution)/shard_map/all_to_all | solution.py:61
  97.1 23.2 %attend.1 = (bf16[2,144,2048]{2,1,0:T(8,128)(2,1)}, bf16[2,144,2048]{2,1,0:T(8,128)(2,1)}, bf16[2,144,2048]{2,1,0:T(8,128)(2,1)}, bf16[2,144,2048]{2,1,0:T(8,128...) custom-call(s32[2]{0:T(128)} %copy-done.6, s32[16,32]{1,0:T(8,128)} %sel.1, bf16[32,16,64]{2,1,0:T(8,128)(2,1)} %bitcast.38, ...), custom_call_target="tpu_custom_call" | custom-call | tf_op jit(solution)/shard_map/attend/pallas_call | solution.py:35
  120.3 3.7 %all-to-all-start.2 = ((bf16[8,4,16,1024]{3,2,1,0:T(8,128)(2,1)}), bf16[8,4,16,1024]{3,2,1,0:T(8,128)(2,1)S(1)}, u32[]{:S(2)}, u32[]{:S(2)}) async-start(bf16[8,4,16,1024]{3,2,1,0:T(8,128)(2,1)} %bitcast.36), calls=%async_computation.2 | async-start | bytes 2097152 | tf_op jit(solution)/shard_map/all_to_all | solution.py:61
  124.5 1.5 pair.2
  126.0 1.6 collective-permute-start.17
  127.9 1.2 collective-permute-start.16
  129.0 13.2 %collective-permute-done.17.got = bf16[144,2048]{1,0:T(8,128)(2,1)S(1)} collective-permute-done((bf16[144,2048]{1,0:T(8,128)(2,1)S(1)}, bf16[144,2048]{1,0:T(8,128)(2,1)S(1)}, u32[]{:S(2)}, u32[]{:S(2)}) %collective-permute-start.17) | collective-permute-done | bytes 589856 | tf_op jit(solution)/shard_map/ppermute | solution.py:57
  142.2 0.8 owner.3
  143.0 1.6 collective-permute-start.18
  144.7 1.5 collective-permute-start.20
  146.1 3.3 %collective-permute-start.22 = (bf16[144,512]{1,0:T(8,128)(2,1)}, bf16[144,512]{1,0:T(8,128)(2,1)S(1)}, u32[]{:S(2)}, u32[]{:S(2)}) collective-permute-start(bf16[144,512]{1,0:T(8,128)(2,1)} %get-tuple-element.43), channel_id=1, source_target_pairs={{0,20},{4,16},{8,28},{12,24},{16,4},{20,0},{24,12},{28,8},{1,21},{... | collective-permute-start | bytes 442376 | tf_op jit(solution)/shard_map/ppermute | solution.py:57
  149.8 4.5 %collective-permute-done.16.got = bf16[144,2048]{1,0:T(8,128)(2,1)S(1)} collective-permute-done((bf16[144,2048]{1,0:T(8,128)(2,1)S(1)}, bf16[144,2048]{1,0:T(8,128)(2,1)S(1)}, u32[]{:S(2)}, u32[]{:S(2)}) %collective-permute-start.16) | collective-permute-done | bytes 589856 | tf_op jit(solution)/shard_map/ppermute | solution.py:57
  154.2 0.8 owner.2
  155.0 1.7 collective-permute-start.19
  156.8 2.4 %collective-permute-start.21 = (bf16[144,512]{1,0:T(8,128)(2,1)}, bf16[144,512]{1,0:T(8,128)(2,1)S(1)}, u32[]{:S(2)}, u32[]{:S(2)}) collective-permute-start(bf16[144,512]{1,0:T(8,128)(2,1)} %get-tuple-element.42), channel_id=1, source_target_pairs={{0,16},{4,20},{8,24},{12,28},{16,0},{20,4},{24,8},{28,12},{1,17},{... | collective-permute-start | bytes 442376 | tf_op jit(solution)/shard_map/ppermute | solution.py:57
  159.2 1.5 collective-permute-start.23
  160.6 1.1 reduce.1
  161.8 6.3 %all-to-all-start.3 = ((bf16[8,4,16,256]{3,2,1,0:T(8,128)(2,1)}), bf16[8,4,16,256]{3,2,1,0:T(8,128)(2,1)S(1)}, u32[]{:S(2)}, u32[]{:S(2)}) async-start(bf16[8,4,16,256]{3,2,1,0:T(8,128)(2,1)} %reduce.1), calls=%async_computation.3 | async-start | bytes 524288 | tf_op jit(solution)/shard_map/all_to_all | solution.py:61
  168.1 8.1 %collective-permute-done.21.refs_4_ = bf16[144,512]{1,0:T(8,128)(2,1)S(1)} collective-permute-done((bf16[144,512]{1,0:T(8,128)(2,1)}, bf16[144,512]{1,0:T(8,128)(2,1)S(1)}, u32[]{:S(2)}, u32[]{:S(2)}) %collective-permute-start.21) | collective-permute-done | bytes 147488 | tf_op jit(solution)/shard_map/ppermute | solution.py:57
  176.2 2.0 %scatter.1.refs_0_ = bf16[144,1024]{1,0:T(8,128)(2,1)S(1)} custom-call(s32[2]{0:T(128)S(1)} %copy-done.7, s32[8,64]{1,0:T(8,128)S(1)} %concatenate.12.refs_1_.rows, bf16[144,512]{1,0:T(8,128)(2,1)S(1)} %get-tuple-element.36.refs_0_, bf16[144,512]{1,0:T(8,128)(2,1)S(1)} %collective-permute-done.18.refs_1_, ...), custom_call_target="tpu_custom_call" | custom-call | tf_op jit(solution)/shard_map/scatter/pallas_call | solution.py:35
  178.2 1.6 collective-permute-start.26
  179.7 5.2 %collective-permute-done.26.refs_2_ = bf16[144,1024]{1,0:T(8,128)(2,1)S(1)} collective-permute-done((bf16[144,1024]{1,0:T(8,128)(2,1)S(1)}, bf16[144,1024]{1,0:T(8,128)(2,1)S(1)}, u32[]{:S(2)}, u32[]{:S(2)}) %collective-permute-start.26) | collective-permute-done | bytes 294944 | tf_op jit(solution)/shard_map/ppermute | solution.py:57
  185.0 0.7 copy.33
  187.1 2.1 %assemble.1 = f32[576,1024]{1,0:T(8,128)} custom-call(s32[2]{0:T(128)S(1)} %copy-done.7, bf16[144,1024]{1,0:T(8,128)(2,1)S(1)} %scatter.1.refs_0_, bf16[144,1024]{1,0:T(8,128)(2,1)S(1)} %collective-permute-done.25.refs_1_, bf16[144,1024]{1,0:T(8,128)(2,1)S(1)} %collective-permute-done.26.refs_2_, bf16[144,1024]{1,0:T(8,128)(2,1)S(1)} %collective-permute-done.27.refs_3_), custom_call_target="tpu_custom_call" | custom-call | tf_op jit(solution)/shard_map/assemble/pallas_call | solution.py:35
  (80 shorter events, 5.0 us)
Async XLA Ops:
  0.6 7.7 %copy-start.8 = (s32[1,64]{1,0:T(1,128)S(1)}, s32[1,64]{1,0:T(1,128)}, u32[]{:S(2)}) copy-start(s32[1,64]{1,0:T(1,128)} %own.1) | copy-start | bytes 772
  0.7 34.2 %copy-start.6 = (s32[2]{0:T(128)}, s32[2]{0:T(128)S(1)}, u32[]{:S(2)}) copy-start(s32[2]{0:T(128)S(1)} %pad_add_fusion.1.ids) | copy-start | bytes 28
  0.7 1.3 copy-start.3
  2.0 14.3 %copy-start.13 = (bf16[32,8192]{1,0:T(8,128)(2,1)S(1)}, bf16[32,8192]{1,0:T(8,128)(2,1)}, u32[]{:S(2)}) copy-start(bf16[32,8192]{1,0:T(8,128)(2,1)} %param.11) | copy-start | bytes 1572868
  2.6 14.2 %copy-start.14 = (bf16[32,8192]{1,0:T(8,128)(2,1)S(1)}, bf16[32,8192]{1,0:T(8,128)(2,1)}, u32[]{:S(2)}) copy-start(bf16[32,8192]{1,0:T(8,128)(2,1)} %param.12) | copy-start | bytes 1572868
  2.6 18.6 %collective-permute-start.1 = (bf16[144,1024]{1,0:T(8,128)(2,1)S(1)}, bf16[144,1024]{1,0:T(8,128)(2,1)S(1)}, u32[]{:S(2)}, u32[]{:S(2)}) collective-permute-start(bf16[144,1024]{1,0:T(8,128)(2,1)S(1)} %cut.1.refs_0_), channel_id=1, source_target_pairs={{0,16},{4,20},{8,24},{12,28},{16,0},{20,4},{24,8},{28,12},{1,17},{... | collective-permute-start | bytes 884744 | tf_op jit(solution)/shard_map/ppermute | solution.py:57
  6.7 14.5 %collective-permute-start = (bf16[144,1024]{1,0:T(8,128)(2,1)S(1)}, bf16[144,1024]{1,0:T(8,128)(2,1)S(1)}, u32[]{:S(2)}, u32[]{:S(2)}) collective-permute-start(bf16[144,1024]{1,0:T(8,128)(2,1)S(1)} %cut.1.refs_0_), channel_id=1, source_target_pairs={{0,8},{4,12},{8,0},{12,4},{16,24},{20,28},{24,16},{28,20},{1,9},{5... | collective-permute-start | bytes 884744 | tf_op jit(solution)/shard_map/ppermute | solution.py:57
  8.3 3.5 %collective-permute-start.2 = (s32[1,64]{1,0:T(1,128)S(1)}, s32[1,64]{1,0:T(1,128)S(1)}, u32[]{:S(2)}, u32[]{:S(2)}) collective-permute-start(s32[1,64]{1,0:T(1,128)S(1)} %copy-done.8), channel_id=1, source_target_pairs={{0,4},{4,0},{8,12},{12,8},{16,20},{20,16},{24,28},{28,24},{1,5},{5... | collective-permute-start | bytes 776 | tf_op jit(solution)/shard_map/ppermute | solution.py:57
  11.9 9.3 %collective-permute-start.5 = (s32[2,64]{1,0:T(2,128)S(1)}, s32[2,64]{1,0:T(2,128)S(1)}, u32[]{:S(2)}, u32[]{:S(2)}) collective-permute-start(s32[2,64]{1,0:T(2,128)S(1)} %pad_add_fusion), channel_id=1, source_target_pairs={{0,24},{4,28},{8,16},{12,20},{16,8},{20,12},{24,0},{28,4},{1,25},{... | collective-permute-start | bytes 1544 | tf_op jit(solution)/shard_map/ppermute | solution.py:57
  11.9 9.3 %collective-permute-start.4 = (s32[2,64]{1,0:T(2,128)S(1)}, s32[2,64]{1,0:T(2,128)S(1)}, u32[]{:S(2)}, u32[]{:S(2)}) collective-permute-start(s32[2,64]{1,0:T(2,128)S(1)} %pad_add_fusion), channel_id=1, source_target_pairs={{0,16},{4,20},{8,24},{12,28},{16,0},{20,4},{24,8},{28,12},{1,17},{... | collective-permute-start | bytes 1544 | tf_op jit(solution)/shard_map/ppermute | solution.py:57
  13.8 7.4 %collective-permute-start.3 = (s32[2,64]{1,0:T(2,128)S(1)}, s32[2,64]{1,0:T(2,128)S(1)}, u32[]{:S(2)}, u32[]{:S(2)}) collective-permute-start(s32[2,64]{1,0:T(2,128)S(1)} %pad_add_fusion), channel_id=1, source_target_pairs={{0,8},{4,12},{8,0},{12,4},{16,24},{20,28},{24,16},{28,20},{1,9},{5... | collective-permute-start | bytes 1544 | tf_op jit(solution)/shard_map/ppermute | solution.py:57
  16.7 5.4 %copy-start.17 = (bf16[16,32,128]{2,1,0:T(8,128)(2,1)S(1)}, bf16[16,32,128]{2,1,0:T(8,128)(2,1)}, u32[]{:S(2)}) copy-start(bf16[16,32,128]{2,1,0:T(8,128)(2,1)} %param.13) | copy-start | bytes 393220
  16.7 5.4 %copy-start.18 = (bf16[16,32,128]{2,1,0:T(8,128)(2,1)S(1)}, bf16[16,32,128]{2,1,0:T(8,128)(2,1)}, u32[]{:S(2)}) copy-start(bf16[16,32,128]{2,1,0:T(8,128)(2,1)} %param.8) | copy-start | bytes 393220
  21.3 7.7 %collective-permute-start.6 = (bf16[144,1024]{1,0:T(8,128)(2,1)S(1)}, bf16[144,1024]{1,0:T(8,128)(2,1)S(1)}, u32[]{:S(2)}, u32[]{:S(2)}) collective-permute-start(bf16[144,1024]{1,0:T(8,128)(2,1)S(1)} %after.2.refs_2_), channel_id=1, source_target_pairs={{0,8},{4,12},{8,0},{12,4},{16,24},{20,28},{24,16},{28,20},{1,9},{5... | collective-permute-start | bytes 884744 | tf_op jit(solution)/shard_map/ppermute | solution.py:57
  29.0 36.8 %all-to-all-start = ((bf16[32,160,128]{2,1,0:T(8,128)(2,1)}), bf16[32,160,128]{2,1,0:T(8,128)(2,1)S(1)}, u32[]{:S(2)}, u32[]{:S(2)}) async-start(bf16[32,160,128]{2,1,0:T(8,128)(2,1)} %after.3), calls=%async_computation | async-start | bytes 2621440 | tf_op jit(solution)/shard_map/all_to_all | solution.py:61
  38.3 35.1 %copy-start.5 = (bf16[144,2048]{1,0:T(8,128)(2,1)}, bf16[144,2048]{1,0:T(8,128)(2,1)S(1)}, u32[]{:S(2)}) copy-start(bf16[144,2048]{1,0:T(8,128)(2,1)S(1)} %get-tuple-element.26.refs_0_) | copy-start | bytes 1769476
  38.3 25.1 %collective-permute-start.7 = (bf16[144,2048]{1,0:T(8,128)(2,1)S(1)}, bf16[144,2048]{1,0:T(8,128)(2,1)S(1)}, u32[]{:S(2)}, u32[]{:S(2)}) collective-permute-start(bf16[144,2048]{1,0:T(8,128)(2,1)S(1)} %get-tuple-element.25), channel_id=1, source_target_pairs={{0,4},{4,0},{8,12},{12,8},{16,20},{20,16},{24,28},{28,24},{1,5},{5... | collective-permute-start | bytes 1769480 | tf_op jit(solution)/shard_map/ppermute | solution.py:57
  40.4 23.0 %collective-permute-start.8 = (bf16[144,2048]{1,0:T(8,128)(2,1)S(1)}, bf16[144,2048]{1,0:T(8,128)(2,1)S(1)}, u32[]{:S(2)}, u32[]{:S(2)}) collective-permute-start(bf16[144,2048]{1,0:T(8,128)(2,1)S(1)} %get-tuple-element.26.refs_0_), channel_id=1, source_target_pairs={{0,2},{1,3},{2,0},{3,1},{4,6},{5,7},{6,4},{7,5},{8,10},{9,11},{10,... | collective-permute-start | bytes 1769480 | tf_op jit(solution)/shard_map/ppermute | solution.py:57
  63.4 9.9 %copy-start = (bf16[144,2048]{1,0:T(8,128)(2,1)}, bf16[144,2048]{1,0:T(8,128)(2,1)S(1)}, u32[]{:S(2)}) copy-start(bf16[144,2048]{1,0:T(8,128)(2,1)S(1)} %collective-permute-done.7.away.refs_4_) | copy-start | bytes 1769476
  63.4 10.4 %copy-start.1 = (bf16[144,2048]{1,0:T(8,128)(2,1)}, bf16[144,2048]{1,0:T(8,128)(2,1)S(1)}, u32[]{:S(2)}) copy-start(bf16[144,2048]{1,0:T(8,128)(2,1)S(1)} %collective-permute-done.8.over_x.refs_2_) | copy-start | bytes 1769476
  67.2 18.6 %copy-start.15 = (bf16[16,32,64]{2,1,0:T(8,128)(2,1)S(1)}, bf16[16,32,64]{2,1,0:T(8,128)(2,1)}, u32[]{:S(2)}) copy-start(bf16[16,32,64]{2,1,0:T(8,128)(2,1)} %param.9) | copy-start | bytes 196612
  67.2 29.9 %all-to-all-start.1 = ((bf16[8,4,16,1024]{3,2,1,0:T(8,128)(2,1)}), bf16[8,4,16,1024]{3,2,1,0:T(8,128)(2,1)}, u32[]{:S(2)}, u32[]{:S(2)}) async-start(bf16[8,4,16,1024]{3,2,1,0:T(8,128)(2,1)} %expand.1), calls=%async_computation.1 | async-start | bytes 2097152 | tf_op jit(solution)/shard_map/all_to_all | solution.py:61
  71.8 14.0 %collective-permute-start.12 = (bf16[144,2048]{1,0:T(8,128)(2,1)S(1)}, bf16[144,2048]{1,0:T(8,128)(2,1)S(1)}, u32[]{:S(2)}, u32[]{:S(2)}) collective-permute-start(bf16[144,2048]{1,0:T(8,128)(2,1)S(1)} %collective-permute-done.7.away.refs_4_), channel_id=1, source_target_pairs={{0,2},{1,3},{2,0},{3,1},{4,6},{5,7},{6,4},{7,5},{8,10},{9,11},{10,... | collective-permute-start | bytes 1769480 | tf_op jit(solution)/shard_map/ppermute | solution.py:57
  73.3 13.2 %collective-permute-start.9 = (bf16[144,2048]{1,0:T(8,128)(2,1)S(1)}, bf16[144,2048]{1,0:T(8,128)(2,1)S(1)}, u32[]{:S(2)}, u32[]{:S(2)}) collective-permute-start(bf16[144,2048]{1,0:T(8,128)(2,1)S(1)} %get-tuple-element.26.refs_0_), channel_id=1, source_target_pairs={{0,1},{1,0},{2,3},{3,2},{4,5},{5,4},{6,7},{7,6},{8,9},{9,8},{10,11... | collective-permute-start | bytes 1769480 | tf_op jit(solution)/shard_map/ppermute | solution.py:57
  73.4 13.2 %collective-permute-start.11 = (bf16[144,2048]{1,0:T(8,128)(2,1)S(1)}, bf16[144,2048]{1,0:T(8,128)(2,1)S(1)}, u32[]{:S(2)}, u32[]{:S(2)}) collective-permute-start(bf16[144,2048]{1,0:T(8,128)(2,1)S(1)} %collective-permute-done.7.away.refs_4_), channel_id=1, source_target_pairs={{0,1},{1,0},{2,3},{3,2},{4,5},{5,4},{6,7},{7,6},{8,9},{9,8},{10,11... | collective-permute-start | bytes 1769480 | tf_op jit(solution)/shard_map/ppermute | solution.py:57
  73.9 12.7 %collective-permute-start.10 = (bf16[144,2048]{1,0:T(8,128)(2,1)S(1)}, bf16[144,2048]{1,0:T(8,128)(2,1)S(1)}, u32[]{:S(2)}, u32[]{:S(2)}) collective-permute-start(bf16[144,2048]{1,0:T(8,128)(2,1)S(1)} %collective-permute-done.8.over_x.refs_2_), channel_id=1, source_target_pairs={{0,1},{1,0},{2,3},{3,2},{4,5},{5,4},{6,7},{7,6},{8,9},{9,8},{10,11... | collective-permute-start | bytes 1769480 | tf_op jit(solution)/shard_map/ppermute | solution.py:57
  85.8 2.7 %collective-permute-start.13 = (bf16[144,2048]{1,0:T(8,128)(2,1)S(1)}, bf16[144,2048]{1,0:T(8,128)(2,1)}, u32[]{:S(2)}, u32[]{:S(2)}) collective-permute-start(bf16[144,2048]{1,0:T(8,128)(2,1)S(1)} %collective-permute-done.12.refs_6_), channel_id=1, source_target_pairs={{0,1},{1,0},{2,3},{3,2},{4,5},{5,4},{6,7},{7,6},{8,9},{9,8},{10,11... | collective-permute-start | bytes 1769480 | tf_op jit(solution)/shard_map/ppermute | solution.py:57
  86.5 1.0 copy-start.11
  120.2 4.2 %copy-start.2 = (bf16[2,144,2048]{2,1,0:T(8,128)(2,1)S(1)}, bf16[2,144,2048]{2,1,0:T(8,128)(2,1)}, u32[]{:S(2)}) copy-start(bf16[2,144,2048]{2,1,0:T(8,128)(2,1)} %get-tuple-element.29.keep) | copy-start | bytes 3538948
  120.3 4.2 %collective-permute-start.14 = (bf16[2,144,2048]{2,1,0:T(8,128)(2,1)}, bf16[2,144,2048]{2,1,0:T(8,128)(2,1)}, u32[]{:S(2)}, u32[]{:S(2)}) collective-permute-start(bf16[2,144,2048]{2,1,0:T(8,128)(2,1)} %get-tuple-element.30), channel_id=1, source_target_pairs={{0,1},{1,0},{2,3},{3,2},{4,5},{5,4},{6,7},{7,6},{8,9},{9,8},{10,11... | collective-permute-start | bytes 3538952 | tf_op jit(solution)/shard_map/ppermute | solution.py:57
  120.3 40.3 %all-to-all-start.2 = ((bf16[8,4,16,1024]{3,2,1,0:T(8,128)(2,1)}), bf16[8,4,16,1024]{3,2,1,0:T(8,128)(2,1)S(1)}, u32[]{:S(2)}, u32[]{:S(2)}) async-start(bf16[8,4,16,1024]{3,2,1,0:T(8,128)(2,1)} %bitcast.36), calls=%async_computation.2 | async-start | bytes 2097152 | tf_op jit(solution)/shard_map/all_to_all | solution.py:61
  124.0 3.6 %copy-start.4 = (bf16[2,144,2048]{2,1,0:T(8,128)(2,1)S(1)}, bf16[2,144,2048]{2,1,0:T(8,128)(2,1)}, u32[]{:S(2)}) copy-start(bf16[2,144,2048]{2,1,0:T(8,128)(2,1)} %get-tuple-element.32.refs_1_) | copy-start | bytes 3538948
  124.1 3.5 %collective-permute-start.15 = (bf16[2,144,2048]{2,1,0:T(8,128)(2,1)}, bf16[2,144,2048]{2,1,0:T(8,128)(2,1)S(1)}, u32[]{:S(2)}, u32[]{:S(2)}) collective-permute-start(bf16[2,144,2048]{2,1,0:T(8,128)(2,1)} %get-tuple-element.33), channel_id=1, source_target_pairs={{0,1},{1,0},{2,3},{3,2},{4,5},{5,4},{6,7},{7,6},{8,9},{9,8},{10,11... | collective-permute-start | bytes 3538952 | tf_op jit(solution)/shard_map/ppermute | solution.py:57
  126.0 16.2 %collective-permute-start.17 = (bf16[144,2048]{1,0:T(8,128)(2,1)S(1)}, bf16[144,2048]{1,0:T(8,128)(2,1)S(1)}, u32[]{:S(2)}, u32[]{:S(2)}) collective-permute-start(bf16[144,2048]{1,0:T(8,128)(2,1)S(1)} %get-tuple-element.38), channel_id=1, source_target_pairs={{0,2},{1,3},{2,0},{3,1},{4,6},{5,7},{6,4},{7,5},{8,10},{9,11},{10,... | collective-permute-start | bytes 1769480 | tf_op jit(solution)/shard_map/ppermute | solution.py:57
  127.9 26.4 %collective-permute-start.16 = (bf16[144,2048]{1,0:T(8,128)(2,1)S(1)}, bf16[144,2048]{1,0:T(8,128)(2,1)S(1)}, u32[]{:S(2)}, u32[]{:S(2)}) collective-permute-start(bf16[144,2048]{1,0:T(8,128)(2,1)S(1)} %get-tuple-element.35), channel_id=1, source_target_pairs={{0,2},{1,3},{2,0},{3,1},{4,6},{5,7},{6,4},{7,5},{8,10},{9,11},{10,... | collective-permute-start | bytes 1769480 | tf_op jit(solution)/shard_map/ppermute | solution.py:57
  143.0 13.7 %collective-permute-start.18 = (bf16[144,512]{1,0:T(8,128)(2,1)S(1)}, bf16[144,512]{1,0:T(8,128)(2,1)S(1)}, u32[]{:S(2)}, u32[]{:S(2)}) collective-permute-start(bf16[144,512]{1,0:T(8,128)(2,1)S(1)} %get-tuple-element.39), channel_id=1, source_target_pairs={{0,4},{4,0},{8,12},{12,8},{16,20},{20,16},{24,28},{28,24},{1,5},{5... | collective-permute-start | bytes 442376 | tf_op jit(solution)/shard_map/ppermute | solution.py:57
  144.7 14.5 %collective-permute-start.20 = (bf16[144,512]{1,0:T(8,128)(2,1)S(1)}, bf16[144,512]{1,0:T(8,128)(2,1)S(1)}, u32[]{:S(2)}, u32[]{:S(2)}) collective-permute-start(bf16[144,512]{1,0:T(8,128)(2,1)S(1)} %get-tuple-element.41), channel_id=1, source_target_pairs={{0,12},{4,8},{8,4},{12,0},{16,28},{20,24},{24,20},{28,16},{1,13},{... | collective-permute-start | bytes 442376 | tf_op jit(solution)/shard_map/ppermute | solution.py:57
  146.1 22.0 %collective-permute-start.22 = (bf16[144,512]{1,0:T(8,128)(2,1)}, bf16[144,512]{1,0:T(8,128)(2,1)S(1)}, u32[]{:S(2)}, u32[]{:S(2)}) collective-permute-start(bf16[144,512]{1,0:T(8,128)(2,1)} %get-tuple-element.43), channel_id=1, source_target_pairs={{0,20},{4,16},{8,28},{12,24},{16,4},{20,0},{24,12},{28,8},{1,21},{... | collective-permute-start | bytes 442376 | tf_op jit(solution)/shard_map/ppermute | solution.py:57
  149.4 18.7 %collective-permute-start.24 = (bf16[144,512]{1,0:T(8,128)(2,1)}, bf16[144,512]{1,0:T(8,128)(2,1)S(1)}, u32[]{:S(2)}, u32[]{:S(2)}) collective-permute-start(bf16[144,512]{1,0:T(8,128)(2,1)} %get-tuple-element.45), channel_id=1, source_target_pairs={{0,28},{4,24},{8,20},{12,16},{16,12},{20,8},{24,4},{28,0},{1,29},{... | collective-permute-start | bytes 442376 | tf_op jit(solution)/shard_map/ppermute | solution.py:57
  155.0 13.1 %collective-permute-start.19 = (bf16[144,512]{1,0:T(8,128)(2,1)}, bf16[144,512]{1,0:T(8,128)(2,1)S(1)}, u32[]{:S(2)}, u32[]{:S(2)}) collective-permute-start(bf16[144,512]{1,0:T(8,128)(2,1)} %get-tuple-element.40), channel_id=1, source_target_pairs={{0,8},{4,12},{8,0},{12,4},{16,24},{20,28},{24,16},{28,20},{1,9},{5... | collective-permute-start | bytes 442376 | tf_op jit(solution)/shard_map/ppermute | solution.py:57
  156.8 19.4 %collective-permute-start.21 = (bf16[144,512]{1,0:T(8,128)(2,1)}, bf16[144,512]{1,0:T(8,128)(2,1)S(1)}, u32[]{:S(2)}, u32[]{:S(2)}) collective-permute-start(bf16[144,512]{1,0:T(8,128)(2,1)} %get-tuple-element.42), channel_id=1, source_target_pairs={{0,16},{4,20},{8,24},{12,28},{16,0},{20,4},{24,8},{28,12},{1,17},{... | collective-permute-start | bytes 442376 | tf_op jit(solution)/shard_map/ppermute | solution.py:57
  159.2 17.0 %copy-start.7 = (s32[2]{0:T(128)S(1)}, s32[2]{0:T(128)}, u32[]{:S(2)}) copy-start(s32[2]{0:T(128)} %copy-done.6) | copy-start | bytes 28
  159.2 17.0 %collective-permute-start.23 = (bf16[144,512]{1,0:T(8,128)(2,1)}, bf16[144,512]{1,0:T(8,128)(2,1)S(1)}, u32[]{:S(2)}, u32[]{:S(2)}) collective-permute-start(bf16[144,512]{1,0:T(8,128)(2,1)} %get-tuple-element.44), channel_id=1, source_target_pairs={{0,24},{4,28},{8,16},{12,20},{16,8},{20,12},{24,0},{28,4},{1,25},{... | collective-permute-start | bytes 442376 | tf_op jit(solution)/shard_map/ppermute | solution.py:57
  161.8 23.2 %copy-start.16 = (bf16[512,64]{1,0:T(8,128)(2,1)S(1)}, bf16[512,64]{1,0:T(8,128)(2,1)}, u32[]{:S(2)}) copy-start(bf16[512,64]{1,0:T(8,128)(2,1)} %get-tuple-element.28) | copy-start | bytes 196612
  161.8 23.9 %all-to-all-start.3 = ((bf16[8,4,16,256]{3,2,1,0:T(8,128)(2,1)}), bf16[8,4,16,256]{3,2,1,0:T(8,128)(2,1)S(1)}, u32[]{:S(2)}, u32[]{:S(2)}) async-start(bf16[8,4,16,256]{3,2,1,0:T(8,128)(2,1)} %reduce.1), calls=%async_computation.3 | async-start | bytes 524288 | tf_op jit(solution)/shard_map/all_to_all | solution.py:61
  178.2 6.8 %collective-permute-start.26 = (bf16[144,1024]{1,0:T(8,128)(2,1)S(1)}, bf16[144,1024]{1,0:T(8,128)(2,1)S(1)}, u32[]{:S(2)}, u32[]{:S(2)}) collective-permute-start(bf16[144,1024]{1,0:T(8,128)(2,1)S(1)} %scatter.1.refs_0_), channel_id=1, source_target_pairs={{0,2},{1,3},{2,0},{3,1},{4,6},{5,7},{6,4},{7,5},{8,10},{9,11},{10,... | collective-permute-start | bytes 884744 | tf_op jit(solution)/shard_map/ppermute | solution.py:57
  179.7 7.4 %collective-permute-start.25 = (bf16[144,1024]{1,0:T(8,128)(2,1)S(1)}, bf16[144,1024]{1,0:T(8,128)(2,1)S(1)}, u32[]{:S(2)}, u32[]{:S(2)}) collective-permute-start(bf16[144,1024]{1,0:T(8,128)(2,1)S(1)} %scatter.1.refs_0_), channel_id=1, source_target_pairs={{0,1},{1,0},{2,3},{3,2},{4,5},{5,4},{6,7},{7,6},{8,9},{9,8},{10,11... | collective-permute-start | bytes 884744 | tf_op jit(solution)/shard_map/ppermute | solution.py:57
  184.9 2.1 %collective-permute-start.27 = (bf16[144,1024]{1,0:T(8,128)(2,1)S(1)}, bf16[144,1024]{1,0:T(8,128)(2,1)S(1)}, u32[]{:S(2)}, u32[]{:S(2)}) collective-permute-start(bf16[144,1024]{1,0:T(8,128)(2,1)S(1)} %collective-permute-done.26.refs_2_), channel_id=1, source_target_pairs={{0,1},{1,0},{2,3},{3,2},{4,5},{5,4},{6,7},{7,6},{8,9},{9,8},{10,11... | collective-permute-start | bytes 884744 | tf_op jit(solution)/shard_map/ppermute | solution.py:57
  (3 other events, 2.5 us)

commit v4 on v2

--- a/solution.py
+++ b/solution.py
@@ -65,9 +65,12 @@
     pass
 
 
-def cut_kernel(ids, cache, out):
+def cut_kernel(ids, cache, out, sem):
     depth = out.shape[0]
-    out[...] = cache[pl.ds(pl.multiple_of(ids[1] * depth, 16), depth), :]
+    part = cache.at[pl.ds(pl.multiple_of(ids[1] * depth, 16), depth), :]
+    copy = pltpu.make_async_copy(part, out, sem)
+    copy.start()
+    copy.wait()
 
 
 def gather_kernel(per_peer, ids, own, other, *refs):
@@ -284,7 +287,15 @@
     scale = 1.0 / math.sqrt(nope + rope)
 
     row1 = swap(slot_blocks, "seq", 1)
-    (c0,) = call(cut_kernel, "cut", (ids, cache.T), [SMEM, VMEM], [((depth, tokens), BF16)])
+    (c0,) = call(
+        cut_kernel,
+        "cut",
+        (ids, cache.T),
+        [SMEM, ANY],
+        [((depth, tokens), BF16)],
+        [pltpu.SemaphoreType.DMA],
+        62,
+    )
     asked_y = jnp.concatenate([slot_blocks, row1], axis=0)
     asked = jnp.concatenate([asked_y] + [swap(asked_y, "seq", bit) for bit in (2, 4, 6)], axis=0)
     c2 = swap(c0, "seq", 4)

time: 191 us -> 193 us (1.010)
  no operation moved by 1% of the time
where the time goes in v4:
time: 193 us; the launch traced here: 190 us
  waiting for transfers between devices  87.5 us (45%)
  starting transfers between devices  56 us (29%)
  Pallas kernels  38 us (20%)
  local copies, waits for them, and re-layouts  5.55 us (3%)
    ppermute x28, waiting for transfers between devices, swap(): return lax.ppermute(x, axis, [(i, i ^ bit) for i in range(n)])  76.5 us
    pallas_call x13, Pallas kernels, call(): pl.pallas_call(body, out_shape=out_shape, in_specs=specs, out_specs=out_s...  38 us
    ppermute x28, starting transfers between devices, swap(): return lax.ppermute(x, axis, [(i, i ^ bit) for i in range(n)])  35.2 us
    all_to_all x4, starting transfers between devices, seq_swap(): return lax.all_to_all(x, 'seq', split_axis=0, concat_axis=0, tiled=True)  20.7 us
    all_to_all x4, waiting for transfers between devices, seq_swap(): return lax.all_to_all(x, 'seq', split_axis=0, concat_axis=0, tiled=True)  11 us
    unnamed x42, local copies, waits for them, and re-layouts  4.23 us
  transfers between devices with their start and end apart: 32, of which 11 were waited for; matrix products, arithmetic and copies ran while one was open for 3% of the time, Pallas kernels for 5%

profile of v4, /device:TPU:0, one launch (start us, length us, event | category | flops | bytes accessed | tf_op | source)
XLA Modules:
  0.0 189.6 jit_solution(9142904880354563212)
XLA Ops:
  1.2 2.4 %cut.1.refs_0_ = bf16[144,1024]{1,0:T(8,128)(2,1)} custom-call(s32[2]{0:T(128)} %pad_add_fusion.1.ids, bf16[576,1024]{1,0:T(8,128)(2,1)} %bitcast.35), custom_call_target="tpu_custom_call" | custom-call | tf_op jit(solution)/shard_map/cut/pallas_call | solution.py:35
  3.6 4.1 %collective-permute-start.1 = (bf16[144,1024]{1,0:T(8,128)(2,1)}, bf16[144,1024]{1,0:T(8,128)(2,1)S(1)}, u32[]{:S(2)}, u32[]{:S(2)}) collective-permute-start(bf16[144,1024]{1,0:T(8,128)(2,1)} %cut.1.refs_0_), channel_id=1, source_target_pairs={{0,16},{4,20},{8,24},{12,28},{16,0},{20,4},{24,8},{28,12},{1,17},{... | collective-permute-start | bytes 884744 | tf_op jit(solution)/shard_map/ppermute | solution.py:57
  7.7 1.6 collective-permute-start
  9.3 1.5 collective-permute-start.2
  10.8 2.0 %collective-permute-done.2.other = s32[1,64]{1,0:T(1,128)S(1)} collective-permute-done((s32[1,64]{1,0:T(1,128)S(1)}, s32[1,64]{1,0:T(1,128)S(1)}, u32[]{:S(2)}, u32[]{:S(2)}) %collective-permute-start.2) | collective-permute-done | bytes 288 | tf_op jit(solution)/shard_map/ppermute | solution.py:57
  12.9 1.9 %collective-permute-start.4 = (s32[2,64]{1,0:T(2,128)S(1)}, s32[2,64]{1,0:T(2,128)S(1)}, u32[]{:S(2)}, u32[]{:S(2)}) collective-permute-start(s32[2,64]{1,0:T(2,128)S(1)} %pad_add_fusion), channel_id=1, source_target_pairs={{0,16},{4,20},{8,24},{12,28},{16,0},{20,4},{24,8},{28,12},{1,17},{... | collective-permute-start | bytes 1544 | tf_op jit(solution)/shard_map/ppermute | solution.py:57
  14.8 2.5 %collective-permute-start.3 = (s32[2,64]{1,0:T(2,128)S(1)}, s32[2,64]{1,0:T(2,128)S(1)}, u32[]{:S(2)}, u32[]{:S(2)}) collective-permute-start(s32[2,64]{1,0:T(2,128)S(1)} %pad_add_fusion), channel_id=1, source_target_pairs={{0,8},{4,12},{8,0},{12,4},{16,24},{20,28},{24,16},{28,20},{1,9},{5... | collective-permute-start | bytes 1544 | tf_op jit(solution)/shard_map/ppermute | solution.py:57
  17.9 4.5 %collective-permute-done.5 = s32[2,64]{1,0:T(2,128)S(1)} collective-permute-done((s32[2,64]{1,0:T(2,128)S(1)}, s32[2,64]{1,0:T(2,128)S(1)}, u32[]{:S(2)}, u32[]{:S(2)}) %collective-permute-start.5) | collective-permute-done | bytes 544 | tf_op jit(solution)/shard_map/ppermute | solution.py:57
  22.5 0.8 collective-permute-start.6
  23.4 1.1 pad_maximum_fusion.refs_0_
  24.5 5.7 %collective-permute-done.6.refs_2_.refs_3_ = bf16[144,1024]{1,0:T(8,128)(2,1)S(1)} collective-permute-done((bf16[144,1024]{1,0:T(8,128)(2,1)S(1)}, bf16[144,1024]{1,0:T(8,128)(2,1)S(1)}, u32[]{:S(2)}, u32[]{:S(2)}) %collective-permute-start.6) | collective-permute-done | bytes 294944 | tf_op jit(solution)/shard_map/ppermute | solution.py:57
  30.2 6.1 %all-to-all-start = ((bf16[32,160,128]{2,1,0:T(8,128)(2,1)}), bf16[32,160,128]{2,1,0:T(8,128)(2,1)S(1)}, u32[]{:S(2)}, u32[]{:S(2)}) async-start(bf16[32,160,128]{2,1,0:T(8,128)(2,1)} %after.3), calls=%async_computation | async-start | bytes 2621440 | tf_op jit(solution)/shard_map/all_to_all | solution.py:61
  36.3 3.3 %gather.1 = (bf16[144,2048]{1,0:T(8,128)(2,1)S(1)}, bf16[144,2048]{1,0:T(8,128)(2,1)S(1)}) custom-call(s32[2]{0:T(128)S(1)} %copy-done.6, s32[1,64]{1,0:T(1,128)S(1)} %copy-done.8, s32[1,64]{1,0:T(1,128)S(1)} %collective-permute-done.2.other, bf16[144,1024]{1,0:T(8,128)(2,1)S(1)} %copy-done.3, bf16[144,1024]{1,0:T(8,128)(2,1)S(1)} %collective-permute-done.refs_2_.refs_1_, ...), custom_call_target="tpu_custom_call" | custom-call | tf_op jit(solution)/shard_map/gather/pallas_call | solution.py:35
  39.6 2.1 %collective-permute-start.7 = (bf16[144,2048]{1,0:T(8,128)(2,1)S(1)}, bf16[144,2048]{1,0:T(8,128)(2,1)S(1)}, u32[]{:S(2)}, u32[]{:S(2)}) collective-permute-start(bf16[144,2048]{1,0:T(8,128)(2,1)S(1)} %get-tuple-element.25), channel_id=1, source_target_pairs={{0,4},{4,0},{8,12},{12,8},{16,20},{20,16},{24,28},{28,24},{1,5},{5... | collective-permute-start | bytes 1769480 | tf_op jit(solution)/shard_map/ppermute | solution.py:57
  41.7 1.5 collective-permute-start.8
  43.2 21.5 %collective-permute-done.7.away.refs_4_ = bf16[144,2048]{1,0:T(8,128)(2,1)S(1)} collective-permute-done((bf16[144,2048]{1,0:T(8,128)(2,1)S(1)}, bf16[144,2048]{1,0:T(8,128)(2,1)S(1)}, u32[]{:S(2)}, u32[]{:S(2)}) %collective-permute-start.7) | collective-permute-done | bytes 589856 | tf_op jit(solution)/shard_map/ppermute | solution.py:57
  64.7 2.4 %all-to-all-done = bf16[32,160,128]{2,1,0:T(8,128)(2,1)S(1)} async-done(((bf16[32,160,128]{2,1,0:T(8,128)(2,1)}), bf16[32,160,128]{2,1,0:T(8,128)(2,1)S(1)}, u32[]{:S(2)}, u32[]{:S(2)}) %all-to-all-start) | async-done | bytes 1310752 | tf_op jit(solution)/shard_map/all_to_all | solution.py:61
  67.1 1.4 expand.1
  68.5 4.6 %all-to-all-start.1 = ((bf16[8,4,16,1024]{3,2,1,0:T(8,128)(2,1)}), bf16[8,4,16,1024]{3,2,1,0:T(8,128)(2,1)}, u32[]{:S(2)}, u32[]{:S(2)}) async-start(bf16[8,4,16,1024]{3,2,1,0:T(8,128)(2,1)} %expand.1), calls=%async_computation.1 | async-start | bytes 2097152 | tf_op jit(solution)/shard_map/all_to_all | solution.py:61
  73.1 1.6 collective-permute-start.12
  75.3 11.8 %collective-permute-done.12.refs_6_ = bf16[144,2048]{1,0:T(8,128)(2,1)S(1)} collective-permute-done((bf16[144,2048]{1,0:T(8,128)(2,1)S(1)}, bf16[144,2048]{1,0:T(8,128)(2,1)S(1)}, u32[]{:S(2)}, u32[]{:S(2)}) %collective-permute-start.12) | collective-permute-done | bytes 589856 | tf_op jit(solution)/shard_map/ppermute | solution.py:57
  87.1 0.8 copy.34
  87.9 0.7 copy-done.10
  88.9 0.9 copy-done.12
  89.8 8.6 %all-to-all-done.1 = bf16[8,4,16,1024]{3,2,1,0:T(8,128)(2,1)} async-done(((bf16[8,4,16,1024]{3,2,1,0:T(8,128)(2,1)}), bf16[8,4,16,1024]{3,2,1,0:T(8,128)(2,1)}, u32[]{:S(2)}, u32[]{:S(2)}) %all-to-all-start.1) | async-done | bytes 1048608 | tf_op jit(solution)/shard_map/all_to_all | solution.py:61
  98.4 22.3 %attend.1 = (bf16[2,144,2048]{2,1,0:T(8,128)(2,1)}, bf16[2,144,2048]{2,1,0:T(8,128)(2,1)}, bf16[2,144,2048]{2,1,0:T(8,128)(2,1)}, bf16[2,144,2048]{2,1,0:T(8,128...) custom-call(s32[2]{0:T(128)} %pad_add_fusion.1.ids, s32[16,32]{1,0:T(8,128)} %sel.1, ...), custom_call_target="tpu_custom_call" | custom-call | tf_op jit(solution)/shard_map/attend/pallas_call | solution.py:35
  120.8 3.7 %all-to-all-start.2 = ((bf16[8,4,16,1024]{3,2,1,0:T(8,128)(2,1)}), bf16[8,4,16,1024]{3,2,1,0:T(8,128)(2,1)S(1)}, u32[]{:S(2)}, u32[]{:S(2)}) async-start(bf16[8,4,16,1024]{3,2,1,0:T(8,128)(2,1)} %bitcast.36), calls=%async_computation.2 | async-start | bytes 2097152 | tf_op jit(solution)/shard_map/all_to_all | solution.py:61
  124.9 1.5 pair.2
  126.5 1.6 collective-permute-start.17
  128.3 1.2 collective-permute-start.16
  129.5 13.2 %collective-permute-done.17.got = bf16[144,2048]{1,0:T(8,128)(2,1)S(1)} collective-permute-done((bf16[144,2048]{1,0:T(8,128)(2,1)S(1)}, bf16[144,2048]{1,0:T(8,128)(2,1)S(1)}, u32[]{:S(2)}, u32[]{:S(2)}) %collective-permute-start.17) | collective-permute-done | bytes 589856 | tf_op jit(solution)/shard_map/ppermute | solution.py:57
  142.7 0.8 owner.3
  143.5 1.6 collective-permute-start.18
  145.1 1.5 collective-permute-start.20
  146.6 3.3 %collective-permute-start.22 = (bf16[144,512]{1,0:T(8,128)(2,1)}, bf16[144,512]{1,0:T(8,128)(2,1)S(1)}, u32[]{:S(2)}, u32[]{:S(2)}) collective-permute-start(bf16[144,512]{1,0:T(8,128)(2,1)} %get-tuple-element.43), channel_id=1, source_target_pairs={{0,20},{4,16},{8,28},{12,24},{16,4},{20,0},{24,12},{28,8},{1,21},{... | collective-permute-start | bytes 442376 | tf_op jit(solution)/shard_map/ppermute | solution.py:57
  150.2 4.5 %collective-permute-done.16.got = bf16[144,2048]{1,0:T(8,128)(2,1)S(1)} collective-permute-done((bf16[144,2048]{1,0:T(8,128)(2,1)S(1)}, bf16[144,2048]{1,0:T(8,128)(2,1)S(1)}, u32[]{:S(2)}, u32[]{:S(2)}) %collective-permute-start.16) | collective-permute-done | bytes 589856 | tf_op jit(solution)/shard_map/ppermute | solution.py:57
  154.7 0.8 owner.2
  155.5 1.7 collective-permute-start.19
  157.2 2.4 %collective-permute-start.21 = (bf16[144,512]{1,0:T(8,128)(2,1)}, bf16[144,512]{1,0:T(8,128)(2,1)S(1)}, u32[]{:S(2)}, u32[]{:S(2)}) collective-permute-start(bf16[144,512]{1,0:T(8,128)(2,1)} %get-tuple-element.42), channel_id=1, source_target_pairs={{0,16},{4,20},{8,24},{12,28},{16,0},{20,4},{24,8},{28,12},{1,17},{... | collective-permute-start | bytes 442376 | tf_op jit(solution)/shard_map/ppermute | solution.py:57
  159.6 1.5 collective-permute-start.23
  161.1 1.1 reduce.1
  162.2 6.4 %all-to-all-start.3 = ((bf16[8,4,16,256]{3,2,1,0:T(8,128)(2,1)}), bf16[8,4,16,256]{3,2,1,0:T(8,128)(2,1)S(1)}, u32[]{:S(2)}, u32[]{:S(2)}) async-start(bf16[8,4,16,256]{3,2,1,0:T(8,128)(2,1)} %reduce.1), calls=%async_computation.3 | async-start | bytes 524288 | tf_op jit(solution)/shard_map/all_to_all | solution.py:61
  168.6 8.0 %collective-permute-done.21.refs_4_ = bf16[144,512]{1,0:T(8,128)(2,1)S(1)} collective-permute-done((bf16[144,512]{1,0:T(8,128)(2,1)}, bf16[144,512]{1,0:T(8,128)(2,1)S(1)}, u32[]{:S(2)}, u32[]{:S(2)}) %collective-permute-start.21) | collective-permute-done | bytes 147488 | tf_op jit(solution)/shard_map/ppermute | solution.py:57
  176.6 2.0 %scatter.1.refs_0_ = bf16[144,1024]{1,0:T(8,128)(2,1)S(1)} custom-call(s32[2]{0:T(128)S(1)} %copy-done.7, s32[8,64]{1,0:T(8,128)S(1)} %concatenate.12.refs_1_.rows, bf16[144,512]{1,0:T(8,128)(2,1)S(1)} %get-tuple-element.36.refs_0_, bf16[144,512]{1,0:T(8,128)(2,1)S(1)} %collective-permute-done.18.refs_1_, ...), custom_call_target="tpu_custom_call" | custom-call | tf_op jit(solution)/shard_map/scatter/pallas_call | solution.py:35
  178.6 1.6 collective-permute-start.26
  180.2 5.2 %collective-permute-done.26.refs_2_ = bf16[144,1024]{1,0:T(8,128)(2,1)S(1)} collective-permute-done((bf16[144,1024]{1,0:T(8,128)(2,1)S(1)}, bf16[144,1024]{1,0:T(8,128)(2,1)S(1)}, u32[]{:S(2)}, u32[]{:S(2)}) %collective-permute-start.26) | collective-permute-done | bytes 294944 | tf_op jit(solution)/shard_map/ppermute | solution.py:57
  185.4 0.7 copy.33
  187.5 2.1 %assemble.1 = f32[576,1024]{1,0:T(8,128)} custom-call(s32[2]{0:T(128)S(1)} %copy-done.7, bf16[144,1024]{1,0:T(8,128)(2,1)S(1)} %scatter.1.refs_0_, bf16[144,1024]{1,0:T(8,128)(2,1)S(1)} %collective-permute-done.25.refs_1_, bf16[144,1024]{1,0:T(8,128)(2,1)S(1)} %collective-permute-done.26.refs_2_, bf16[144,1024]{1,0:T(8,128)(2,1)S(1)} %collective-permute-done.27.refs_3_), custom_call_target="tpu_custom_call" | custom-call | tf_op jit(solution)/shard_map/assemble/pallas_call | solution.py:35
  (80 shorter events, 4.9 us)
Async XLA Ops:
  0.6 8.7 %copy-start.8 = (s32[1,64]{1,0:T(1,128)S(1)}, s32[1,64]{1,0:T(1,128)}, u32[]{:S(2)}) copy-start(s32[1,64]{1,0:T(1,128)} %own.1) | copy-start | bytes 772
  0.6 16.7 %copy-start.13 = (bf16[32,8192]{1,0:T(8,128)(2,1)S(1)}, bf16[32,8192]{1,0:T(8,128)(2,1)}, u32[]{:S(2)}) copy-start(bf16[32,8192]{1,0:T(8,128)(2,1)} %param.11) | copy-start | bytes 1572868
  3.6 14.2 %copy-start.14 = (bf16[32,8192]{1,0:T(8,128)(2,1)S(1)}, bf16[32,8192]{1,0:T(8,128)(2,1)}, u32[]{:S(2)}) copy-start(bf16[32,8192]{1,0:T(8,128)(2,1)} %param.12) | copy-start | bytes 1572868
  3.6 18.8 %collective-permute-start.1 = (bf16[144,1024]{1,0:T(8,128)(2,1)}, bf16[144,1024]{1,0:T(8,128)(2,1)S(1)}, u32[]{:S(2)}, u32[]{:S(2)}) collective-permute-start(bf16[144,1024]{1,0:T(8,128)(2,1)} %cut.1.refs_0_), channel_id=1, source_target_pairs={{0,16},{4,20},{8,24},{12,28},{16,0},{20,4},{24,8},{28,12},{1,17},{... | collective-permute-start | bytes 884744 | tf_op jit(solution)/shard_map/ppermute | solution.py:57
  7.7 14.7 %collective-permute-start = (bf16[144,1024]{1,0:T(8,128)(2,1)}, bf16[144,1024]{1,0:T(8,128)(2,1)S(1)}, u32[]{:S(2)}, u32[]{:S(2)}) collective-permute-start(bf16[144,1024]{1,0:T(8,128)(2,1)} %cut.1.refs_0_), channel_id=1, source_target_pairs={{0,8},{4,12},{8,0},{12,4},{16,24},{20,28},{24,16},{28,20},{1,9},{5... | collective-permute-start | bytes 884744 | tf_op jit(solution)/shard_map/ppermute | solution.py:57
  9.3 3.5 %collective-permute-start.2 = (s32[1,64]{1,0:T(1,128)S(1)}, s32[1,64]{1,0:T(1,128)S(1)}, u32[]{:S(2)}, u32[]{:S(2)}) collective-permute-start(s32[1,64]{1,0:T(1,128)S(1)} %copy-done.8), channel_id=1, source_target_pairs={{0,4},{4,0},{8,12},{12,8},{16,20},{20,16},{24,28},{28,24},{1,5},{5... | collective-permute-start | bytes 776 | tf_op jit(solution)/shard_map/ppermute | solution.py:57
  12.8 9.6 %collective-permute-start.5 = (s32[2,64]{1,0:T(2,128)S(1)}, s32[2,64]{1,0:T(2,128)S(1)}, u32[]{:S(2)}, u32[]{:S(2)}) collective-permute-start(s32[2,64]{1,0:T(2,128)S(1)} %pad_add_fusion), channel_id=1, source_target_pairs={{0,24},{4,28},{8,16},{12,20},{16,8},{20,12},{24,0},{28,4},{1,25},{... | collective-permute-start | bytes 1544 | tf_op jit(solution)/shard_map/ppermute | solution.py:57
  12.9 9.5 %collective-permute-start.4 = (s32[2,64]{1,0:T(2,128)S(1)}, s32[2,64]{1,0:T(2,128)S(1)}, u32[]{:S(2)}, u32[]{:S(2)}) collective-permute-start(s32[2,64]{1,0:T(2,128)S(1)} %pad_add_fusion), channel_id=1, source_target_pairs={{0,16},{4,20},{8,24},{12,28},{16,0},{20,4},{24,8},{28,12},{1,17},{... | collective-permute-start | bytes 1544 | tf_op jit(solution)/shard_map/ppermute | solution.py:57
  14.8 7.6 %collective-permute-start.3 = (s32[2,64]{1,0:T(2,128)S(1)}, s32[2,64]{1,0:T(2,128)S(1)}, u32[]{:S(2)}, u32[]{:S(2)}) collective-permute-start(s32[2,64]{1,0:T(2,128)S(1)} %pad_add_fusion), channel_id=1, source_target_pairs={{0,8},{4,12},{8,0},{12,4},{16,24},{20,28},{24,16},{28,20},{1,9},{5... | collective-permute-start | bytes 1544 | tf_op jit(solution)/shard_map/ppermute | solution.py:57
  17.7 5.6 %copy-start.17 = (bf16[16,32,128]{2,1,0:T(8,128)(2,1)S(1)}, bf16[16,32,128]{2,1,0:T(8,128)(2,1)}, u32[]{:S(2)}) copy-start(bf16[16,32,128]{2,1,0:T(8,128)(2,1)} %param.13) | copy-start | bytes 393220
  17.7 5.6 %copy-start.18 = (bf16[16,32,128]{2,1,0:T(8,128)(2,1)S(1)}, bf16[16,32,128]{2,1,0:T(8,128)(2,1)}, u32[]{:S(2)}) copy-start(bf16[16,32,128]{2,1,0:T(8,128)(2,1)} %param.8) | copy-start | bytes 393220
  22.5 7.7 %collective-permute-start.6 = (bf16[144,1024]{1,0:T(8,128)(2,1)S(1)}, bf16[144,1024]{1,0:T(8,128)(2,1)S(1)}, u32[]{:S(2)}, u32[]{:S(2)}) collective-permute-start(bf16[144,1024]{1,0:T(8,128)(2,1)S(1)} %after.2.refs_2_), channel_id=1, source_target_pairs={{0,8},{4,12},{8,0},{12,4},{16,24},{20,28},{24,16},{28,20},{1,9},{5... | collective-permute-start | bytes 884744 | tf_op jit(solution)/shard_map/ppermute | solution.py:57
  30.2 6.1 %copy-start.3 = (bf16[144,1024]{1,0:T(8,128)(2,1)S(1)}, bf16[144,1024]{1,0:T(8,128)(2,1)}, u32[]{:S(2)}) copy-start(bf16[144,1024]{1,0:T(8,128)(2,1)} %cut.1.refs_0_) | copy-start | bytes 884740
  30.2 6.1 %copy-start.6 = (s32[2]{0:T(128)S(1)}, s32[2]{0:T(128)}, u32[]{:S(2)}) copy-start(s32[2]{0:T(128)} %pad_add_fusion.1.ids) | copy-start | bytes 28
  30.2 36.9 %all-to-all-start = ((bf16[32,160,128]{2,1,0:T(8,128)(2,1)}), bf16[32,160,128]{2,1,0:T(8,128)(2,1)S(1)}, u32[]{:S(2)}, u32[]{:S(2)}) async-start(bf16[32,160,128]{2,1,0:T(8,128)(2,1)} %after.3), calls=%async_computation | async-start | bytes 2621440 | tf_op jit(solution)/shard_map/all_to_all | solution.py:61
  39.6 35.1 %copy-start.5 = (bf16[144,2048]{1,0:T(8,128)(2,1)}, bf16[144,2048]{1,0:T(8,128)(2,1)S(1)}, u32[]{:S(2)}) copy-start(bf16[144,2048]{1,0:T(8,128)(2,1)S(1)} %get-tuple-element.26.refs_0_) | copy-start | bytes 1769476
  39.6 25.1 %collective-permute-start.7 = (bf16[144,2048]{1,0:T(8,128)(2,1)S(1)}, bf16[144,2048]{1,0:T(8,128)(2,1)S(1)}, u32[]{:S(2)}, u32[]{:S(2)}) collective-permute-start(bf16[144,2048]{1,0:T(8,128)(2,1)S(1)} %get-tuple-element.25), channel_id=1, source_target_pairs={{0,4},{4,0},{8,12},{12,8},{16,20},{20,16},{24,28},{28,24},{1,5},{5... | collective-permute-start | bytes 1769480 | tf_op jit(solution)/shard_map/ppermute | solution.py:57
  41.7 23.0 %collective-permute-start.8 = (bf16[144,2048]{1,0:T(8,128)(2,1)S(1)}, bf16[144,2048]{1,0:T(8,128)(2,1)S(1)}, u32[]{:S(2)}, u32[]{:S(2)}) collective-permute-start(bf16[144,2048]{1,0:T(8,128)(2,1)S(1)} %get-tuple-element.26.refs_0_), channel_id=1, source_target_pairs={{0,2},{1,3},{2,0},{3,1},{4,6},{5,7},{6,4},{7,5},{8,10},{9,11},{10,... | collective-permute-start | bytes 1769480 | tf_op jit(solution)/shard_map/ppermute | solution.py:57
  64.7 9.9 %copy-start = (bf16[144,2048]{1,0:T(8,128)(2,1)}, bf16[144,2048]{1,0:T(8,128)(2,1)S(1)}, u32[]{:S(2)}) copy-start(bf16[144,2048]{1,0:T(8,128)(2,1)S(1)} %collective-permute-done.7.away.refs_4_) | copy-start | bytes 1769476
  64.7 10.4 %copy-start.1 = (bf16[144,2048]{1,0:T(8,128)(2,1)}, bf16[144,2048]{1,0:T(8,128)(2,1)S(1)}, u32[]{:S(2)}) copy-start(bf16[144,2048]{1,0:T(8,128)(2,1)S(1)} %collective-permute-done.8.over_x.refs_2_) | copy-start | bytes 1769476
  68.5 18.6 %copy-start.15 = (bf16[16,32,64]{2,1,0:T(8,128)(2,1)S(1)}, bf16[16,32,64]{2,1,0:T(8,128)(2,1)}, u32[]{:S(2)}) copy-start(bf16[16,32,64]{2,1,0:T(8,128)(2,1)} %param.9) | copy-start | bytes 196612
  68.5 29.9 %all-to-all-start.1 = ((bf16[8,4,16,1024]{3,2,1,0:T(8,128)(2,1)}), bf16[8,4,16,1024]{3,2,1,0:T(8,128)(2,1)}, u32[]{:S(2)}, u32[]{:S(2)}) async-start(bf16[8,4,16,1024]{3,2,1,0:T(8,128)(2,1)} %expand.1), calls=%async_computation.1 | async-start | bytes 2097152 | tf_op jit(solution)/shard_map/all_to_all | solution.py:61
  73.1 14.0 %collective-permute-start.12 = (bf16[144,2048]{1,0:T(8,128)(2,1)S(1)}, bf16[144,2048]{1,0:T(8,128)(2,1)S(1)}, u32[]{:S(2)}, u32[]{:S(2)}) collective-permute-start(bf16[144,2048]{1,0:T(8,128)(2,1)S(1)} %collective-permute-done.7.away.refs_4_), channel_id=1, source_target_pairs={{0,2},{1,3},{2,0},{3,1},{4,6},{5,7},{6,4},{7,5},{8,10},{9,11},{10,... | collective-permute-start | bytes 1769480 | tf_op jit(solution)/shard_map/ppermute | solution.py:57
  74.7 13.2 %collective-permute-start.9 = (bf16[144,2048]{1,0:T(8,128)(2,1)S(1)}, bf16[144,2048]{1,0:T(8,128)(2,1)S(1)}, u32[]{:S(2)}, u32[]{:S(2)}) collective-permute-start(bf16[144,2048]{1,0:T(8,128)(2,1)S(1)} %get-tuple-element.26.refs_0_), channel_id=1, source_target_pairs={{0,1},{1,0},{2,3},{3,2},{4,5},{5,4},{6,7},{7,6},{8,9},{9,8},{10,11... | collective-permute-start | bytes 1769480 | tf_op jit(solution)/shard_map/ppermute | solution.py:57
  74.7 13.2 %collective-permute-start.11 = (bf16[144,2048]{1,0:T(8,128)(2,1)S(1)}, bf16[144,2048]{1,0:T(8,128)(2,1)S(1)}, u32[]{:S(2)}, u32[]{:S(2)}) collective-permute-start(bf16[144,2048]{1,0:T(8,128)(2,1)S(1)} %collective-permute-done.7.away.refs_4_), channel_id=1, source_target_pairs={{0,1},{1,0},{2,3},{3,2},{4,5},{5,4},{6,7},{7,6},{8,9},{9,8},{10,11... | collective-permute-start | bytes 1769480 | tf_op jit(solution)/shard_map/ppermute | solution.py:57
  75.2 12.7 %collective-permute-start.10 = (bf16[144,2048]{1,0:T(8,128)(2,1)S(1)}, bf16[144,2048]{1,0:T(8,128)(2,1)S(1)}, u32[]{:S(2)}, u32[]{:S(2)}) collective-permute-start(bf16[144,2048]{1,0:T(8,128)(2,1)S(1)} %collective-permute-done.8.over_x.refs_2_), channel_id=1, source_target_pairs={{0,1},{1,0},{2,3},{3,2},{4,5},{5,4},{6,7},{7,6},{8,9},{9,8},{10,11... | collective-permute-start | bytes 1769480 | tf_op jit(solution)/shard_map/ppermute | solution.py:57
  87.1 2.7 %collective-permute-start.13 = (bf16[144,2048]{1,0:T(8,128)(2,1)S(1)}, bf16[144,2048]{1,0:T(8,128)(2,1)}, u32[]{:S(2)}, u32[]{:S(2)}) collective-permute-start(bf16[144,2048]{1,0:T(8,128)(2,1)S(1)} %collective-permute-done.12.refs_6_), channel_id=1, source_target_pairs={{0,1},{1,0},{2,3},{3,2},{4,5},{5,4},{6,7},{7,6},{8,9},{9,8},{10,11... | collective-permute-start | bytes 1769480 | tf_op jit(solution)/shard_map/ppermute | solution.py:57
  87.9 1.0 copy-start.11
  120.7 4.2 %copy-start.2 = (bf16[2,144,2048]{2,1,0:T(8,128)(2,1)S(1)}, bf16[2,144,2048]{2,1,0:T(8,128)(2,1)}, u32[]{:S(2)}) copy-start(bf16[2,144,2048]{2,1,0:T(8,128)(2,1)} %get-tuple-element.29.keep) | copy-start | bytes 3538948
  120.7 4.2 %collective-permute-start.14 = (bf16[2,144,2048]{2,1,0:T(8,128)(2,1)}, bf16[2,144,2048]{2,1,0:T(8,128)(2,1)}, u32[]{:S(2)}, u32[]{:S(2)}) collective-permute-start(bf16[2,144,2048]{2,1,0:T(8,128)(2,1)} %get-tuple-element.30), channel_id=1, source_target_pairs={{0,1},{1,0},{2,3},{3,2},{4,5},{5,4},{6,7},{7,6},{8,9},{9,8},{10,11... | collective-permute-start | bytes 3538952 | tf_op jit(solution)/shard_map/ppermute | solution.py:57
  120.8 40.3 %all-to-all-start.2 = ((bf16[8,4,16,1024]{3,2,1,0:T(8,128)(2,1)}), bf16[8,4,16,1024]{3,2,1,0:T(8,128)(2,1)S(1)}, u32[]{:S(2)}, u32[]{:S(2)}) async-start(bf16[8,4,16,1024]{3,2,1,0:T(8,128)(2,1)} %bitcast.36), calls=%async_computation.2 | async-start | bytes 2097152 | tf_op jit(solution)/shard_map/all_to_all | solution.py:61
  124.5 3.5 %copy-start.4 = (bf16[2,144,2048]{2,1,0:T(8,128)(2,1)S(1)}, bf16[2,144,2048]{2,1,0:T(8,128)(2,1)}, u32[]{:S(2)}) copy-start(bf16[2,144,2048]{2,1,0:T(8,128)(2,1)} %get-tuple-element.32.refs_1_) | copy-start | bytes 3538948
  124.5 3.5 %collective-permute-start.15 = (bf16[2,144,2048]{2,1,0:T(8,128)(2,1)}, bf16[2,144,2048]{2,1,0:T(8,128)(2,1)S(1)}, u32[]{:S(2)}, u32[]{:S(2)}) collective-permute-start(bf16[2,144,2048]{2,1,0:T(8,128)(2,1)} %get-tuple-element.33), channel_id=1, source_target_pairs={{0,1},{1,0},{2,3},{3,2},{4,5},{5,4},{6,7},{7,6},{8,9},{9,8},{10,11... | collective-permute-start | bytes 3538952 | tf_op jit(solution)/shard_map/ppermute | solution.py:57
  126.5 16.2 %collective-permute-start.17 = (bf16[144,2048]{1,0:T(8,128)(2,1)S(1)}, bf16[144,2048]{1,0:T(8,128)(2,1)S(1)}, u32[]{:S(2)}, u32[]{:S(2)}) collective-permute-start(bf16[144,2048]{1,0:T(8,128)(2,1)S(1)} %get-tuple-element.38), channel_id=1, source_target_pairs={{0,2},{1,3},{2,0},{3,1},{4,6},{5,7},{6,4},{7,5},{8,10},{9,11},{10,... | collective-permute-start | bytes 1769480 | tf_op jit(solution)/shard_map/ppermute | solution.py:57
  128.3 26.4 %collective-permute-start.16 = (bf16[144,2048]{1,0:T(8,128)(2,1)S(1)}, bf16[144,2048]{1,0:T(8,128)(2,1)S(1)}, u32[]{:S(2)}, u32[]{:S(2)}) collective-permute-start(bf16[144,2048]{1,0:T(8,128)(2,1)S(1)} %get-tuple-element.35), channel_id=1, source_target_pairs={{0,2},{1,3},{2,0},{3,1},{4,6},{5,7},{6,4},{7,5},{8,10},{9,11},{10,... | collective-permute-start | bytes 1769480 | tf_op jit(solution)/shard_map/ppermute | solution.py:57
  143.5 13.7 %collective-permute-start.18 = (bf16[144,512]{1,0:T(8,128)(2,1)S(1)}, bf16[144,512]{1,0:T(8,128)(2,1)S(1)}, u32[]{:S(2)}, u32[]{:S(2)}) collective-permute-start(bf16[144,512]{1,0:T(8,128)(2,1)S(1)} %get-tuple-element.39), channel_id=1, source_target_pairs={{0,4},{4,0},{8,12},{12,8},{16,20},{20,16},{24,28},{28,24},{1,5},{5... | collective-permute-start | bytes 442376 | tf_op jit(solution)/shard_map/ppermute | solution.py:57
  145.1 14.5 %collective-permute-start.20 = (bf16[144,512]{1,0:T(8,128)(2,1)S(1)}, bf16[144,512]{1,0:T(8,128)(2,1)S(1)}, u32[]{:S(2)}, u32[]{:S(2)}) collective-permute-start(bf16[144,512]{1,0:T(8,128)(2,1)S(1)} %get-tuple-element.41), channel_id=1, source_target_pairs={{0,12},{4,8},{8,4},{12,0},{16,28},{20,24},{24,20},{28,16},{1,13},{... | collective-permute-start | bytes 442376 | tf_op jit(solution)/shard_map/ppermute | solution.py:57
  146.6 22.0 %collective-permute-start.22 = (bf16[144,512]{1,0:T(8,128)(2,1)}, bf16[144,512]{1,0:T(8,128)(2,1)S(1)}, u32[]{:S(2)}, u32[]{:S(2)}) collective-permute-start(bf16[144,512]{1,0:T(8,128)(2,1)} %get-tuple-element.43), channel_id=1, source_target_pairs={{0,20},{4,16},{8,28},{12,24},{16,4},{20,0},{24,12},{28,8},{1,21},{... | collective-permute-start | bytes 442376 | tf_op jit(solution)/shard_map/ppermute | solution.py:57
  149.9 18.7 %collective-permute-start.24 = (bf16[144,512]{1,0:T(8,128)(2,1)}, bf16[144,512]{1,0:T(8,128)(2,1)S(1)}, u32[]{:S(2)}, u32[]{:S(2)}) collective-permute-start(bf16[144,512]{1,0:T(8,128)(2,1)} %get-tuple-element.45), channel_id=1, source_target_pairs={{0,28},{4,24},{8,20},{12,16},{16,12},{20,8},{24,4},{28,0},{1,29},{... | collective-permute-start | bytes 442376 | tf_op jit(solution)/shard_map/ppermute | solution.py:57
  155.5 13.1 %collective-permute-start.19 = (bf16[144,512]{1,0:T(8,128)(2,1)}, bf16[144,512]{1,0:T(8,128)(2,1)S(1)}, u32[]{:S(2)}, u32[]{:S(2)}) collective-permute-start(bf16[144,512]{1,0:T(8,128)(2,1)} %get-tuple-element.40), channel_id=1, source_target_pairs={{0,8},{4,12},{8,0},{12,4},{16,24},{20,28},{24,16},{28,20},{1,9},{5... | collective-permute-start | bytes 442376 | tf_op jit(solution)/shard_map/ppermute | solution.py:57
  157.2 19.4 %collective-permute-start.21 = (bf16[144,512]{1,0:T(8,128)(2,1)}, bf16[144,512]{1,0:T(8,128)(2,1)S(1)}, u32[]{:S(2)}, u32[]{:S(2)}) collective-permute-start(bf16[144,512]{1,0:T(8,128)(2,1)} %get-tuple-element.42), channel_id=1, source_target_pairs={{0,16},{4,20},{8,24},{12,28},{16,0},{20,4},{24,8},{28,12},{1,17},{... | collective-permute-start | bytes 442376 | tf_op jit(solution)/shard_map/ppermute | solution.py:57
  159.6 17.0 %copy-start.7 = (s32[2]{0:T(128)S(1)}, s32[2]{0:T(128)}, u32[]{:S(2)}) copy-start(s32[2]{0:T(128)} %pad_add_fusion.1.ids) | copy-start | bytes 28
  159.6 17.0 %collective-permute-start.23 = (bf16[144,512]{1,0:T(8,128)(2,1)}, bf16[144,512]{1,0:T(8,128)(2,1)S(1)}, u32[]{:S(2)}, u32[]{:S(2)}) collective-permute-start(bf16[144,512]{1,0:T(8,128)(2,1)} %get-tuple-element.44), channel_id=1, source_target_pairs={{0,24},{4,28},{8,16},{12,20},{16,8},{20,12},{24,0},{28,4},{1,25},{... | collective-permute-start | bytes 442376 | tf_op jit(solution)/shard_map/ppermute | solution.py:57
  162.2 23.2 %copy-start.16 = (bf16[512,64]{1,0:T(8,128)(2,1)S(1)}, bf16[512,64]{1,0:T(8,128)(2,1)}, u32[]{:S(2)}) copy-start(bf16[512,64]{1,0:T(8,128)(2,1)} %get-tuple-element.28) | copy-start | bytes 196612
  162.2 23.9 %all-to-all-start.3 = ((bf16[8,4,16,256]{3,2,1,0:T(8,128)(2,1)}), bf16[8,4,16,256]{3,2,1,0:T(8,128)(2,1)S(1)}, u32[]{:S(2)}, u32[]{:S(2)}) async-start(bf16[8,4,16,256]{3,2,1,0:T(8,128)(2,1)} %reduce.1), calls=%async_computation.3 | async-start | bytes 524288 | tf_op jit(solution)/shard_map/all_to_all | solution.py:61
  178.6 6.8 %collective-permute-start.26 = (bf16[144,1024]{1,0:T(8,128)(2,1)S(1)}, bf16[144,1024]{1,0:T(8,128)(2,1)S(1)}, u32[]{:S(2)}, u32[]{:S(2)}) collective-permute-start(bf16[144,1024]{1,0:T(8,128)(2,1)S(1)} %scatter.1.refs_0_), channel_id=1, source_target_pairs={{0,2},{1,3},{2,0},{3,1},{4,6},{5,7},{6,4},{7,5},{8,10},{9,11},{10,... | collective-permute-start | bytes 884744 | tf_op jit(solution)/shard_map/ppermute | solution.py:57
  180.2 7.4 %collective-permute-start.25 = (bf16[144,1024]{1,0:T(8,128)(2,1)S(1)}, bf16[144,1024]{1,0:T(8,128)(2,1)S(1)}, u32[]{:S(2)}, u32[]{:S(2)}) collective-permute-start(bf16[144,1024]{1,0:T(8,128)(2,1)S(1)} %scatter.1.refs_0_), channel_id=1, source_target_pairs={{0,1},{1,0},{2,3},{3,2},{4,5},{5,4},{6,7},{7,6},{8,9},{9,8},{10,11... | collective-permute-start | bytes 884744 | tf_op jit(solution)/shard_map/ppermute | solution.py:57
  185.4 2.1 %collective-permute-start.27 = (bf16[144,1024]{1,0:T(8,128)(2,1)S(1)}, bf16[144,1024]{1,0:T(8,128)(2,1)S(1)}, u32[]{:S(2)}, u32[]{:S(2)}) collective-permute-start(bf16[144,1024]{1,0:T(8,128)(2,1)S(1)} %collective-permute-done.26.refs_2_), channel_id=1, source_target_pairs={{0,1},{1,0},{2,3},{3,2},{4,5},{5,4},{6,7},{7,6},{8,9},{9,8},{10,11... | collective-permute-start | bytes 884744 | tf_op jit(solution)/shard_map/ppermute | solution.py:57
  (3 other events, 2.5 us)
